TPU v7x, 512 devices: a whole 4x8x8 slice. The times are simulated.
512 devices in a mesh: blk: 128 (over z, y_lo, x), grp: 4 (over y_hi, core).
Axes of the slice: x: 4, y: 8 (y_hi: 2, y_lo: 4; y = y_hi * 4 + y_lo), z: 8, core: 2. Of those that a mesh axis runs over, the one named last changes fastest.
Arguments:
- photo_vectors: bfloat16 [98304, 1152], P('blk'), may hold values from -1 to 1
- caption_vectors: bfloat16 [98304, 1152], P(('blk', 'grp')), may hold values from -1 to 1
- matching_column: int32 [128, 768], P('blk'), may hold values from 0 to 767, each once within a row
- scale_exponent: float32 [1], replicated, may hold values from 0 to 1.4
- score_intercept: float32 [1], replicated, may hold values from -4 to 0
Outputs:
- image_grad: float32 [98304, 1152], P(('blk', 'grp'))
- text_grad: float32 [98304, 1152], P(('blk', 'grp'))
Inputs may be any that keep to these rules, and one draw needn't show every extreme that they name: `matching_column`: each row is an arrangement of 0 .. 767.
All inputs are finite; a program needn't handle non-finite values.
Results may differ from a plain program's by a relative error of at most 0.0024.
Values may be sent and summed in bfloat16 or wider, within the bound.
No kernel may reach another device: no remote copies, remote signals or barrier semaphores. Data moves between devices by JAX's collectives and lax.ppermute only.
A program may use at most 64 MiB of HBM per device.

v0:
```python
import jax
import jax.numpy as jnp
from jax import lax
from jax.sharding import PartitionSpec as P

STEPS = 2


def passed_along(block, axis, distance):
    devices = range(lax.axis_size(axis))
    route = [((i - distance) % len(devices), i) for i in devices]
    return lax.ppermute(block, axis, route)


def advance(travelling):
    return passed_along(travelling, "blk", 1)


def on_device(photo_vectors, caption_vectors, matching_column, scale_exponent, score_intercept):
    score_multiplier = jnp.exp(scale_exponent[0])
    group_displacement = score_intercept[0]
    width = caption_vectors.shape[0]
    columns = lax.axis_index("grp") * width + lax.iota(jnp.int32, width)
    matched = matching_column[0][:, None] == columns[None, :]
    first_target = jnp.where(matched, jnp.float32(1.0), jnp.float32(-1.0))

    def contribute(caption_rows, target):
        couple_scores = (
            score_multiplier
            * lax.dot_general(
                photo_vectors,
                caption_rows,
                (((1,), (1,)), ((), ())),
                preferred_element_type=jnp.float32,
            )
            + group_displacement
        )
        couple_weight = (-target * jax.nn.sigmoid(-target * couple_scores)).astype(jnp.bfloat16)
        photo_segment = score_multiplier * jnp.dot(
            couple_weight, caption_rows, preferred_element_type=jnp.float32
        )
        caption_segment = score_multiplier * lax.dot_general(
            couple_weight,
            photo_vectors,
            (((0,), (0,)), ((), ())),
            preferred_element_type=jnp.float32,
        )
        return (photo_segment, caption_segment)

    image_total, own_part = contribute(caption_vectors, first_target)
    travelling = caption_vectors
    carried = own_part
    for cycle_step in range(STEPS):
        travelling = advance(travelling)
        carried = passed_along(carried, "blk", 1)
        photo_segment, caption_segment = contribute(travelling, jnp.float32(-1.0))
        image_total = image_total + photo_segment
        carried = carried + caption_segment
    text_total = passed_along(carried, "blk", -STEPS)
    image_share = lax.psum_scatter(image_total, "grp", scatter_dimension=0, tiled=True)
    return (image_share, text_total)


def solution(mesh):
    in_specs = (P("blk", None), P(("blk", "grp"), None), P("blk", None), P(), P())
    out_specs = (P(("blk", "grp"), None), P(("blk", "grp"), None))
    return jax.shard_map(
        on_device, mesh=mesh, in_specs=in_specs, out_specs=out_specs, check_vma=False
    )
```

profile of v0, /device:TPU:254, one launch (start us, length us, event | category | flops | bytes accessed | tf_op | source)
XLA Modules:
  0.0 169.2 jit_solution(16712916728690443758)
XLA Ops:
  7.2 0.0 reduce-scatter.2.cloned.1.call-start
  7.2 7.9 %collective-permute-start = (bf16[192,1152]{1,0:T(8,128)(2,1)}, bf16[192,1152]{1,0:T(8,128)(2,1)S(1)}, u32[]{:S(2)}, u32[]{:S(2)}) collective-permute-start(bf16[192,1152]{1,0:T(8,128)(2,1)} %param.6), channel_id=1, source_target_pairs={{508,0},{0,4},{4,8},{8,12},{12,16},{16,20},{20,24},{24,28},{28,32}... | collective-permute-start | bytes 1327112 | tf_op jit(solution)/shard_map/ppermute | solution.py:12
  16.5 0.7 reduce
  17.2 1.9 %fusion.21 = bf16[768,192]{0,1:T(8,128)(2,1)S(1)} fusion(bf16[768,1152]{1,0:T(8,128)(2,1)S(1)} %copy-done, bf16[192,1152]{1,0:T(8,128)(2,1)} %param.6, f32[]{:T(128)} %bitcast.20, f32[]{:T(128)} %bitcast, s32[768]{0:T(1024)S(1)} %reduce, s32[192]{0:T(256)S(1)} %iota_add_fusion), kind=kOutput, calls=%fused_computation.29 | convolution fusion | flops 341360640 | bytes 2510600 | tf_op jit(solution)/shard_map/dot_general | solution.py:30
  19.1 0.7 fusion.22
  19.8 5.1 %collective-permute-done = bf16[192,1152]{1,0:T(8,128)(2,1)S(1)} collective-permute-done((bf16[192,1152]{1,0:T(8,128)(2,1)}, bf16[192,1152]{1,0:T(8,128)(2,1)S(1)}, u32[]{:S(2)}, u32[]{:S(2)}) %collective-permute-start) | collective-permute-done | bytes 442400 | tf_op jit(solution)/shard_map/ppermute | solution.py:12
  24.8 10.3 %collective-permute-start.1 = (bf16[192,1152]{1,0:T(8,128)(2,1)S(1)}, bf16[192,1152]{1,0:T(8,128)(2,1)S(1)}, u32[]{:S(2)}, u32[]{:S(2)}) collective-permute-start(bf16[192,1152]{1,0:T(8,128)(2,1)S(1)} %collective-permute-done), channel_id=1, source_target_pairs={{508,0},{0,4},{4,8},{8,12},{12,16},{16,20},{20,24},{24,28},{28,32}... | collective-permute-start | bytes 1327112 | tf_op jit(solution)/shard_map/ppermute | solution.py:12
  35.1 0.7 fusion.20
  35.9 0.7 convolution_add_fusion.1
  36.6 7.0 %collective-permute-done.1 = bf16[192,1152]{1,0:T(8,128)(2,1)S(1)} collective-permute-done((bf16[192,1152]{1,0:T(8,128)(2,1)S(1)}, bf16[192,1152]{1,0:T(8,128)(2,1)S(1)}, u32[]{:S(2)}, u32[]{:S(2)}) %collective-permute-start.1) | collective-permute-done | bytes 442400 | tf_op jit(solution)/shard_map/ppermute | solution.py:12
  43.7 0.7 fusion.19
  44.4 2.5 %fusion = f32[768,1152]{1,0:T(8,128)} fusion(f32[768,1152]{1,0:T(8,128)S(1)} %convolution_add_fusion.1, bf16[768,192]{0,1:T(8,128)(2,1)S(1)} %fusion.19, bf16[192,1152]{1,0:T(8,128)(2,1)S(1)} %collective-permute-done.1, f32[]{:T(128)} %bitcast), kind=kOutput, calls=%fused_computation.1 | convolution fusion | flops 341508096 | bytes 7815172 | tf_op jit(solution)/shard_map/dot_general | solution.py:39
  46.9 0.0 reduce-scatter.2.cloned.1.call-update
  46.9 0.6 convolution_multiply_fusion.2
  47.5 10.4 %collective-permute-start.2 = (f32[192,1152]{1,0:T(8,128)S(1)}, f32[192,1152]{1,0:T(8,128)S(1)}, u32[]{:S(2)}, u32[]{:S(2)}) collective-permute-start(f32[192,1152]{1,0:T(8,128)S(1)} %convolution_multiply_fusion.2), channel_id=1, source_target_pairs={{508,0},{0,4},{4,8},{8,12},{12,16},{16,20},{20,24},{24,28},{28,32}... | collective-permute-start | bytes 2654216 | tf_op jit(solution)/shard_map/ppermute | solution.py:12
  57.9 17.1 %collective-permute-done.2 = f32[192,1152]{1,0:T(8,128)S(1)} collective-permute-done((f32[192,1152]{1,0:T(8,128)S(1)}, f32[192,1152]{1,0:T(8,128)S(1)}, u32[]{:S(2)}, u32[]{:S(2)}) %collective-permute-start.2) | collective-permute-done | bytes 884768 | tf_op jit(solution)/shard_map/ppermute | solution.py:12
  75.0 0.6 fusion.1
  75.6 10.4 %collective-permute-start.3 = (f32[192,1152]{1,0:T(8,128)S(1)}, f32[192,1152]{1,0:T(8,128)S(1)}, u32[]{:S(2)}, u32[]{:S(2)}) collective-permute-start(f32[192,1152]{1,0:T(8,128)S(1)} %fusion.1), channel_id=1, source_target_pairs={{508,0},{0,4},{4,8},{8,12},{12,16},{16,20},{20,24},{24,28},{28,32}... | collective-permute-start | bytes 2654216 | tf_op jit(solution)/shard_map/ppermute | solution.py:12
  86.0 0.6 convolution_multiply_fusion
  86.6 53.5 %collective-permute-done.3 = f32[192,1152]{1,0:T(8,128)S(1)} collective-permute-done((f32[192,1152]{1,0:T(8,128)S(1)}, f32[192,1152]{1,0:T(8,128)S(1)}, u32[]{:S(2)}, u32[]{:S(2)}) %collective-permute-start.3) | collective-permute-done | bytes 884768 | tf_op jit(solution)/shard_map/ppermute | solution.py:12
  140.1 0.1 add.59
  140.2 1.9 %collective-permute-start.4 = (f32[192,1152]{1,0:T(8,128)S(1)}, f32[192,1152]{1,0:T(8,128)S(1)}, u32[]{:S(2)}, u32[]{:S(2)}) collective-permute-start(f32[192,1152]{1,0:T(8,128)S(1)} %add.59), channel_id=1, source_target_pairs={{8,0},{12,4},{16,8},{20,12},{24,16},{28,20},{32,24},{36,28},{40,32... | collective-permute-start | bytes 2654216 | tf_op jit(solution)/shard_map/ppermute | solution.py:12
  142.1 19.3 %collective-permute-done.4 = f32[192,1152]{1,0:T(8,128)S(1)} collective-permute-done((f32[192,1152]{1,0:T(8,128)S(1)}, f32[192,1152]{1,0:T(8,128)S(1)}, u32[]{:S(2)}, u32[]{:S(2)}) %collective-permute-start.4) | collective-permute-done | bytes 884768 | tf_op jit(solution)/shard_map/ppermute | solution.py:12
  161.5 0.9 copy.10
  (6 shorter events, 0.0 us)
Async XLA Ops:
  7.2 10.0 %copy-start = (bf16[768,1152]{1,0:T(8,128)(2,1)S(1)}, bf16[768,1152]{1,0:T(8,128)(2,1)}, u32[]{:S(2)}) copy-start(bf16[768,1152]{1,0:T(8,128)(2,1)} %param.5) | copy-start | bytes 5308420
  7.2 154.3 %reduce-scatter.2.cloned.1.call-start = ((), (), s32[]{:S(2)}) async-start(), calls=%async_computation.1 | async-start | bytes 4423680 | tf_op jit(solution)/shard_map/reduce_scatter | solution.py:60
  7.2 17.6 %collective-permute-start = (bf16[192,1152]{1,0:T(8,128)(2,1)}, bf16[192,1152]{1,0:T(8,128)(2,1)S(1)}, u32[]{:S(2)}, u32[]{:S(2)}) collective-permute-start(bf16[192,1152]{1,0:T(8,128)(2,1)} %param.6), channel_id=1, source_target_pairs={{508,0},{0,4},{4,8},{8,12},{12,16},{16,20},{20,24},{24,28},{28,32}... | collective-permute-start | bytes 1327112 | tf_op jit(solution)/shard_map/ppermute | solution.py:12
  17.2 1.9 %copy-start.1 = (bf16[192,1152]{1,0:T(8,128)(2,1)S(1)}, bf16[192,1152]{1,0:T(8,128)(2,1)}, u32[]{:S(2)}) copy-start(bf16[192,1152]{1,0:T(8,128)(2,1)} %param.6) | copy-start | bytes 1327108
  24.8 18.8 %collective-permute-start.1 = (bf16[192,1152]{1,0:T(8,128)(2,1)S(1)}, bf16[192,1152]{1,0:T(8,128)(2,1)S(1)}, u32[]{:S(2)}, u32[]{:S(2)}) collective-permute-start(bf16[192,1152]{1,0:T(8,128)(2,1)S(1)} %collective-permute-done), channel_id=1, source_target_pairs={{508,0},{0,4},{4,8},{8,12},{12,16},{16,20},{20,24},{24,28},{28,32}... | collective-permute-start | bytes 1327112 | tf_op jit(solution)/shard_map/ppermute | solution.py:12
  47.5 27.5 %collective-permute-start.2 = (f32[192,1152]{1,0:T(8,128)S(1)}, f32[192,1152]{1,0:T(8,128)S(1)}, u32[]{:S(2)}, u32[]{:S(2)}) collective-permute-start(f32[192,1152]{1,0:T(8,128)S(1)} %convolution_multiply_fusion.2), channel_id=1, source_target_pairs={{508,0},{0,4},{4,8},{8,12},{12,16},{16,20},{20,24},{24,28},{28,32}... | collective-permute-start | bytes 2654216 | tf_op jit(solution)/shard_map/ppermute | solution.py:12
  75.6 64.5 %collective-permute-start.3 = (f32[192,1152]{1,0:T(8,128)S(1)}, f32[192,1152]{1,0:T(8,128)S(1)}, u32[]{:S(2)}, u32[]{:S(2)}) collective-permute-start(f32[192,1152]{1,0:T(8,128)S(1)} %fusion.1), channel_id=1, source_target_pairs={{508,0},{0,4},{4,8},{8,12},{12,16},{16,20},{20,24},{24,28},{28,32}... | collective-permute-start | bytes 2654216 | tf_op jit(solution)/shard_map/ppermute | solution.py:12
  140.2 21.2 %collective-permute-start.4 = (f32[192,1152]{1,0:T(8,128)S(1)}, f32[192,1152]{1,0:T(8,128)S(1)}, u32[]{:S(2)}, u32[]{:S(2)}) collective-permute-start(f32[192,1152]{1,0:T(8,128)S(1)} %add.59), channel_id=1, source_target_pairs={{8,0},{12,4},{16,8},{20,12},{24,16},{28,20},{32,24},{36,28},{40,32... | collective-permute-start | bytes 2654216 | tf_op jit(solution)/shard_map/ppermute | solution.py:12
Sparse Core Ops, SparseCore 0:
  47.1 76.3 reduce-scatter.1
where the time goes:
time: 170 us; the launch traced here: 169 us
  waiting for transfers between devices  102 us (60%)
  starting transfers between devices  41 us (24%)
  between operations  15.5 us (9%)
  matrix products  8.97 us (5%)
    ppermute x5, waiting for transfers between devices, passed_along(): return lax.ppermute(block, axis, route)  102 us
    ppermute x5, starting transfers between devices, passed_along(): return lax.ppermute(block, axis, route)  40.9 us
    dot_general x3, matrix products, contribute(): jnp.dot(couple_weight, caption_rows, preferred_element_type=jnp.float32)  3.96 us
  transfers between devices with their start and end apart: 6, of which 5 were waited for; matrix products, arithmetic and copies ran while one was open for 4% of the time, Pallas kernels for 0%

commit v1 on v0

v1 whole, which is shorter than its diff:
```python
import jax
import jax.numpy as jnp
from jax import lax
from jax.sharding import PartitionSpec as P

BF = jnp.bfloat16
F32 = jnp.float32
AXES = ("blk", "grp")
X, Y = 4, 4


def route(distance):
    blocks, parts = lax.axis_size("blk"), lax.axis_size("grp")
    pairs = []
    for b in range(blocks):
        to = (b + distance) % blocks
        wraps = (b // X) % Y > (to // X) % Y
        for g in range(parts):
            pairs.append((b * parts + g, to * parts + (g ^ 2 if wraps else g)))
    return pairs


def sent(block, distance):
    return lax.ppermute(block, AXES, route(distance))


def returned(block, distance):
    return lax.ppermute(block, AXES, [(j, i) for i, j in route(distance)])


def swapped(block, bit):
    n = lax.axis_size("grp")
    return lax.ppermute(block, "grp", [(i, i ^ bit) for i in range(n)])


def on_device(photo, caption, matching_column, scale_exponent, score_intercept):
    scale = jnp.exp(scale_exponent[0])
    bias = score_intercept[0]
    width = caption.shape[0]
    place = lax.axis_index("grp")

    text1 = sent(caption, 1)

    def ordered(rows):
        parts = [
            lax.dynamic_slice_in_dim(rows, (place ^ bits) * width, width, 0)
            for bits in (3, 1, 2, 0)
        ]
        return jnp.concatenate(parts, 0)

    photo = ordered(photo)
    columns = place * width + lax.iota(jnp.int32, width)
    matched = ordered(matching_column[0])[:, None] == columns[None, :]
    own_target = jnp.where(matched, F32(1.0), F32(-1.0))

    def weight(text, target):
        scores = (
            scale
            * lax.dot_general(
                photo, text, (((1,), (1,)), ((), ())), preferred_element_type=F32
            )
            + bias
        )
        return (-target * jax.nn.sigmoid(-target * scores)).astype(BF)

    def text_term(w):
        return scale * lax.dot_general(
            w, photo, (((0,), (0,)), ((), ())), preferred_element_type=F32
        )

    w0 = weight(caption, own_target)
    going, w0 = lax.optimization_barrier((caption, w0))
    text2 = sent(going, 2)
    text_grad = text_term(w0)
    text1, text_grad = lax.optimization_barrier((text1, text_grad))
    w1 = weight(text1, F32(-1.0))
    term1 = text_term(w1).astype(BF)
    early = jnp.dot(w0, caption, preferred_element_type=F32) + jnp.dot(
        w1, text1, preferred_element_type=F32
    )
    text2, term1, early = lax.optimization_barrier((text2, term1, early))
    w2 = weight(text2, F32(-1.0))

    def image_part(rows):
        return scale * (
            early[rows] + jnp.dot(w2[rows], text2, preferred_element_type=F32)
        )

    give = image_part(slice(0, 2 * width)).astype(BF)
    give, w2, term1 = lax.optimization_barrier((give, w2, term1))
    got = swapped(give, 1)
    back1 = returned(term1, 1)
    keep = image_part(slice(2 * width, 4 * width))
    far = (keep[:width] + got[:width].astype(F32)).astype(BF)
    near = keep[width:] + got[width:].astype(F32)
    other = swapped(far, 2)
    back2 = returned(text_term(w2).astype(BF), 2)

    text_grad = text_grad + back1.astype(F32) + back2.astype(F32)
    text_grad, other = lax.optimization_barrier((text_grad, other))
    image_grad = near + other.astype(F32)
    return image_grad, text_grad


def solution(mesh):
    in_specs = (P("blk", None), P(("blk", "grp"), None), P("blk", None), P(), P())
    out_specs = (P(("blk", "grp"), None), P(("blk", "grp"), None))
    return jax.shard_map(
        on_device, mesh=mesh, in_specs=in_specs, out_specs=out_specs, check_vma=False
    )
```

time: 170 us -> 88.7 us (0.52)
  the two profiles are of different devices: /device:TPU:254 before, /device:TPU:1 now
where the time goes in v1:
time: 88.7 us; the launch traced here: 88.4 us
  waiting for transfers between devices  51.5 us (58%)
  starting transfers between devices  23.7 us (27%)
  matrix products  6.38 us (7%)
  local copies, waits for them, and re-layouts  2.46 us (3%)
  other arithmetic  2.23 us (3%)
  between operations  2.14 us (2%)
    ppermute x2, waiting for transfers between devices, returned(): return lax.ppermute(block, AXES, [(j, i) for i, j in route(distance)])  32.2 us
    ppermute x2, waiting for transfers between devices, sent(): return lax.ppermute(block, AXES, route(distance))  19.3 us
    ppermute x2, starting transfers between devices, sent(): return lax.ppermute(block, AXES, route(distance))  8.31 us
    ppermute x2, starting transfers between devices, swapped(): return lax.ppermute(block, 'grp', [(i, i ^ bit) for i in range(n)])  8.05 us
    ppermute x2, starting transfers between devices, returned(): return lax.ppermute(block, AXES, [(j, i) for i, j in route(distance)])  7.36 us
    dynamic_slice x2, local copies, waits for them, and re-layouts, ordered(): lax.dynamic_slice_in_dim(rows, (place ^ bits) * width, width, 0)  2.46 us
    dot_general x3, matrix products, weight(): lax.dot_general(photo, text, (((1,), (1,)), ((), ())), preferred_element_...  2.26 us
  transfers between devices with their start and end apart: 6, of which 4 were waited for; matrix products, arithmetic and copies ran while one was open for 10% of the time, Pallas kernels for 0%

profile of v1, /device:TPU:1, one launch (start us, length us, event | category | flops | bytes accessed | tf_op | source)
XLA Modules:
  0.0 88.4 jit_solution(2906968097077434558)
XLA Ops:
  0.6 4.0 %collective-permute-start.1 = (bf16[192,1152]{1,0:T(8,128)(2,1)}, bf16[192,1152]{1,0:T(8,128)(2,1)S(1)}, u32[]{:S(2)}, u32[]{:S(2)}) collective-permute-start(bf16[192,1152]{1,0:T(8,128)(2,1)} %param.6), channel_id=1, source_target_pairs={{0,4},{1,5},{2,6},{3,7},{4,8},{5,9},{6,10},{7,11},{8,12},{9,13},{1... | collective-permute-start | bytes 1327112 | tf_op jit(solution)/shard_map/ppermute | solution.py:24
  6.0 0.8 constant_dynamic-slice_fusion.7
  6.8 1.6 %constant_dynamic-slice_fusion.3 = (bf16[192,1152]{1,0:T(8,128)(2,1)S(1)}, bf16[192,1152]{1,0:T(8,128)(2,1)S(1)}, bf16[192,1152]{1,0:T(8,128)(2,1)S(1)}, bf16[192,1152]{1,0:T(8,128)(2,1)S(1)}) fusion(bf16[768,1152]{1,0:T(8,128)(2,1)} %param.5, s32[]{:T(128)S(6)} %select_n.20, s32[]{:T(128)S(6)} %select_n.21, s32[]{:T(128)S(6)} %select_n.23, s32[]{:T(128)S(6)} %select_n.22), kind=kLoop, calls=%fused_computation.45 | loop fusion | bytes 3538960 | tf_op jit(solution)/shard_map/dynamic_slice | solution.py:46
  8.5 0.8 fusion.21
  9.3 4.4 %collective-permute-start = (bf16[192,1152]{1,0:T(8,128)(2,1)S(1)}, bf16[192,1152]{1,0:T(8,128)(2,1)S(1)}, u32[]{:S(2)}, u32[]{:S(2)}) collective-permute-start(bf16[192,1152]{1,0:T(8,128)(2,1)S(1)} %copy-done), channel_id=1, source_target_pairs={{0,8},{1,9},{2,10},{3,11},{4,12},{5,13},{6,14},{7,15},{8,16},{9,17... | collective-permute-start | bytes 1327112 | tf_op jit(solution)/shard_map/ppermute | solution.py:24
  13.7 0.6 convolution_multiply_fusion.2
  14.2 0.7 fusion.32
  15.0 13.1 %collective-permute-done.1 = bf16[192,1152]{1,0:T(8,128)(2,1)S(1)} collective-permute-done((bf16[192,1152]{1,0:T(8,128)(2,1)}, bf16[192,1152]{1,0:T(8,128)(2,1)S(1)}, u32[]{:S(2)}, u32[]{:S(2)}) %collective-permute-start.1) | collective-permute-done | bytes 442400 | tf_op jit(solution)/shard_map/ppermute | solution.py:24
  28.1 0.7 fusion.20
  28.8 0.6 fusion
  29.4 0.7 convolution_add_fusion
  30.1 6.2 %collective-permute-done = bf16[192,1152]{1,0:T(8,128)(2,1)S(1)} collective-permute-done((bf16[192,1152]{1,0:T(8,128)(2,1)S(1)}, bf16[192,1152]{1,0:T(8,128)(2,1)S(1)}, u32[]{:S(2)}, u32[]{:S(2)}) %collective-permute-start) | collective-permute-done | bytes 442400 | tf_op jit(solution)/shard_map/ppermute | solution.py:24
  36.3 0.7 fusion.19
  37.1 0.5 multiply_convert_fusion
  37.5 3.6 %collective-permute-start.2 = (bf16[384,1152]{1,0:T(8,128)(2,1)S(1)}, bf16[384,1152]{1,0:T(8,128)(2,1)S(1)}, u32[]{:S(2)}, u32[]{:S(2)}) collective-permute-start(bf16[384,1152]{1,0:T(8,128)(2,1)S(1)} %multiply_convert_fusion), channel_id=1, source_target_pairs={{0,1},{1,0},{2,3},{3,2},{4,5},{5,4},{6,7},{7,6},{8,9},{9,8},{10,11... | collective-permute-start | bytes 2654216 | tf_op jit(solution)/shard_map/ppermute | solution.py:33
  41.2 5.4 %collective-permute-start.3 = (bf16[192,1152]{1,0:T(8,128)(2,1)S(1)}, bf16[192,1152]{1,0:T(8,128)(2,1)S(1)}, u32[]{:S(2)}, u32[]{:S(2)}) collective-permute-start(bf16[192,1152]{1,0:T(8,128)(2,1)S(1)} %fusion), channel_id=1, source_target_pairs={{4,0},{5,1},{6,2},{7,3},{8,4},{9,5},{10,6},{11,7},{12,8},{13,9},{1... | collective-permute-start | bytes 1327112 | tf_op jit(solution)/shard_map/ppermute | solution.py:28
  46.6 0.6 fusion.1
  47.2 1.9 %collective-permute-start.4 = (bf16[192,1152]{1,0:T(8,128)(2,1)S(1)}, bf16[192,1152]{1,0:T(8,128)(2,1)S(1)}, u32[]{:S(2)}, u32[]{:S(2)}) collective-permute-start(bf16[192,1152]{1,0:T(8,128)(2,1)S(1)} %fusion.1), channel_id=1, source_target_pairs={{8,0},{9,1},{10,2},{11,3},{12,4},{13,5},{14,6},{15,7},{16,8},{17,9... | collective-permute-start | bytes 1327112 | tf_op jit(solution)/shard_map/ppermute | solution.py:28
  49.1 0.5 add_multiply_fusion
  49.7 4.4 %collective-permute-start.5 = (bf16[192,1152]{1,0:T(8,128)(2,1)S(1)}, bf16[192,1152]{1,0:T(8,128)(2,1)S(1)}, u32[]{:S(2)}, u32[]{:S(2)}) collective-permute-start(bf16[192,1152]{1,0:T(8,128)(2,1)S(1)} %fusion.22), channel_id=1, source_target_pairs={{0,2},{1,3},{2,0},{3,1},{4,6},{5,7},{6,4},{7,5},{8,10},{9,11},{10,... | collective-permute-start | bytes 1327112 | tf_op jit(solution)/shard_map/ppermute | solution.py:33
  54.1 6.3 %collective-permute-done.3 = bf16[192,1152]{1,0:T(8,128)(2,1)S(1)} collective-permute-done((bf16[192,1152]{1,0:T(8,128)(2,1)S(1)}, bf16[192,1152]{1,0:T(8,128)(2,1)S(1)}, u32[]{:S(2)}, u32[]{:S(2)}) %collective-permute-start.3) | collective-permute-done | bytes 442400 | tf_op jit(solution)/shard_map/ppermute | solution.py:28
  60.5 25.8 %collective-permute-done.4 = bf16[192,1152]{1,0:T(8,128)(2,1)S(1)} collective-permute-done((bf16[192,1152]{1,0:T(8,128)(2,1)S(1)}, bf16[192,1152]{1,0:T(8,128)(2,1)S(1)}, u32[]{:S(2)}, u32[]{:S(2)}) %collective-permute-start.4) | collective-permute-done | bytes 442400 | tf_op jit(solution)/shard_map/ppermute | solution.py:28
  86.3 1.0 %convert_add_fusion = f32[192,1152]{1,0:T(8,128)} fusion(bf16[192,1152]{1,0:T(8,128)(2,1)S(1)} %collective-permute-done.4, f32[192,1152]{1,0:T(8,128)S(1)} %convolution_multiply_fusion.2, bf16[192,1152]{1,0:T(8,128)(2,1)S(1)} %collective-permute-done.3), kind=kLoop, calls=%fused_computation.36 | loop fusion | flops 884736 | bytes 2654208 | tf_op jit(solution)/shard_map/add | solution.py:99
  87.4 1.0 %fusion.23 = f32[192,1152]{1,0:T(8,128)} fusion(f32[384,1152]{1,0:T(8,128)S(1)} %add_multiply_fusion, bf16[192,1152]{1,0:T(8,128)(2,1)S(1)} %collective-permute-done.5, bf16[384,1152]{1,0:T(8,128)(2,1)S(1)} %collective-permute-done.2), kind=kLoop, calls=%fused_computation.35 | loop fusion | flops 884736 | bytes 2654208 | tf_op jit(solution)/shard_map/add | solution.py:101
  (7 shorter events, 0.2 us)
Async XLA Ops:
  0.6 27.4 %collective-permute-start.1 = (bf16[192,1152]{1,0:T(8,128)(2,1)}, bf16[192,1152]{1,0:T(8,128)(2,1)S(1)}, u32[]{:S(2)}, u32[]{:S(2)}) collective-permute-start(bf16[192,1152]{1,0:T(8,128)(2,1)} %param.6), channel_id=1, source_target_pairs={{0,4},{1,5},{2,6},{3,7},{4,8},{5,9},{6,10},{7,11},{8,12},{9,13},{1... | collective-permute-start | bytes 1327112 | tf_op jit(solution)/shard_map/ppermute | solution.py:24
  6.8 1.7 %copy-start = (bf16[192,1152]{1,0:T(8,128)(2,1)S(1)}, bf16[192,1152]{1,0:T(8,128)(2,1)}, u32[]{:S(2)}) copy-start(bf16[192,1152]{1,0:T(8,128)(2,1)} %param.6) | copy-start | bytes 1327108
  9.3 27.0 %collective-permute-start = (bf16[192,1152]{1,0:T(8,128)(2,1)S(1)}, bf16[192,1152]{1,0:T(8,128)(2,1)S(1)}, u32[]{:S(2)}, u32[]{:S(2)}) collective-permute-start(bf16[192,1152]{1,0:T(8,128)(2,1)S(1)} %copy-done), channel_id=1, source_target_pairs={{0,8},{1,9},{2,10},{3,11},{4,12},{5,13},{6,14},{7,15},{8,16},{9,17... | collective-permute-start | bytes 1327112 | tf_op jit(solution)/shard_map/ppermute | solution.py:24
  37.5 12.1 %collective-permute-start.2 = (bf16[384,1152]{1,0:T(8,128)(2,1)S(1)}, bf16[384,1152]{1,0:T(8,128)(2,1)S(1)}, u32[]{:S(2)}, u32[]{:S(2)}) collective-permute-start(bf16[384,1152]{1,0:T(8,128)(2,1)S(1)} %multiply_convert_fusion), channel_id=1, source_target_pairs={{0,1},{1,0},{2,3},{3,2},{4,5},{5,4},{6,7},{7,6},{8,9},{9,8},{10,11... | collective-permute-start | bytes 2654216 | tf_op jit(solution)/shard_map/ppermute | solution.py:33
  41.2 19.3 %collective-permute-start.3 = (bf16[192,1152]{1,0:T(8,128)(2,1)S(1)}, bf16[192,1152]{1,0:T(8,128)(2,1)S(1)}, u32[]{:S(2)}, u32[]{:S(2)}) collective-permute-start(bf16[192,1152]{1,0:T(8,128)(2,1)S(1)} %fusion), channel_id=1, source_target_pairs={{4,0},{5,1},{6,2},{7,3},{8,4},{9,5},{10,6},{11,7},{12,8},{13,9},{1... | collective-permute-start | bytes 1327112 | tf_op jit(solution)/shard_map/ppermute | solution.py:28
  47.2 39.1 %collective-permute-start.4 = (bf16[192,1152]{1,0:T(8,128)(2,1)S(1)}, bf16[192,1152]{1,0:T(8,128)(2,1)S(1)}, u32[]{:S(2)}, u32[]{:S(2)}) collective-permute-start(bf16[192,1152]{1,0:T(8,128)(2,1)S(1)} %fusion.1), channel_id=1, source_target_pairs={{8,0},{9,1},{10,2},{11,3},{12,4},{13,5},{14,6},{15,7},{16,8},{17,9... | collective-permute-start | bytes 1327112 | tf_op jit(solution)/shard_map/ppermute | solution.py:28
  49.7 37.7 %collective-permute-start.5 = (bf16[192,1152]{1,0:T(8,128)(2,1)S(1)}, bf16[192,1152]{1,0:T(8,128)(2,1)S(1)}, u32[]{:S(2)}, u32[]{:S(2)}) collective-permute-start(bf16[192,1152]{1,0:T(8,128)(2,1)S(1)} %fusion.22), channel_id=1, source_target_pairs={{0,2},{1,3},{2,0},{3,1},{4,6},{5,7},{6,4},{7,5},{8,10},{9,11},{10,... | collective-permute-start | bytes 1327112 | tf_op jit(solution)/shard_map/ppermute | solution.py:33

commit v2 on v1

--- a/solution.py
+++ b/solution.py
@@ -24,8 +24,19 @@
     return lax.ppermute(block, AXES, route(distance))
 
 
-def returned(block, distance):
-    return lax.ppermute(block, AXES, [(j, i) for i, j in route(distance)])
+def turned(block, distance):
+    blocks = lax.axis_size("blk")
+    return lax.ppermute(
+        block,
+        "blk",
+        [(b, b // X * X + (b - distance) % X) for b in range(blocks)],
+    )
+
+
+def handed_down(block):
+    parts = lax.axis_size("grp")
+    crossing = [(i, j) for i, j in route(X) if i // parts % X >= X - 2]
+    return lax.ppermute(block, AXES, [(j, i) for i, j in crossing])
 
 
 def swapped(block, bit):
@@ -89,16 +100,24 @@
     give = image_part(slice(0, 2 * width)).astype(BF)
     give, w2, term1 = lax.optimization_barrier((give, w2, term1))
     got = swapped(give, 1)
-    back1 = returned(term1, 1)
+    back1 = turned(term1, 1)
     keep = image_part(slice(2 * width, 4 * width))
     far = (keep[:width] + got[:width].astype(F32)).astype(BF)
     near = keep[width:] + got[width:].astype(F32)
+    back2 = turned(text_term(w2).astype(BF), 2)
     other = swapped(far, 2)
-    back2 = returned(text_term(w2).astype(BF), 2)
+    x = lax.axis_index("blk") % X
+    back1, back2 = back1.astype(F32), back2.astype(F32)
+    down = handed_down(jnp.where(x == X - 1, back1 + back2, back2).astype(BF))
+    text_grad = (
+        text_grad
+        + jnp.where(x == X - 1, F32(0.0), back1)
+        + jnp.where(x >= X - 2, F32(0.0), back2)
+    )
 
-    text_grad = text_grad + back1.astype(F32) + back2.astype(F32)
-    text_grad, other = lax.optimization_barrier((text_grad, other))
     image_grad = near + other.astype(F32)
+    image_grad, down = lax.optimization_barrier((image_grad, down))
+    text_grad = text_grad + down.astype(F32)
     return image_grad, text_grad
 
 

time: 88.7 us -> 85 us (0.958)
  the two profiles are of different devices: /device:TPU:1 before, /device:TPU:6 now
where the time goes in v2:
time: 85 us; the launch traced here: 84.5 us
  starting transfers between devices  40.1 us (47%)
  waiting for transfers between devices  23.6 us (28%)
  matrix products  11.6 us (14%)
  other arithmetic  4.49 us (5%)
  local copies, waits for them, and re-layouts  2.51 us (3%)
  between operations  2.33 us (3%)
    ppermute x2, starting transfers between devices, turned(): lax.ppermute(block, 'blk', [(b, b // X * X + (b - distance) % X) for b in...  17.8 us
    ppermute x2, waiting for transfers between devices, turned(): lax.ppermute(block, 'blk', [(b, b // X * X + (b - distance) % X) for b in...  11.3 us
    ppermute x1, starting transfers between devices, handed_down(): return lax.ppermute(block, AXES, [(j, i) for i, j in crossing])  7.8 us
    ppermute x2, starting transfers between devices, sent(): return lax.ppermute(block, AXES, route(distance))  7.73 us
    ppermute x1, waiting for transfers between devices, handed_down(): return lax.ppermute(block, AXES, [(j, i) for i, j in crossing])  7.59 us
    ppermute x2, starting transfers between devices, swapped(): return lax.ppermute(block, 'grp', [(i, i ^ bit) for i in range(n)])  6.75 us
    dot_general x3, matrix products, text_term(): lax.dot_general(w, photo, (((0,), (0,)), ((), ())), preferred_element_typ...  4.97 us
    ppermute x2, waiting for transfers between devices, sent(): return lax.ppermute(block, AXES, route(distance))  4.61 us
  transfers between devices with their start and end apart: 7, of which 4 were waited for; matrix products, arithmetic and copies ran while one was open for 18% of the time, Pallas kernels for 0%

profile of v2, /device:TPU:6, one launch (start us, length us, event | category | flops | bytes accessed | tf_op | source)
XLA Modules:
  0.0 84.5 jit_solution(9178589026637171021)
XLA Ops:
  0.6 3.4 %collective-permute-start.1 = (bf16[192,1152]{1,0:T(8,128)(2,1)}, bf16[192,1152]{1,0:T(8,128)(2,1)S(1)}, u32[]{:S(2)}, u32[]{:S(2)}) collective-permute-start(bf16[192,1152]{1,0:T(8,128)(2,1)} %param.6), channel_id=1, source_target_pairs={{0,4},{1,5},{2,6},{3,7},{4,8},{5,9},{6,10},{7,11},{8,12},{9,13},{1... | collective-permute-start | bytes 1327112 | tf_op jit(solution)/shard_map/ppermute | solution.py:24
  4.1 0.8 %constant_dynamic-slice_fusion.7 = (s32[1,192]{1,0:T(1,128)S(1)}, s32[1,192]{1,0:T(1,128)S(1)}, s32[1,192]{1,0:T(1,128)S(1)}, s32[1,192]{1,0:T(1,128)S(1)}) fusion(s32[1,768]{1,0:T(1,128)} %param.7, s32[]{:T(128)S(6)} %select_n.47, s32[]{:T(128)S(6)} %select_n.48, s32[]{:T(128)S(6)} %select_n.50, s32[]{:T(128)S(6)} %select_n.49), kind=kLoop, calls=%fused_computation.55 | loop fusion | bytes 6160 | tf_op jit(solution)/shard_map/dynamic_slice | solution.py:57
  4.9 1.6 %constant_dynamic-slice_fusion.3 = (bf16[192,1152]{1,0:T(8,128)(2,1)S(1)}, bf16[192,1152]{1,0:T(8,128)(2,1)S(1)}, bf16[192,1152]{1,0:T(8,128)(2,1)S(1)}, bf16[192,1152]{1,0:T(8,128)(2,1)S(1)}) fusion(bf16[768,1152]{1,0:T(8,128)(2,1)} %param.5, s32[]{:T(128)S(6)} %select_n.47, s32[]{:T(128)S(6)} %select_n.48, s32[]{:T(128)S(6)} %select_n.50, s32[]{:T(128)S(6)} %select_n.49), kind=kLoop, calls=%fused_computation.51 | loop fusion | bytes 3538960 | tf_op jit(solution)/shard_map/dynamic_slice | solution.py:57
  8.0 0.8 fusion.21
  8.8 4.3 %collective-permute-start = (bf16[192,1152]{1,0:T(8,128)(2,1)S(1)}, bf16[192,1152]{1,0:T(8,128)(2,1)S(1)}, u32[]{:S(2)}, u32[]{:S(2)}) collective-permute-start(bf16[192,1152]{1,0:T(8,128)(2,1)S(1)} %copy-done.3), channel_id=1, source_target_pairs={{0,8},{1,9},{2,10},{3,11},{4,12},{5,13},{6,14},{7,15},{8,16},{9,17... | collective-permute-start | bytes 1327112 | tf_op jit(solution)/shard_map/ppermute | solution.py:24
  13.2 1.5 %convolution_multiply_fusion.2 = f32[192,1152]{1,0:T(8,128)} fusion(bf16[768,192]{0,1:T(8,128)(2,1)S(1)} %fusion.21, f32[]{:T(128)} %bitcast, bf16[192,1152]{1,0:T(8,128)(2,1)S(1)} %get-tuple-element.28, bf16[192,1152]{1,0:T(8,128)(2,1)S(1)} %get-tuple-element.29, bf16[192,1152]{1,0:T(8,128)(2,1)S(1)} %get-tuple-element.27, ...), kind=kOutput, calls=%fused_computation.3 | convolution fusion | flops 347037696 | bytes 2949124 | tf_op jit(solution)/shard_map/dot_general | solution.py:78
  15.4 0.7 fusion.20
  16.2 1.3 %fusion = bf16[192,1152]{1,0:T(8,128)(2,1)} fusion(bf16[768,192]{0,1:T(8,128)(2,1)S(1)} %fusion.20, f32[]{:T(128)} %bitcast, bf16[192,1152]{1,0:T(8,128)(2,1)S(1)} %get-tuple-element.28, bf16[192,1152]{1,0:T(8,128)(2,1)S(1)} %get-tuple-element.29, bf16[192,1152]{1,0:T(8,128)(2,1)S(1)} %get-tuple-element.27, bf16[192,1152]{1,0:T(8,128)(2,1)S(1)} %get-tuple-element.26), kind=kOutput, calls=%fused_computation.4 | convolution fusion | flops 347258880 | bytes 2506756 | tf_op jit(solution)/shard_map/dot_general | solution.py:78
  17.5 1.8 %convolution_add_fusion = f32[768,1152]{1,0:T(8,128)S(1)} fusion(f32[768,1152]{1,0:T(8,128)S(1)} %fusion.36, bf16[768,192]{0,1:T(8,128)(2,1)S(1)} %fusion.20, bf16[192,1152]{1,0:T(8,128)(2,1)} %copy-done.8), kind=kOutput, calls=%fused_computation | convolution fusion | flops 340623360 | bytes 7815168 | tf_op jit(solution)/shard_map/dot_general | solution.py:89
  19.2 4.6 %collective-permute-done = bf16[192,1152]{1,0:T(8,128)(2,1)S(1)} collective-permute-done((bf16[192,1152]{1,0:T(8,128)(2,1)S(1)}, bf16[192,1152]{1,0:T(8,128)(2,1)S(1)}, u32[]{:S(2)}, u32[]{:S(2)}) %collective-permute-start) | collective-permute-done | bytes 442400 | tf_op jit(solution)/shard_map/ppermute | solution.py:24
  23.9 0.7 fusion.19
  24.6 1.4 %multiply_convert_fusion = bf16[384,1152]{1,0:T(8,128)(2,1)} fusion(f32[768,1152]{1,0:T(8,128)S(1)} %convolution_add_fusion, f32[]{:T(128)} %bitcast, bf16[192,1152]{1,0:T(8,128)(2,1)S(1)} %collective-permute-done, bf16[768,192]{0,1:T(8,128)(2,1)S(1)} %fusion.19), kind=kOutput, calls=%fused_computation.8 | convolution fusion | flops 171196416 | bytes 3244036 | tf_op jit(solution)/shard_map/dot_general | solution.py:97
  26.0 1.9 %collective-permute-start.2 = (bf16[384,1152]{1,0:T(8,128)(2,1)}, bf16[384,1152]{1,0:T(8,128)(2,1)}, u32[]{:S(2)}, u32[]{:S(2)}) collective-permute-start(bf16[384,1152]{1,0:T(8,128)(2,1)} %multiply_convert_fusion), channel_id=1, source_target_pairs={{0,1},{1,0},{2,3},{3,2},{4,5},{5,4},{6,7},{7,6},{8,9},{9,8},{10,11... | collective-permute-start | bytes 2654216 | tf_op jit(solution)/shard_map/ppermute | solution.py:44
  28.0 2.2 %fusion.1 = bf16[192,1152]{1,0:T(8,128)(2,1)S(1)} fusion(bf16[768,192]{0,1:T(8,128)(2,1)} %copy-done.9, f32[]{:T(128)} %bitcast, bf16[192,1152]{1,0:T(8,128)(2,1)} %copy-done.6, bf16[192,1152]{1,0:T(8,128)(2,1)} %copy-done.7, bf16[192,1152]{1,0:T(8,128)(2,1)} %copy-done.5, bf16[192,1152]{1,0:T(8,128)(2,1)} %copy-done.4), kind=kOutput, calls=%fused_computation.5 | convolution fusion | flops 347258880 | bytes 2506756 | tf_op jit(solution)/shard_map/dot_general | solution.py:78
  30.2 15.4 %collective-permute-start.5 = (bf16[192,1152]{1,0:T(8,128)(2,1)S(1)}, bf16[192,1152]{1,0:T(8,128)(2,1)S(1)}, u32[]{:S(2)}, u32[]{:S(2)}) collective-permute-start(bf16[192,1152]{1,0:T(8,128)(2,1)S(1)} %fusion.1), channel_id=1, source_target_pairs={{0,8},{4,12},{8,0},{12,4},{16,24},{20,28},{24,16},{28,20},{32,40},... | collective-permute-start | bytes 1327112 | tf_op jit(solution)/shard_map/ppermute | solution.py:29
  45.5 2.5 %collective-permute-start.4 = (bf16[192,1152]{1,0:T(8,128)(2,1)S(1)}, bf16[192,1152]{1,0:T(8,128)(2,1)S(1)}, u32[]{:S(2)}, u32[]{:S(2)}) collective-permute-start(bf16[192,1152]{1,0:T(8,128)(2,1)S(1)} %copy-done.11), channel_id=1, source_target_pairs={{0,12},{4,0},{8,4},{12,8},{16,28},{20,16},{24,20},{28,24},{32,44},... | collective-permute-start | bytes 1327112 | tf_op jit(solution)/shard_map/ppermute | solution.py:29
  48.5 1.1 %fusion.26 = bf16[192,1152]{1,0:T(8,128)(2,1)S(1)} fusion(f32[384,1152]{1,0:T(8,128)S(1)} %add_multiply_fusion, bf16[384,1152]{1,0:T(8,128)(2,1)} %collective-permute-done.2), kind=kLoop, calls=%fused_computation.40 | loop fusion | flops 663552 | bytes 1769472 | tf_op jit(solution)/shard_map/convert_element_type | solution.py:105
  49.6 4.8 %collective-permute-start.3 = (bf16[192,1152]{1,0:T(8,128)(2,1)S(1)}, bf16[192,1152]{1,0:T(8,128)(2,1)S(1)}, u32[]{:S(2)}, u32[]{:S(2)}) collective-permute-start(bf16[192,1152]{1,0:T(8,128)(2,1)S(1)} %fusion.26), channel_id=1, source_target_pairs={{0,2},{1,3},{2,0},{3,1},{4,6},{5,7},{6,4},{7,5},{8,10},{9,11},{10,... | collective-permute-start | bytes 1327112 | tf_op jit(solution)/shard_map/ppermute | solution.py:44
  54.5 2.1 %collective-permute-done.5 = bf16[192,1152]{1,0:T(8,128)(2,1)S(1)} collective-permute-done((bf16[192,1152]{1,0:T(8,128)(2,1)S(1)}, bf16[192,1152]{1,0:T(8,128)(2,1)S(1)}, u32[]{:S(2)}, u32[]{:S(2)}) %collective-permute-start.5) | collective-permute-done | bytes 442400 | tf_op jit(solution)/shard_map/ppermute | solution.py:29
  56.6 9.2 %collective-permute-done.4 = bf16[192,1152]{1,0:T(8,128)(2,1)S(1)} collective-permute-done((bf16[192,1152]{1,0:T(8,128)(2,1)S(1)}, bf16[192,1152]{1,0:T(8,128)(2,1)S(1)}, u32[]{:S(2)}, u32[]{:S(2)}) %collective-permute-start.4) | collective-permute-done | bytes 442400 | tf_op jit(solution)/shard_map/ppermute | solution.py:29
  66.0 7.8 %collective-permute-start.6 = (bf16[192,1152]{1,0:T(8,128)(2,1)S(1)}, bf16[192,1152]{1,0:T(8,128)(2,1)S(1)}, u32[]{:S(2)}, u32[]{:S(2)}) collective-permute-start(bf16[192,1152]{1,0:T(8,128)(2,1)S(1)} %fusion.25), channel_id=1, source_target_pairs={{24,8},{25,9},{26,10},{27,11},{28,12},{29,13},{30,14},{31,15},{40,... | collective-permute-start | bytes 1327112 | tf_op jit(solution)/shard_map/ppermute | solution.py:39
  73.8 2.0 %fusion.27 = f32[192,1152]{1,0:T(8,128)} fusion(f32[384,1152]{1,0:T(8,128)S(1)} %add_multiply_fusion, bf16[192,1152]{1,0:T(8,128)(2,1)S(1)} %collective-permute-done.3, bf16[384,1152]{1,0:T(8,128)(2,1)} %collective-permute-done.2), kind=kLoop, calls=%fused_computation.42 | loop fusion | flops 884736 | bytes 2654208 | tf_op jit(solution)/shard_map/add | solution.py:118
  75.8 7.6 %collective-permute-done.6 = bf16[192,1152]{1,0:T(8,128)(2,1)S(1)} collective-permute-done((bf16[192,1152]{1,0:T(8,128)(2,1)S(1)}, bf16[192,1152]{1,0:T(8,128)(2,1)S(1)}, u32[]{:S(2)}, u32[]{:S(2)}) %collective-permute-start.6) | collective-permute-done | bytes 442400 | tf_op jit(solution)/shard_map/ppermute | solution.py:39
  83.4 1.1 %fusion.24 = f32[192,1152]{1,0:T(8,128)} fusion(f32[192,1152]{1,0:T(8,128)S(1)} %copy-done.2, bf16[192,1152]{1,0:T(8,128)(2,1)S(1)} %collective-permute-done.4, bf16[192,1152]{1,0:T(8,128)(2,1)S(1)} %collective-permute-done.5, bf16[192,1152]{1,0:T(8,128)(2,1)S(1)} %collective-permute-done.6, pred[]{:T(512)S(6)} %ge.3, pred[]{:T(512)S(6)} %eq.22), kind=kLoop, calls=%fused_computation.37 | loop fusion | flops 1769472 | bytes 3096578 | tf_op jit(solution)/shard_map/add | solution.py:120
  (32 shorter events, 1.5 us)
Async XLA Ops:
  0.6 14.7 %collective-permute-start.1 = (bf16[192,1152]{1,0:T(8,128)(2,1)}, bf16[192,1152]{1,0:T(8,128)(2,1)S(1)}, u32[]{:S(2)}, u32[]{:S(2)}) collective-permute-start(bf16[192,1152]{1,0:T(8,128)(2,1)} %param.6), channel_id=1, source_target_pairs={{0,4},{1,5},{2,6},{3,7},{4,8},{5,9},{6,10},{7,11},{8,12},{9,13},{1... | collective-permute-start | bytes 1327112 | tf_op jit(solution)/shard_map/ppermute | solution.py:24
  4.9 3.1 %copy-start.3 = (bf16[192,1152]{1,0:T(8,128)(2,1)S(1)}, bf16[192,1152]{1,0:T(8,128)(2,1)}, u32[]{:S(2)}) copy-start(bf16[192,1152]{1,0:T(8,128)(2,1)} %param.6) | copy-start | bytes 1327108
  6.5 17.3 %copy-start.4 = (bf16[192,1152]{1,0:T(8,128)(2,1)}, bf16[192,1152]{1,0:T(8,128)(2,1)S(1)}, u32[]{:S(2)}) copy-start(bf16[192,1152]{1,0:T(8,128)(2,1)S(1)} %get-tuple-element.26) | copy-start | bytes 1327108
  6.6 17.3 %copy-start.5 = (bf16[192,1152]{1,0:T(8,128)(2,1)}, bf16[192,1152]{1,0:T(8,128)(2,1)S(1)}, u32[]{:S(2)}) copy-start(bf16[192,1152]{1,0:T(8,128)(2,1)S(1)} %get-tuple-element.27) | copy-start | bytes 1327108
  6.6 17.3 %copy-start.6 = (bf16[192,1152]{1,0:T(8,128)(2,1)}, bf16[192,1152]{1,0:T(8,128)(2,1)S(1)}, u32[]{:S(2)}) copy-start(bf16[192,1152]{1,0:T(8,128)(2,1)S(1)} %get-tuple-element.28) | copy-start | bytes 1327108
  6.6 17.3 %copy-start.7 = (bf16[192,1152]{1,0:T(8,128)(2,1)}, bf16[192,1152]{1,0:T(8,128)(2,1)S(1)}, u32[]{:S(2)}) copy-start(bf16[192,1152]{1,0:T(8,128)(2,1)S(1)} %get-tuple-element.29) | copy-start | bytes 1327108
  8.8 15.0 %collective-permute-start = (bf16[192,1152]{1,0:T(8,128)(2,1)S(1)}, bf16[192,1152]{1,0:T(8,128)(2,1)S(1)}, u32[]{:S(2)}, u32[]{:S(2)}) collective-permute-start(bf16[192,1152]{1,0:T(8,128)(2,1)S(1)} %copy-done.3), channel_id=1, source_target_pairs={{0,8},{1,9},{2,10},{3,11},{4,12},{5,13},{6,14},{7,15},{8,16},{9,17... | collective-permute-start | bytes 1327112 | tf_op jit(solution)/shard_map/ppermute | solution.py:24
  15.4 0.8 copy-start.8
  23.9 0.8 copy-start
  24.6 1.4 %copy-start.9 = (bf16[768,192]{0,1:T(8,128)(2,1)}, bf16[768,192]{0,1:T(8,128)(2,1)S(1)}, u32[]{:S(2)}) copy-start(bf16[768,192]{0,1:T(8,128)(2,1)S(1)} %fusion.19) | copy-start | bytes 884740
  26.0 22.5 %collective-permute-start.2 = (bf16[384,1152]{1,0:T(8,128)(2,1)}, bf16[384,1152]{1,0:T(8,128)(2,1)}, u32[]{:S(2)}, u32[]{:S(2)}) collective-permute-start(bf16[384,1152]{1,0:T(8,128)(2,1)} %multiply_convert_fusion), channel_id=1, source_target_pairs={{0,1},{1,0},{2,3},{3,2},{4,5},{5,4},{6,7},{7,6},{8,9},{9,8},{10,11... | collective-permute-start | bytes 2654216 | tf_op jit(solution)/shard_map/ppermute | solution.py:44
  28.0 17.6 %copy-start.11 = (bf16[192,1152]{1,0:T(8,128)(2,1)S(1)}, bf16[192,1152]{1,0:T(8,128)(2,1)}, u32[]{:S(2)}) copy-start(bf16[192,1152]{1,0:T(8,128)(2,1)} %fusion) | copy-start | bytes 1327108
  28.0 20.0 %copy-start.1 = (bf16[192,1152]{1,0:T(8,128)(2,1)S(1)}, bf16[192,1152]{1,0:T(8,128)(2,1)}, u32[]{:S(2)}) copy-start(bf16[192,1152]{1,0:T(8,128)(2,1)} %copy-done) | copy-start | bytes 1327108
  28.0 20.0 %copy-start.10 = (bf16[768,192]{0,1:T(8,128)(2,1)S(1)}, bf16[768,192]{0,1:T(8,128)(2,1)}, u32[]{:S(2)}) copy-start(bf16[768,192]{0,1:T(8,128)(2,1)} %copy-done.9) | copy-start | bytes 884740
  30.2 26.4 %collective-permute-start.5 = (bf16[192,1152]{1,0:T(8,128)(2,1)S(1)}, bf16[192,1152]{1,0:T(8,128)(2,1)S(1)}, u32[]{:S(2)}, u32[]{:S(2)}) collective-permute-start(bf16[192,1152]{1,0:T(8,128)(2,1)S(1)} %fusion.1), channel_id=1, source_target_pairs={{0,8},{4,12},{8,0},{12,4},{16,24},{20,28},{24,16},{28,20},{32,40},... | collective-permute-start | bytes 1327112 | tf_op jit(solution)/shard_map/ppermute | solution.py:29
  45.5 20.3 %collective-permute-start.4 = (bf16[192,1152]{1,0:T(8,128)(2,1)S(1)}, bf16[192,1152]{1,0:T(8,128)(2,1)S(1)}, u32[]{:S(2)}, u32[]{:S(2)}) collective-permute-start(bf16[192,1152]{1,0:T(8,128)(2,1)S(1)} %copy-done.11), channel_id=1, source_target_pairs={{0,12},{4,0},{8,4},{12,8},{16,28},{20,16},{24,20},{28,24},{32,44},... | collective-permute-start | bytes 1327112 | tf_op jit(solution)/shard_map/ppermute | solution.py:29
  49.6 33.8 %copy-start.2 = (f32[192,1152]{1,0:T(8,128)S(1)}, f32[192,1152]{1,0:T(8,128)}, u32[]{:S(2)}) copy-start(f32[192,1152]{1,0:T(8,128)} %convolution_multiply_fusion.2) | copy-start | bytes 2654212
  49.6 24.1 %collective-permute-start.3 = (bf16[192,1152]{1,0:T(8,128)(2,1)S(1)}, bf16[192,1152]{1,0:T(8,128)(2,1)S(1)}, u32[]{:S(2)}, u32[]{:S(2)}) collective-permute-start(bf16[192,1152]{1,0:T(8,128)(2,1)S(1)} %fusion.26), channel_id=1, source_target_pairs={{0,2},{1,3},{2,0},{3,1},{4,6},{5,7},{6,4},{7,5},{8,10},{9,11},{10,... | collective-permute-start | bytes 1327112 | tf_op jit(solution)/shard_map/ppermute | solution.py:44
  66.0 17.4 %collective-permute-start.6 = (bf16[192,1152]{1,0:T(8,128)(2,1)S(1)}, bf16[192,1152]{1,0:T(8,128)(2,1)S(1)}, u32[]{:S(2)}, u32[]{:S(2)}) collective-permute-start(bf16[192,1152]{1,0:T(8,128)(2,1)S(1)} %fusion.25), channel_id=1, source_target_pairs={{24,8},{25,9},{26,10},{27,11},{28,12},{29,13},{30,14},{31,15},{40,... | collective-permute-start | bytes 1327112 | tf_op jit(solution)/shard_map/ppermute | solution.py:39

commit v3 on v1

--- a/solution.py
+++ b/solution.py
@@ -24,13 +24,20 @@
     return lax.ppermute(block, AXES, route(distance))
 
 
-def returned(block, distance):
-    return lax.ppermute(block, AXES, [(j, i) for i, j in route(distance)])
+def back(distance):
+    return [(j, i) for i, j in route(distance)]
 
 
-def swapped(block, bit):
-    n = lax.axis_size("grp")
-    return lax.ppermute(block, "grp", [(i, i ^ bit) for i in range(n)])
+def across(bit):
+    count = lax.axis_size("blk") * lax.axis_size("grp")
+    return [(i, i ^ bit) for i in range(count)]
+
+
+def moved(even, odd, even_pairs, odd_pairs):
+    pairs = [p for p in even_pairs if p[0] % 2 == 0]
+    pairs += [p for p in odd_pairs if p[0] % 2 == 1]
+    payload = jnp.where(lax.axis_index("grp") % 2 == 0, even, odd)
+    return lax.ppermute(payload, AXES, pairs)
 
 
 def on_device(photo, caption, matching_column, scale_exponent, score_intercept):
@@ -71,8 +78,6 @@
     w0 = weight(caption, own_target)
     going, w0 = lax.optimization_barrier((caption, w0))
     text2 = sent(going, 2)
-    text_grad = text_term(w0)
-    text1, text_grad = lax.optimization_barrier((text1, text_grad))
     w1 = weight(text1, F32(-1.0))
     term1 = text_term(w1).astype(BF)
     early = jnp.dot(w0, caption, preferred_element_type=F32) + jnp.dot(
@@ -88,17 +93,24 @@
 
     give = image_part(slice(0, 2 * width)).astype(BF)
     give, w2, term1 = lax.optimization_barrier((give, w2, term1))
-    got = swapped(give, 1)
-    back1 = returned(term1, 1)
+    got = lax.ppermute(give, AXES, across(1))
     keep = image_part(slice(2 * width, 4 * width))
     far = (keep[:width] + got[:width].astype(F32)).astype(BF)
     near = keep[width:] + got[width:].astype(F32)
-    other = swapped(far, 2)
-    back2 = returned(text_term(w2).astype(BF), 2)
+    far, w2, term1 = lax.optimization_barrier((far, w2, term1))
+    first = moved(far, term1, across(2), back(1))
+    term2 = text_term(w2).astype(BF)
+    second = moved(term1, term2, back(1), back(2))
+    third = moved(term2, far, back(2), across(2))
+    w0, term2 = lax.optimization_barrier((w0, term2))
+    text_grad = text_term(w0)
 
+    even = place % 2 == 0
+    other = jnp.where(even, first, third)
+    back1 = jnp.where(even, second, first)
+    back2 = jnp.where(even, third, second)
+    image_grad = near + other.astype(F32)
     text_grad = text_grad + back1.astype(F32) + back2.astype(F32)
-    text_grad, other = lax.optimization_barrier((text_grad, other))
-    image_grad = near + other.astype(F32)
     return image_grad, text_grad
 
 

time: 88.7 us -> 87.4 us (0.985)
  the two profiles are of different devices: /device:TPU:1 before, /device:TPU:253 now
where the time goes in v3:
time: 87.4 us; the launch traced here: 86.9 us
  waiting for transfers between devices  41.4 us (47%)
  starting transfers between devices  25.6 us (29%)
  matrix products  11.2 us (13%)
  other arithmetic  3.41 us (4%)
  local copies, waits for them, and re-layouts  2.96 us (3%)
  between operations  2.3 us (3%)
    ppermute x3, waiting for transfers between devices, moved(): return lax.ppermute(payload, AXES, pairs)  34.8 us
    ppermute x3, starting transfers between devices, moved(): return lax.ppermute(payload, AXES, pairs)  14.9 us
    ppermute x2, starting transfers between devices, sent(): return lax.ppermute(block, AXES, route(distance))  7.48 us
    ppermute x2, waiting for transfers between devices, sent(): return lax.ppermute(block, AXES, route(distance))  5.98 us
    dot_general x3, matrix products, text_term(): lax.dot_general(w, photo, (((0,), (0,)), ((), ())), preferred_element_typ...  3.41 us
    ppermute x1, starting transfers between devices, on_device(): got = lax.ppermute(give, AXES, across(1))  3.24 us
    dot_general x2, matrix products, image_part(): jnp.dot(w2[rows], text2, preferred_element_type=F32)  3.08 us
    dynamic_slice x2, local copies, waits for them, and re-layouts, ordered(): lax.dynamic_slice_in_dim(rows, (place ^ bits) * width, width, 0)  2.45 us
  transfers between devices with their start and end apart: 6, of which 5 were waited for; matrix products, arithmetic and copies ran while one was open for 13% of the time, Pallas kernels for 0%

profile of v3, /device:TPU:253, one launch (start us, length us, event | category | flops | bytes accessed | tf_op | source)
XLA Modules:
  0.0 86.9 jit_solution(10022901127974507713)
XLA Ops:
  0.6 2.8 %collective-permute-start.1 = (bf16[192,1152]{1,0:T(8,128)(2,1)}, bf16[192,1152]{1,0:T(8,128)(2,1)S(1)}, u32[]{:S(2)}, u32[]{:S(2)}) collective-permute-start(bf16[192,1152]{1,0:T(8,128)(2,1)} %param.6), channel_id=1, source_target_pairs={{0,4},{1,5},{2,6},{3,7},{4,8},{5,9},{6,10},{7,11},{8,12},{9,13},{1... | collective-permute-start | bytes 1327112 | tf_op jit(solution)/shard_map/ppermute | solution.py:24
  4.8 0.8 constant_dynamic-slice_fusion.7
  5.7 1.6 %constant_dynamic-slice_fusion.3 = (bf16[192,1152]{1,0:T(8,128)(2,1)S(1)}, bf16[192,1152]{1,0:T(8,128)(2,1)S(1)}, bf16[192,1152]{1,0:T(8,128)(2,1)S(1)}, bf16[192,1152]{1,0:T(8,128)(2,1)S(1)}) fusion(bf16[768,1152]{1,0:T(8,128)(2,1)} %param.5, s32[]{:T(128)S(6)} %select_n.61, s32[]{:T(128)S(6)} %select_n.62, s32[]{:T(128)S(6)} %select_n.64, s32[]{:T(128)S(6)} %select_n.63), kind=kLoop, calls=%fused_computation.48 | loop fusion | bytes 3538960 | tf_op jit(solution)/shard_map/dynamic_slice | solution.py:53
  7.4 0.8 fusion.21
  8.2 4.7 %collective-permute-start = (bf16[192,1152]{1,0:T(8,128)(2,1)S(1)}, bf16[192,1152]{1,0:T(8,128)(2,1)S(1)}, u32[]{:S(2)}, u32[]{:S(2)}) collective-permute-start(bf16[192,1152]{1,0:T(8,128)(2,1)S(1)} %copy-done.1), channel_id=1, source_target_pairs={{0,8},{1,9},{2,10},{3,11},{4,12},{5,13},{6,14},{7,15},{8,16},{9,17... | collective-permute-start | bytes 1327112 | tf_op jit(solution)/shard_map/ppermute | solution.py:24
  12.9 0.7 fusion.32
  13.8 0.7 fusion.20
  14.5 1.3 %fusion = bf16[192,1152]{1,0:T(8,128)(2,1)} fusion(bf16[768,192]{0,1:T(8,128)(2,1)S(1)} %fusion.20, f32[]{:T(128)} %bitcast, bf16[192,1152]{1,0:T(8,128)(2,1)S(1)} %get-tuple-element.28, bf16[192,1152]{1,0:T(8,128)(2,1)S(1)} %get-tuple-element.29, bf16[192,1152]{1,0:T(8,128)(2,1)S(1)} %get-tuple-element.27, bf16[192,1152]{1,0:T(8,128)(2,1)S(1)} %get-tuple-element.26), kind=kOutput, calls=%fused_computation.4 | convolution fusion | flops 347258880 | bytes 2506756 | tf_op jit(solution)/shard_map/dot_general | solution.py:74
  15.9 1.7 %convolution_add_fusion = f32[768,1152]{1,0:T(8,128)S(1)} fusion(f32[768,1152]{1,0:T(8,128)S(1)} %fusion.32, bf16[768,192]{0,1:T(8,128)(2,1)S(1)} %fusion.20, bf16[192,1152]{1,0:T(8,128)(2,1)} %copy-done.11), kind=kOutput, calls=%fused_computation | convolution fusion | flops 340623360 | bytes 7815168 | tf_op jit(solution)/shard_map/dot_general | solution.py:83
  17.6 5.8 %collective-permute-done = bf16[192,1152]{1,0:T(8,128)(2,1)S(1)} collective-permute-done((bf16[192,1152]{1,0:T(8,128)(2,1)S(1)}, bf16[192,1152]{1,0:T(8,128)(2,1)S(1)}, u32[]{:S(2)}, u32[]{:S(2)}) %collective-permute-start) | collective-permute-done | bytes 442400 | tf_op jit(solution)/shard_map/ppermute | solution.py:24
  23.5 0.7 fusion.19
  24.3 1.4 %multiply_convert_fusion = bf16[384,1152]{1,0:T(8,128)(2,1)} fusion(f32[768,1152]{1,0:T(8,128)S(1)} %convolution_add_fusion, f32[]{:T(128)} %bitcast, bf16[192,1152]{1,0:T(8,128)(2,1)S(1)} %collective-permute-done, bf16[768,192]{0,1:T(8,128)(2,1)S(1)} %fusion.19), kind=kOutput, calls=%fused_computation.8 | convolution fusion | flops 171196416 | bytes 3244036 | tf_op jit(solution)/shard_map/dot_general | solution.py:91
  25.6 3.2 %collective-permute-start.2 = (bf16[384,1152]{1,0:T(8,128)(2,1)}, bf16[384,1152]{1,0:T(8,128)(2,1)}, u32[]{:S(2)}, u32[]{:S(2)}) collective-permute-start(bf16[384,1152]{1,0:T(8,128)(2,1)} %multiply_convert_fusion), channel_id=1, source_target_pairs={{0,1},{1,0},{2,3},{3,2},{4,5},{5,4},{6,7},{7,6},{8,9},{9,8},{10,11... | collective-permute-start | bytes 2654216 | tf_op jit(solution)/shard_map/ppermute | solution.py:96
  28.9 1.7 %add_multiply_fusion = f32[384,1152]{1,0:T(8,128)S(1)} fusion(f32[768,1152]{1,0:T(8,128)S(1)} %convolution_add_fusion, f32[]{:T(128)} %bitcast, bf16[192,1152]{1,0:T(8,128)(2,1)} %copy-done, bf16[768,192]{0,1:T(8,128)(2,1)} %copy-done.14), kind=kOutput, calls=%fused_computation.7 | convolution fusion | flops 170754048 | bytes 4129280 | tf_op jit(solution)/shard_map/dot_general | solution.py:91
  30.6 0.6 collective-permute-done.2
  31.3 1.1 %fusion.22 = bf16[192,1152]{1,0:T(8,128)(2,1)S(1)} fusion(f32[384,1152]{1,0:T(8,128)S(1)} %add_multiply_fusion, bf16[384,1152]{1,0:T(8,128)(2,1)} %collective-permute-done.2), kind=kLoop, calls=%fused_computation.33 | loop fusion | flops 663552 | bytes 1769472 | tf_op jit(solution)/shard_map/convert_element_type | solution.py:98
  32.4 0.6 fusion.1
  33.6 7.4 %collective-permute-start.4 = (bf16[192,1152]{1,0:T(8,128)(2,1)S(1)}, bf16[192,1152]{1,0:T(8,128)(2,1)S(1)}, u32[]{:S(2)}, u32[]{:S(2)}) collective-permute-start(bf16[192,1152]{1,0:T(8,128)(2,1)S(1)} %get-tuple-element.31), channel_id=1, source_target_pairs={{8,0},{10,2},{12,4},{14,6},{16,8},{18,10},{20,12},{22,14},{24,16},... | collective-permute-start | bytes 1327112 | tf_op jit(solution)/shard_map/ppermute | solution.py:40
  40.9 1.9 %collective-permute-start.3 = (bf16[192,1152]{1,0:T(8,128)(2,1)S(1)}, bf16[192,1152]{1,0:T(8,128)(2,1)S(1)}, u32[]{:S(2)}, u32[]{:S(2)}) collective-permute-start(bf16[192,1152]{1,0:T(8,128)(2,1)S(1)} %get-tuple-element.32), channel_id=1, source_target_pairs={{0,2},{2,0},{4,6},{6,4},{8,10},{10,8},{12,14},{14,12},{16,18},{18,... | collective-permute-start | bytes 1327112 | tf_op jit(solution)/shard_map/ppermute | solution.py:40
  42.9 5.6 %collective-permute-start.5 = (bf16[192,1152]{1,0:T(8,128)(2,1)S(1)}, bf16[192,1152]{1,0:T(8,128)(2,1)S(1)}, u32[]{:S(2)}, u32[]{:S(2)}) collective-permute-start(bf16[192,1152]{1,0:T(8,128)(2,1)S(1)} %get-tuple-element.30), channel_id=1, source_target_pairs={{4,0},{6,2},{8,4},{10,6},{12,8},{14,10},{16,12},{18,14},{20,16},{2... | collective-permute-start | bytes 1327112 | tf_op jit(solution)/shard_map/ppermute | solution.py:40
  48.5 12.0 %collective-permute-done.4 = bf16[192,1152]{1,0:T(8,128)(2,1)S(1)} collective-permute-done((bf16[192,1152]{1,0:T(8,128)(2,1)S(1)}, bf16[192,1152]{1,0:T(8,128)(2,1)S(1)}, u32[]{:S(2)}, u32[]{:S(2)}) %collective-permute-start.4) | collective-permute-done | bytes 442400 | tf_op jit(solution)/shard_map/ppermute | solution.py:40
  60.5 2.1 %fusion.23 = f32[192,1152]{1,0:T(8,128)} fusion(f32[384,1152]{1,0:T(8,128)S(1)} %add_multiply_fusion, bf16[384,1152]{1,0:T(8,128)(2,1)} %collective-permute-done.2, bf16[192,1152]{1,0:T(8,128)(2,1)S(1)} %collective-permute-done.3, bf16[192,1152]{1,0:T(8,128)(2,1)S(1)} %collective-permute-done.4, pred[]{:T(512)S(6)} %eq.27), kind=kLoop, calls=%fused_computation.35 | loop fusion | flops 1105920 | bytes 3096577 | tf_op jit(solution)/shard_map/add | solution.py:112
  62.6 22.8 %collective-permute-done.5 = bf16[192,1152]{1,0:T(8,128)(2,1)S(1)} collective-permute-done((bf16[192,1152]{1,0:T(8,128)(2,1)S(1)}, bf16[192,1152]{1,0:T(8,128)(2,1)S(1)}, u32[]{:S(2)}, u32[]{:S(2)}) %collective-permute-start.5) | collective-permute-done | bytes 442400 | tf_op jit(solution)/shard_map/ppermute | solution.py:40
  85.4 1.5 %convert_add_fusion = f32[192,1152]{1,0:T(8,128)} fusion(bf16[192,1152]{1,0:T(8,128)(2,1)S(1)} %collective-permute-done.4, bf16[192,1152]{1,0:T(8,128)(2,1)S(1)} %collective-permute-done.5, bf16[192,1152]{1,0:T(8,128)(2,1)S(1)} %collective-permute-done.3, bf16[768,192]{0,1:T(8,128)(2,1)S(1)} %copy-done.13, f32[]{:T(128)} %bitcast, pred[]{:T(512)S(6)} %eq.27, ...), kind=kOutput, calls=%fused_computation.36 | convolution fusion | flops 348364800 | bytes 4276229 | tf_op jit(solution)/shard_map/dot_general | solution.py:74
  (37 shorter events, 0.9 us)
Async XLA Ops:
  0.6 13.1 %collective-permute-start.1 = (bf16[192,1152]{1,0:T(8,128)(2,1)}, bf16[192,1152]{1,0:T(8,128)(2,1)S(1)}, u32[]{:S(2)}, u32[]{:S(2)}) collective-permute-start(bf16[192,1152]{1,0:T(8,128)(2,1)} %param.6), channel_id=1, source_target_pairs={{0,4},{1,5},{2,6},{3,7},{4,8},{5,9},{6,10},{7,11},{8,12},{9,13},{1... | collective-permute-start | bytes 1327112 | tf_op jit(solution)/shard_map/ppermute | solution.py:24
  5.7 1.7 %copy-start.1 = (bf16[192,1152]{1,0:T(8,128)(2,1)S(1)}, bf16[192,1152]{1,0:T(8,128)(2,1)}, u32[]{:S(2)}) copy-start(bf16[192,1152]{1,0:T(8,128)(2,1)} %param.6) | copy-start | bytes 1327108
  7.3 16.2 %copy-start.2 = (bf16[192,1152]{1,0:T(8,128)(2,1)}, bf16[192,1152]{1,0:T(8,128)(2,1)S(1)}, u32[]{:S(2)}) copy-start(bf16[192,1152]{1,0:T(8,128)(2,1)S(1)} %get-tuple-element.26) | copy-start | bytes 1327108
  7.3 16.2 %copy-start.4 = (bf16[192,1152]{1,0:T(8,128)(2,1)}, bf16[192,1152]{1,0:T(8,128)(2,1)S(1)}, u32[]{:S(2)}) copy-start(bf16[192,1152]{1,0:T(8,128)(2,1)S(1)} %get-tuple-element.27) | copy-start | bytes 1327108
  7.3 16.1 %copy-start.6 = (bf16[192,1152]{1,0:T(8,128)(2,1)}, bf16[192,1152]{1,0:T(8,128)(2,1)S(1)}, u32[]{:S(2)}) copy-start(bf16[192,1152]{1,0:T(8,128)(2,1)S(1)} %get-tuple-element.28) | copy-start | bytes 1327108
  7.3 16.1 %copy-start.8 = (bf16[192,1152]{1,0:T(8,128)(2,1)}, bf16[192,1152]{1,0:T(8,128)(2,1)S(1)}, u32[]{:S(2)}) copy-start(bf16[192,1152]{1,0:T(8,128)(2,1)S(1)} %get-tuple-element.29) | copy-start | bytes 1327108
  8.2 5.4 %copy-start.12 = (bf16[768,192]{0,1:T(8,128)(2,1)}, bf16[768,192]{0,1:T(8,128)(2,1)S(1)}, u32[]{:S(2)}) copy-start(bf16[768,192]{0,1:T(8,128)(2,1)S(1)} %fusion.21) | copy-start | bytes 884740
  8.2 15.2 %collective-permute-start = (bf16[192,1152]{1,0:T(8,128)(2,1)S(1)}, bf16[192,1152]{1,0:T(8,128)(2,1)S(1)}, u32[]{:S(2)}, u32[]{:S(2)}) collective-permute-start(bf16[192,1152]{1,0:T(8,128)(2,1)S(1)} %copy-done.1), channel_id=1, source_target_pairs={{0,8},{1,9},{2,10},{3,11},{4,12},{5,13},{6,14},{7,15},{8,16},{9,17... | collective-permute-start | bytes 1327112 | tf_op jit(solution)/shard_map/ppermute | solution.py:24
  13.8 0.8 copy-start.11
  23.5 0.8 copy-start
  24.2 1.4 %copy-start.14 = (bf16[768,192]{0,1:T(8,128)(2,1)}, bf16[768,192]{0,1:T(8,128)(2,1)S(1)}, u32[]{:S(2)}) copy-start(bf16[768,192]{0,1:T(8,128)(2,1)S(1)} %fusion.19) | copy-start | bytes 884740
  25.6 5.6 %collective-permute-start.2 = (bf16[384,1152]{1,0:T(8,128)(2,1)}, bf16[384,1152]{1,0:T(8,128)(2,1)}, u32[]{:S(2)}, u32[]{:S(2)}) collective-permute-start(bf16[384,1152]{1,0:T(8,128)(2,1)} %multiply_convert_fusion), channel_id=1, source_target_pairs={{0,1},{1,0},{2,3},{3,2},{4,5},{5,4},{6,7},{7,6},{8,9},{9,8},{10,11... | collective-permute-start | bytes 2654216 | tf_op jit(solution)/shard_map/ppermute | solution.py:96
  28.9 3.5 %copy-start.3 = (bf16[192,1152]{1,0:T(8,128)(2,1)S(1)}, bf16[192,1152]{1,0:T(8,128)(2,1)}, u32[]{:S(2)}) copy-start(bf16[192,1152]{1,0:T(8,128)(2,1)} %copy-done.2) | copy-start | bytes 1327108
  28.9 3.5 %copy-start.5 = (bf16[192,1152]{1,0:T(8,128)(2,1)S(1)}, bf16[192,1152]{1,0:T(8,128)(2,1)}, u32[]{:S(2)}) copy-start(bf16[192,1152]{1,0:T(8,128)(2,1)} %copy-done.4) | copy-start | bytes 1327108
  28.9 3.5 %copy-start.7 = (bf16[192,1152]{1,0:T(8,128)(2,1)S(1)}, bf16[192,1152]{1,0:T(8,128)(2,1)}, u32[]{:S(2)}) copy-start(bf16[192,1152]{1,0:T(8,128)(2,1)} %copy-done.6) | copy-start | bytes 1327108
  28.9 3.5 %copy-start.9 = (bf16[192,1152]{1,0:T(8,128)(2,1)S(1)}, bf16[192,1152]{1,0:T(8,128)(2,1)}, u32[]{:S(2)}) copy-start(bf16[192,1152]{1,0:T(8,128)(2,1)} %copy-done.8) | copy-start | bytes 1327108
  28.9 3.5 %copy-start.15 = (bf16[768,192]{0,1:T(8,128)(2,1)S(1)}, bf16[768,192]{0,1:T(8,128)(2,1)}, u32[]{:S(2)}) copy-start(bf16[768,192]{0,1:T(8,128)(2,1)} %copy-done.14) | copy-start | bytes 884740
  32.4 1.0 %copy-start.10 = (bf16[192,1152]{1,0:T(8,128)(2,1)S(1)}, bf16[192,1152]{1,0:T(8,128)(2,1)}, u32[]{:S(2)}) copy-start(bf16[192,1152]{1,0:T(8,128)(2,1)} %fusion) | copy-start | bytes 1327108
  33.6 51.8 %copy-start.13 = (bf16[768,192]{0,1:T(8,128)(2,1)S(1)}, bf16[768,192]{0,1:T(8,128)(2,1)}, u32[]{:S(2)}) copy-start(bf16[768,192]{0,1:T(8,128)(2,1)} %copy-done.12) | copy-start | bytes 884740
  33.6 26.9 %collective-permute-start.4 = (bf16[192,1152]{1,0:T(8,128)(2,1)S(1)}, bf16[192,1152]{1,0:T(8,128)(2,1)S(1)}, u32[]{:S(2)}, u32[]{:S(2)}) collective-permute-start(bf16[192,1152]{1,0:T(8,128)(2,1)S(1)} %get-tuple-element.31), channel_id=1, source_target_pairs={{8,0},{10,2},{12,4},{14,6},{16,8},{18,10},{20,12},{22,14},{24,16},... | collective-permute-start | bytes 1327112 | tf_op jit(solution)/shard_map/ppermute | solution.py:40
  40.9 19.5 %collective-permute-start.3 = (bf16[192,1152]{1,0:T(8,128)(2,1)S(1)}, bf16[192,1152]{1,0:T(8,128)(2,1)S(1)}, u32[]{:S(2)}, u32[]{:S(2)}) collective-permute-start(bf16[192,1152]{1,0:T(8,128)(2,1)S(1)} %get-tuple-element.32), channel_id=1, source_target_pairs={{0,2},{2,0},{4,6},{6,4},{8,10},{10,8},{12,14},{14,12},{16,18},{18,... | collective-permute-start | bytes 1327112 | tf_op jit(solution)/shard_map/ppermute | solution.py:40
  42.9 42.5 %collective-permute-start.5 = (bf16[192,1152]{1,0:T(8,128)(2,1)S(1)}, bf16[192,1152]{1,0:T(8,128)(2,1)S(1)}, u32[]{:S(2)}, u32[]{:S(2)}) collective-permute-start(bf16[192,1152]{1,0:T(8,128)(2,1)S(1)} %get-tuple-element.30), channel_id=1, source_target_pairs={{4,0},{6,2},{8,4},{10,6},{12,8},{14,10},{16,12},{18,14},{20,16},{2... | collective-permute-start | bytes 1327112 | tf_op jit(solution)/shard_map/ppermute | solution.py:40

commit v4 on v2

--- a/solution.py
+++ b/solution.py
@@ -82,10 +82,9 @@
     w0 = weight(caption, own_target)
     going, w0 = lax.optimization_barrier((caption, w0))
     text2 = sent(going, 2)
-    text_grad = text_term(w0)
-    text1, text_grad = lax.optimization_barrier((text1, text_grad))
     w1 = weight(text1, F32(-1.0))
     term1 = text_term(w1).astype(BF)
+    back1 = turned(term1, 1)
     early = jnp.dot(w0, caption, preferred_element_type=F32) + jnp.dot(
         w1, text1, preferred_element_type=F32
     )
@@ -98,13 +97,15 @@
         )
 
     give = image_part(slice(0, 2 * width)).astype(BF)
-    give, w2, term1 = lax.optimization_barrier((give, w2, term1))
+    give, w2, back1 = lax.optimization_barrier((give, w2, back1))
     got = swapped(give, 1)
-    back1 = turned(term1, 1)
     keep = image_part(slice(2 * width, 4 * width))
     far = (keep[:width] + got[:width].astype(F32)).astype(BF)
     near = keep[width:] + got[width:].astype(F32)
-    back2 = turned(text_term(w2).astype(BF), 2)
+    term2 = text_term(w2).astype(BF)
+    back2 = turned(term2, 2)
+    w0, term2 = lax.optimization_barrier((w0, term2))
+    text_grad = text_term(w0)
     other = swapped(far, 2)
     x = lax.axis_index("blk") % X
     back1, back2 = back1.astype(F32), back2.astype(F32)

time: 85 us -> 84.2 us (level)
  the two profiles are of different devices: /device:TPU:6 before, /device:TPU:254 now
where the time goes in v4:
time: 84.2 us; the launch traced here: 83.7 us
  waiting for transfers between devices  46.9 us (56%)
  starting transfers between devices  23.3 us (28%)
  matrix products  6.35 us (8%)
  other arithmetic  2.55 us (3%)
  local copies, waits for them, and re-layouts  2.46 us (3%)
  between operations  2.17 us (3%)
    ppermute x2, waiting for transfers between devices, turned(): lax.ppermute(block, 'blk', [(b, b // X * X + (b - distance) % X) for b in...  15 us
    ppermute x2, waiting for transfers between devices, swapped(): return lax.ppermute(block, 'grp', [(i, i ^ bit) for i in range(n)])  12 us
    ppermute x1, waiting for transfers between devices, handed_down(): return lax.ppermute(block, AXES, [(j, i) for i, j in crossing])  10.8 us
    ppermute x2, waiting for transfers between devices, sent(): return lax.ppermute(block, AXES, route(distance))  9.08 us
    ppermute x2, starting transfers between devices, sent(): return lax.ppermute(block, AXES, route(distance))  8.94 us
    ppermute x2, starting transfers between devices, swapped(): return lax.ppermute(block, 'grp', [(i, i ^ bit) for i in range(n)])  7.29 us
    ppermute x2, starting transfers between devices, turned(): lax.ppermute(block, 'blk', [(b, b // X * X + (b - distance) % X) for b in...  3.84 us
    ppermute x1, starting transfers between devices, handed_down(): return lax.ppermute(block, AXES, [(j, i) for i, j in crossing])  3.24 us
  transfers between devices with their start and end apart: 7, of which 5 were waited for; matrix products, arithmetic and copies ran while one was open for 12% of the time, Pallas kernels for 0%

profile of v4, /device:TPU:254, one launch (start us, length us, event | category | flops | bytes accessed | tf_op | source)
XLA Modules:
  0.0 83.7 jit_solution(16360648671816130443)
XLA Ops:
  0.6 4.6 %collective-permute-start.1 = (bf16[192,1152]{1,0:T(8,128)(2,1)}, bf16[192,1152]{1,0:T(8,128)(2,1)S(1)}, u32[]{:S(2)}, u32[]{:S(2)}) collective-permute-start(bf16[192,1152]{1,0:T(8,128)(2,1)} %param.6), channel_id=1, source_target_pairs={{0,4},{1,5},{2,6},{3,7},{4,8},{5,9},{6,10},{7,11},{8,12},{9,13},{1... | collective-permute-start | bytes 1327112 | tf_op jit(solution)/shard_map/ppermute | solution.py:24
  5.3 0.8 %constant_dynamic-slice_fusion.7 = (s32[1,192]{1,0:T(1,128)S(1)}, s32[1,192]{1,0:T(1,128)S(1)}, s32[1,192]{1,0:T(1,128)S(1)}, s32[1,192]{1,0:T(1,128)S(1)}) fusion(s32[1,768]{1,0:T(1,128)} %param.7, s32[]{:T(128)S(6)} %select_n.47, s32[]{:T(128)S(6)} %select_n.48, s32[]{:T(128)S(6)} %select_n.50, s32[]{:T(128)S(6)} %select_n.49), kind=kLoop, calls=%fused_computation.55 | loop fusion | bytes 6160 | tf_op jit(solution)/shard_map/dynamic_slice | solution.py:57
  6.2 1.6 %constant_dynamic-slice_fusion.3 = (bf16[192,1152]{1,0:T(8,128)(2,1)S(1)}, bf16[192,1152]{1,0:T(8,128)(2,1)S(1)}, bf16[192,1152]{1,0:T(8,128)(2,1)S(1)}, bf16[192,1152]{1,0:T(8,128)(2,1)S(1)}) fusion(bf16[768,1152]{1,0:T(8,128)(2,1)} %param.5, s32[]{:T(128)S(6)} %select_n.47, s32[]{:T(128)S(6)} %select_n.48, s32[]{:T(128)S(6)} %select_n.50, s32[]{:T(128)S(6)} %select_n.49), kind=kLoop, calls=%fused_computation.51 | loop fusion | bytes 3538960 | tf_op jit(solution)/shard_map/dynamic_slice | solution.py:57
  9.2 0.8 fusion.21
  10.0 4.3 %collective-permute-start = (bf16[192,1152]{1,0:T(8,128)(2,1)S(1)}, bf16[192,1152]{1,0:T(8,128)(2,1)S(1)}, u32[]{:S(2)}, u32[]{:S(2)}) collective-permute-start(bf16[192,1152]{1,0:T(8,128)(2,1)S(1)} %copy-done), channel_id=1, source_target_pairs={{0,8},{1,9},{2,10},{3,11},{4,12},{5,13},{6,14},{7,15},{8,16},{9,17... | collective-permute-start | bytes 1327112 | tf_op jit(solution)/shard_map/ppermute | solution.py:24
  14.3 0.7 fusion.36
  15.0 9.1 %collective-permute-done.1 = bf16[192,1152]{1,0:T(8,128)(2,1)S(1)} collective-permute-done((bf16[192,1152]{1,0:T(8,128)(2,1)}, bf16[192,1152]{1,0:T(8,128)(2,1)S(1)}, u32[]{:S(2)}, u32[]{:S(2)}) %collective-permute-start.1) | collective-permute-done | bytes 442400 | tf_op jit(solution)/shard_map/ppermute | solution.py:24
  24.1 0.7 fusion.20
  24.9 0.6 fusion
  25.4 1.9 %collective-permute-start.2 = (bf16[192,1152]{1,0:T(8,128)(2,1)S(1)}, bf16[192,1152]{1,0:T(8,128)(2,1)S(1)}, u32[]{:S(2)}, u32[]{:S(2)}) collective-permute-start(bf16[192,1152]{1,0:T(8,128)(2,1)S(1)} %fusion), channel_id=1, source_target_pairs={{0,12},{4,0},{8,4},{12,8},{16,28},{20,16},{24,20},{28,24},{32,44},... | collective-permute-start | bytes 1327112 | tf_op jit(solution)/shard_map/ppermute | solution.py:29
  27.4 0.7 convolution_add_fusion
  28.1 0.7 fusion.19
  29.3 7.5 %collective-permute-done.2 = bf16[192,1152]{1,0:T(8,128)(2,1)S(1)} collective-permute-done((bf16[192,1152]{1,0:T(8,128)(2,1)S(1)}, bf16[192,1152]{1,0:T(8,128)(2,1)S(1)}, u32[]{:S(2)}, u32[]{:S(2)}) %collective-permute-start.2) | collective-permute-done | bytes 442400 | tf_op jit(solution)/shard_map/ppermute | solution.py:29
  36.8 1.9 %collective-permute-start.3 = (bf16[384,1152]{1,0:T(8,128)(2,1)S(1)}, bf16[384,1152]{1,0:T(8,128)(2,1)S(1)}, u32[]{:S(2)}, u32[]{:S(2)}) collective-permute-start(bf16[384,1152]{1,0:T(8,128)(2,1)S(1)} %multiply_convert_fusion), channel_id=1, source_target_pairs={{0,1},{1,0},{2,3},{3,2},{4,5},{5,4},{6,7},{7,6},{8,9},{9,8},{10,11... | collective-permute-start | bytes 2654216 | tf_op jit(solution)/shard_map/ppermute | solution.py:44
  38.8 0.6 fusion.1
  39.3 1.9 %collective-permute-start.5 = (bf16[192,1152]{1,0:T(8,128)(2,1)S(1)}, bf16[192,1152]{1,0:T(8,128)(2,1)S(1)}, u32[]{:S(2)}, u32[]{:S(2)}) collective-permute-start(bf16[192,1152]{1,0:T(8,128)(2,1)S(1)} %fusion.1), channel_id=1, source_target_pairs={{0,8},{4,12},{8,0},{12,4},{16,24},{20,28},{24,16},{28,20},{32,40},... | collective-permute-start | bytes 1327112 | tf_op jit(solution)/shard_map/ppermute | solution.py:29
  41.3 0.6 convolution_multiply_fusion
  42.4 5.4 %collective-permute-start.4 = (bf16[192,1152]{1,0:T(8,128)(2,1)S(1)}, bf16[192,1152]{1,0:T(8,128)(2,1)S(1)}, u32[]{:S(2)}, u32[]{:S(2)}) collective-permute-start(bf16[192,1152]{1,0:T(8,128)(2,1)S(1)} %fusion.26), channel_id=1, source_target_pairs={{0,2},{1,3},{2,0},{3,1},{4,6},{5,7},{6,4},{7,5},{8,10},{9,11},{10,... | collective-permute-start | bytes 1327112 | tf_op jit(solution)/shard_map/ppermute | solution.py:44
  47.8 7.5 %collective-permute-done.5 = bf16[192,1152]{1,0:T(8,128)(2,1)S(1)} collective-permute-done((bf16[192,1152]{1,0:T(8,128)(2,1)S(1)}, bf16[192,1152]{1,0:T(8,128)(2,1)S(1)}, u32[]{:S(2)}, u32[]{:S(2)}) %collective-permute-start.5) | collective-permute-done | bytes 442400 | tf_op jit(solution)/shard_map/ppermute | solution.py:29
  55.5 3.2 %collective-permute-start.6 = (bf16[192,1152]{1,0:T(8,128)(2,1)S(1)}, bf16[192,1152]{1,0:T(8,128)(2,1)S(1)}, u32[]{:S(2)}, u32[]{:S(2)}) collective-permute-start(bf16[192,1152]{1,0:T(8,128)(2,1)S(1)} %fusion.25), channel_id=1, source_target_pairs={{24,8},{25,9},{26,10},{27,11},{28,12},{29,13},{30,14},{31,15},{40,... | collective-permute-start | bytes 1327112 | tf_op jit(solution)/shard_map/ppermute | solution.py:39
  58.7 12.0 %collective-permute-done.4 = bf16[192,1152]{1,0:T(8,128)(2,1)S(1)} collective-permute-done((bf16[192,1152]{1,0:T(8,128)(2,1)S(1)}, bf16[192,1152]{1,0:T(8,128)(2,1)S(1)}, u32[]{:S(2)}, u32[]{:S(2)}) %collective-permute-start.4) | collective-permute-done | bytes 442400 | tf_op jit(solution)/shard_map/ppermute | solution.py:44
  70.7 1.1 %fusion.27 = f32[192,1152]{1,0:T(8,128)} fusion(f32[384,1152]{1,0:T(8,128)S(1)} %add_multiply_fusion, bf16[192,1152]{1,0:T(8,128)(2,1)S(1)} %collective-permute-done.4, bf16[384,1152]{1,0:T(8,128)(2,1)S(1)} %collective-permute-done.3), kind=kLoop, calls=%fused_computation.42 | loop fusion | flops 884736 | bytes 2654208 | tf_op jit(solution)/shard_map/add | solution.py:119
  71.7 10.8 %collective-permute-done.6 = bf16[192,1152]{1,0:T(8,128)(2,1)S(1)} collective-permute-done((bf16[192,1152]{1,0:T(8,128)(2,1)S(1)}, bf16[192,1152]{1,0:T(8,128)(2,1)S(1)}, u32[]{:S(2)}, u32[]{:S(2)}) %collective-permute-start.6) | collective-permute-done | bytes 442400 | tf_op jit(solution)/shard_map/ppermute | solution.py:39
  82.6 1.2 %fusion.24 = f32[192,1152]{1,0:T(8,128)} fusion(f32[192,1152]{1,0:T(8,128)S(1)} %convolution_multiply_fusion, bf16[192,1152]{1,0:T(8,128)(2,1)S(1)} %collective-permute-done.2, bf16[192,1152]{1,0:T(8,128)(2,1)S(1)} %collective-permute-done.5, bf16[192,1152]{1,0:T(8,128)(2,1)S(1)} %collective-permute-done.6, pred[]{:T(512)S(6)} %ge.3, pred[]{:T(512)S(6)} %eq.22), kind=kLoop, calls=%fused_computation.37 | loop fusion | flops 1769472 | bytes 3096578 | tf_op jit(solution)/shard_map/add | solution.py:121
  (10 shorter events, 1.3 us)
Async XLA Ops:
  0.6 23.5 %collective-permute-start.1 = (bf16[192,1152]{1,0:T(8,128)(2,1)}, bf16[192,1152]{1,0:T(8,128)(2,1)S(1)}, u32[]{:S(2)}, u32[]{:S(2)}) collective-permute-start(bf16[192,1152]{1,0:T(8,128)(2,1)} %param.6), channel_id=1, source_target_pairs={{0,4},{1,5},{2,6},{3,7},{4,8},{5,9},{6,10},{7,11},{8,12},{9,13},{1... | collective-permute-start | bytes 1327112 | tf_op jit(solution)/shard_map/ppermute | solution.py:24
  6.1 3.0 %copy-start = (bf16[192,1152]{1,0:T(8,128)(2,1)S(1)}, bf16[192,1152]{1,0:T(8,128)(2,1)}, u32[]{:S(2)}) copy-start(bf16[192,1152]{1,0:T(8,128)(2,1)} %param.6) | copy-start | bytes 1327108
  10.0 18.1 %collective-permute-start = (bf16[192,1152]{1,0:T(8,128)(2,1)S(1)}, bf16[192,1152]{1,0:T(8,128)(2,1)S(1)}, u32[]{:S(2)}, u32[]{:S(2)}) collective-permute-start(bf16[192,1152]{1,0:T(8,128)(2,1)S(1)} %copy-done), channel_id=1, source_target_pairs={{0,8},{1,9},{2,10},{3,11},{4,12},{5,13},{6,14},{7,15},{8,16},{9,17... | collective-permute-start | bytes 1327112 | tf_op jit(solution)/shard_map/ppermute | solution.py:24
  25.4 11.4 %collective-permute-start.2 = (bf16[192,1152]{1,0:T(8,128)(2,1)S(1)}, bf16[192,1152]{1,0:T(8,128)(2,1)S(1)}, u32[]{:S(2)}, u32[]{:S(2)}) collective-permute-start(bf16[192,1152]{1,0:T(8,128)(2,1)S(1)} %fusion), channel_id=1, source_target_pairs={{0,12},{4,0},{8,4},{12,8},{16,28},{20,16},{24,20},{28,24},{32,44},... | collective-permute-start | bytes 1327112 | tf_op jit(solution)/shard_map/ppermute | solution.py:29
  36.8 5.5 %collective-permute-start.3 = (bf16[384,1152]{1,0:T(8,128)(2,1)S(1)}, bf16[384,1152]{1,0:T(8,128)(2,1)S(1)}, u32[]{:S(2)}, u32[]{:S(2)}) collective-permute-start(bf16[384,1152]{1,0:T(8,128)(2,1)S(1)} %multiply_convert_fusion), channel_id=1, source_target_pairs={{0,1},{1,0},{2,3},{3,2},{4,5},{5,4},{6,7},{7,6},{8,9},{9,8},{10,11... | collective-permute-start | bytes 2654216 | tf_op jit(solution)/shard_map/ppermute | solution.py:44
  39.3 16.0 %collective-permute-start.5 = (bf16[192,1152]{1,0:T(8,128)(2,1)S(1)}, bf16[192,1152]{1,0:T(8,128)(2,1)S(1)}, u32[]{:S(2)}, u32[]{:S(2)}) collective-permute-start(bf16[192,1152]{1,0:T(8,128)(2,1)S(1)} %fusion.1), channel_id=1, source_target_pairs={{0,8},{4,12},{8,0},{12,4},{16,24},{20,28},{24,16},{28,20},{32,40},... | collective-permute-start | bytes 1327112 | tf_op jit(solution)/shard_map/ppermute | solution.py:29
  42.4 28.2 %collective-permute-start.4 = (bf16[192,1152]{1,0:T(8,128)(2,1)S(1)}, bf16[192,1152]{1,0:T(8,128)(2,1)S(1)}, u32[]{:S(2)}, u32[]{:S(2)}) collective-permute-start(bf16[192,1152]{1,0:T(8,128)(2,1)S(1)} %fusion.26), channel_id=1, source_target_pairs={{0,2},{1,3},{2,0},{3,1},{4,6},{5,7},{6,4},{7,5},{8,10},{9,11},{10,... | collective-permute-start | bytes 1327112 | tf_op jit(solution)/shard_map/ppermute | solution.py:44
  55.5 27.1 %collective-permute-start.6 = (bf16[192,1152]{1,0:T(8,128)(2,1)S(1)}, bf16[192,1152]{1,0:T(8,128)(2,1)S(1)}, u32[]{:S(2)}, u32[]{:S(2)}) collective-permute-start(bf16[192,1152]{1,0:T(8,128)(2,1)S(1)} %fusion.25), channel_id=1, source_target_pairs={{24,8},{25,9},{26,10},{27,11},{28,12},{29,13},{30,14},{31,15},{40,... | collective-permute-start | bytes 1327112 | tf_op jit(solution)/shard_map/ppermute | solution.py:39

commit v5 on v4

--- a/solution.py
+++ b/solution.py
@@ -84,7 +84,6 @@
     text2 = sent(going, 2)
     w1 = weight(text1, F32(-1.0))
     term1 = text_term(w1).astype(BF)
-    back1 = turned(term1, 1)
     early = jnp.dot(w0, caption, preferred_element_type=F32) + jnp.dot(
         w1, text1, preferred_element_type=F32
     )
@@ -97,28 +96,24 @@
         )
 
     give = image_part(slice(0, 2 * width)).astype(BF)
-    give, w2, back1 = lax.optimization_barrier((give, w2, back1))
+    give, w2, term1 = lax.optimization_barrier((give, w2, term1))
     got = swapped(give, 1)
     keep = image_part(slice(2 * width, 4 * width))
     far = (keep[:width] + got[:width].astype(F32)).astype(BF)
     near = keep[width:] + got[width:].astype(F32)
     term2 = text_term(w2).astype(BF)
     back2 = turned(term2, 2)
-    w0, term2 = lax.optimization_barrier((w0, term2))
+    w0, term1, term2 = lax.optimization_barrier((w0, term1, term2))
+    back1 = lax.ppermute(term1, AXES, [(j, i) for i, j in route(1)])
     text_grad = text_term(w0)
     other = swapped(far, 2)
     x = lax.axis_index("blk") % X
-    back1, back2 = back1.astype(F32), back2.astype(F32)
-    down = handed_down(jnp.where(x == X - 1, back1 + back2, back2).astype(BF))
-    text_grad = (
-        text_grad
-        + jnp.where(x == X - 1, F32(0.0), back1)
-        + jnp.where(x >= X - 2, F32(0.0), back2)
-    )
+    down = handed_down(back2)
+    own2 = jnp.where(x >= X - 2, F32(0.0), back2.astype(F32))
 
     image_grad = near + other.astype(F32)
     image_grad, down = lax.optimization_barrier((image_grad, down))
-    text_grad = text_grad + down.astype(F32)
+    text_grad = text_grad + back1.astype(F32) + own2 + down.astype(F32)
     return image_grad, text_grad
 
 

time: 84.2 us -> 76.9 us (0.913)
  waiting for transfers between devices: 46.9 us -> 34.1 us
  matrix products: 6.35 us -> 9.26 us
  other arithmetic: 2.55 us -> 4.35 us
    ppermute x2 -> x1, waiting for transfers between devices: 15 us -> 4.45 us  [turned(): lax.ppermute(block, 'blk', [(b, b // X * X + (b - distance) % X) for b in...]
    dot_general x3, matrix products: 1.7 us -> 4.61 us  [text_term(): lax.dot_general(w, photo, (((0,), (0,)), ((), ())), preferred_element_typ...]
    ppermute x0 -> x1, starting transfers between devices: none -> 1.92 us  [on_device(): back1 = lax.ppermute(term1, AXES, [(j, i) for i, j in route(1)])]
    ppermute x2 -> x1, starting transfers between devices: 3.84 us -> 1.95 us  [turned(): lax.ppermute(block, 'blk', [(b, b // X * X + (b - distance) % X) for b in...]
    ppermute x1, waiting for transfers between devices: 10.8 us -> 9.72 us  [handed_down(): return lax.ppermute(block, AXES, [(j, i) for i, j in crossing])]
    ppermute x2, waiting for transfers between devices: 12 us -> 10.9 us  [swapped(): return lax.ppermute(block, 'grp', [(i, i ^ bit) for i in range(n)])]
    add x1, other arithmetic: 1.16 us -> 2.15 us  [on_device(): text_grad = text_grad + back1.astype(F32) + own2 + down.astype(F32)]
    add x1, other arithmetic: 1.06 us -> 2.04 us  [on_device(): image_grad = near + other.astype(F32)]
  transfers between devices with their start and end apart: 7 -> 7, of which waited for: 5 -> 4; matrix products, arithmetic and copies ran while one was open for 12% -> 17% of each run, Pallas kernels for 0% -> 0%
where the time goes in v5:
time: 76.9 us; the launch traced here: 76.2 us
  waiting for transfers between devices  34.1 us (44%)
  starting transfers between devices  23.8 us (31%)
  matrix products  9.26 us (12%)
  other arithmetic  4.35 us (6%)
  local copies, waits for them, and re-layouts  2.48 us (3%)
  between operations  2.27 us (3%)
    ppermute x2, waiting for transfers between devices, swapped(): return lax.ppermute(block, 'grp', [(i, i ^ bit) for i in range(n)])  10.9 us
    ppermute x1, waiting for transfers between devices, handed_down(): return lax.ppermute(block, AXES, [(j, i) for i, j in crossing])  9.72 us
    ppermute x2, waiting for transfers between devices, sent(): return lax.ppermute(block, AXES, route(distance))  9.01 us
    ppermute x2, starting transfers between devices, sent(): return lax.ppermute(block, AXES, route(distance))  8.94 us
    ppermute x2, starting transfers between devices, swapped(): return lax.ppermute(block, 'grp', [(i, i ^ bit) for i in range(n)])  7.72 us
    dot_general x3, matrix products, text_term(): lax.dot_general(w, photo, (((0,), (0,)), ((), ())), preferred_element_typ...  4.61 us
    ppermute x1, waiting for transfers between devices, turned(): lax.ppermute(block, 'blk', [(b, b // X * X + (b - distance) % X) for b in...  4.45 us
    ppermute x1, starting transfers between devices, handed_down(): return lax.ppermute(block, AXES, [(j, i) for i, j in crossing])  3.25 us
  transfers between devices with their start and end apart: 7, of which 4 were waited for; matrix products, arithmetic and copies ran while one was open for 17% of the time, Pallas kernels for 0%

profile of v5, /device:TPU:254, one launch (start us, length us, event | category | flops | bytes accessed | tf_op | source)
XLA Modules:
  0.0 76.2 jit_solution(11804788951136428258)
XLA Ops:
  0.6 4.6 %collective-permute-start.1 = (bf16[192,1152]{1,0:T(8,128)(2,1)}, bf16[192,1152]{1,0:T(8,128)(2,1)S(1)}, u32[]{:S(2)}, u32[]{:S(2)}) collective-permute-start(bf16[192,1152]{1,0:T(8,128)(2,1)} %param.6), channel_id=1, source_target_pairs={{0,4},{1,5},{2,6},{3,7},{4,8},{5,9},{6,10},{7,11},{8,12},{9,13},{1... | collective-permute-start | bytes 1327112 | tf_op jit(solution)/shard_map/ppermute | solution.py:24
  5.3 0.8 %constant_dynamic-slice_fusion.7 = (s32[1,192]{1,0:T(1,128)S(1)}, s32[1,192]{1,0:T(1,128)S(1)}, s32[1,192]{1,0:T(1,128)S(1)}, s32[1,192]{1,0:T(1,128)S(1)}) fusion(s32[1,768]{1,0:T(1,128)} %param.7, s32[]{:T(128)S(6)} %select_n.35, s32[]{:T(128)S(6)} %select_n.36, s32[]{:T(128)S(6)} %select_n.38, s32[]{:T(128)S(6)} %select_n.37), kind=kLoop, calls=%fused_computation.49 | loop fusion | bytes 6160 | tf_op jit(solution)/shard_map/dynamic_slice | solution.py:57
  6.2 1.6 %constant_dynamic-slice_fusion.3 = (bf16[192,1152]{1,0:T(8,128)(2,1)S(1)}, bf16[192,1152]{1,0:T(8,128)(2,1)S(1)}, bf16[192,1152]{1,0:T(8,128)(2,1)S(1)}, bf16[192,1152]{1,0:T(8,128)(2,1)S(1)}) fusion(bf16[768,1152]{1,0:T(8,128)(2,1)} %param.5, s32[]{:T(128)S(6)} %select_n.35, s32[]{:T(128)S(6)} %select_n.36, s32[]{:T(128)S(6)} %select_n.38, s32[]{:T(128)S(6)} %select_n.37), kind=kLoop, calls=%fused_computation.45 | loop fusion | bytes 3538960 | tf_op jit(solution)/shard_map/dynamic_slice | solution.py:57
  9.2 0.8 %fusion.21 = bf16[768,192]{0,1:T(8,128)(2,1)S(1)} fusion(bf16[192,1152]{1,0:T(8,128)(2,1)S(1)} %copy-done, f32[]{:T(128)} %bitcast.18, f32[]{:T(128)} %bitcast, s32[768]{0:T(1024)S(1)} %pad_add_fusion, s32[192]{0:T(256)S(1)} %iota_add_fusion, bf16[192,1152]{1,0:T(8,128)(2,1)S(1)} %get-tuple-element.28, bf16[192,1152]{1,0:T(8,128)(2,1)S(1)} %get-tuple-element.29, ...), kind=kOutput, calls=%fused_computation.31 | convolution fusion | flops 348438528 | bytes 2510600 | tf_op jit(solution)/shard_map/dot_general | solution.py:70
  10.0 4.3 %collective-permute-start = (bf16[192,1152]{1,0:T(8,128)(2,1)S(1)}, bf16[192,1152]{1,0:T(8,128)(2,1)S(1)}, u32[]{:S(2)}, u32[]{:S(2)}) collective-permute-start(bf16[192,1152]{1,0:T(8,128)(2,1)S(1)} %copy-done), channel_id=1, source_target_pairs={{0,8},{1,9},{2,10},{3,11},{4,12},{5,13},{6,14},{7,15},{8,16},{9,17... | collective-permute-start | bytes 1327112 | tf_op jit(solution)/shard_map/ppermute | solution.py:24
  14.4 0.7 fusion.32
  15.1 9.0 %collective-permute-done.1 = bf16[192,1152]{1,0:T(8,128)(2,1)S(1)} collective-permute-done((bf16[192,1152]{1,0:T(8,128)(2,1)}, bf16[192,1152]{1,0:T(8,128)(2,1)S(1)}, u32[]{:S(2)}, u32[]{:S(2)}) %collective-permute-start.1) | collective-permute-done | bytes 442400 | tf_op jit(solution)/shard_map/ppermute | solution.py:24
  24.1 0.7 fusion.20
  24.9 1.3 %fusion = bf16[192,1152]{1,0:T(8,128)(2,1)} fusion(bf16[768,192]{0,1:T(8,128)(2,1)S(1)} %fusion.20, f32[]{:T(128)} %bitcast, bf16[192,1152]{1,0:T(8,128)(2,1)S(1)} %get-tuple-element.28, bf16[192,1152]{1,0:T(8,128)(2,1)S(1)} %get-tuple-element.29, bf16[192,1152]{1,0:T(8,128)(2,1)S(1)} %get-tuple-element.27, bf16[192,1152]{1,0:T(8,128)(2,1)S(1)} %get-tuple-element.26), kind=kOutput, calls=%fused_computation.4 | convolution fusion | flops 347258880 | bytes 2506756 | tf_op jit(solution)/shard_map/dot_general | solution.py:78
  26.2 0.7 convolution_add_fusion
  27.0 0.7 fusion.19
  27.7 0.5 multiply_convert_fusion
  28.2 1.9 %collective-permute-start.2 = (bf16[384,1152]{1,0:T(8,128)(2,1)S(1)}, bf16[384,1152]{1,0:T(8,128)(2,1)S(1)}, u32[]{:S(2)}, u32[]{:S(2)}) collective-permute-start(bf16[384,1152]{1,0:T(8,128)(2,1)S(1)} %multiply_convert_fusion), channel_id=1, source_target_pairs={{0,1},{1,0},{2,3},{3,2},{4,5},{5,4},{6,7},{7,6},{8,9},{9,8},{10,11... | collective-permute-start | bytes 2654216 | tf_op jit(solution)/shard_map/ppermute | solution.py:44
  30.1 1.3 %fusion.1 = bf16[192,1152]{1,0:T(8,128)(2,1)} fusion(bf16[768,192]{0,1:T(8,128)(2,1)S(1)} %fusion.19, f32[]{:T(128)} %bitcast, bf16[192,1152]{1,0:T(8,128)(2,1)S(1)} %get-tuple-element.28, bf16[192,1152]{1,0:T(8,128)(2,1)S(1)} %get-tuple-element.29, bf16[192,1152]{1,0:T(8,128)(2,1)S(1)} %get-tuple-element.27, bf16[192,1152]{1,0:T(8,128)(2,1)S(1)} %get-tuple-element.26), kind=kOutput, calls=%fused_computation.5 | convolution fusion | flops 347258880 | bytes 2506756 | tf_op jit(solution)/shard_map/dot_general | solution.py:78
  31.5 1.9 %collective-permute-start.4 = (bf16[192,1152]{1,0:T(8,128)(2,1)}, bf16[192,1152]{1,0:T(8,128)(2,1)}, u32[]{:S(2)}, u32[]{:S(2)}) collective-permute-start(bf16[192,1152]{1,0:T(8,128)(2,1)} %fusion.1), channel_id=1, source_target_pairs={{0,8},{4,12},{8,0},{12,4},{16,24},{20,28},{24,16},{28,20},{32,40},... | collective-permute-start | bytes 1327112 | tf_op jit(solution)/shard_map/ppermute | solution.py:29
  34.0 5.8 %collective-permute-start.3 = (bf16[192,1152]{1,0:T(8,128)(2,1)S(1)}, bf16[192,1152]{1,0:T(8,128)(2,1)}, u32[]{:S(2)}, u32[]{:S(2)}) collective-permute-start(bf16[192,1152]{1,0:T(8,128)(2,1)S(1)} %fusion.22), channel_id=1, source_target_pairs={{0,2},{1,3},{2,0},{3,1},{4,6},{5,7},{6,4},{7,5},{8,10},{9,11},{10,... | collective-permute-start | bytes 1327112 | tf_op jit(solution)/shard_map/ppermute | solution.py:44
  39.8 1.9 %collective-permute-start.6 = (bf16[192,1152]{1,0:T(8,128)(2,1)}, bf16[192,1152]{1,0:T(8,128)(2,1)S(1)}, u32[]{:S(2)}, u32[]{:S(2)}) collective-permute-start(bf16[192,1152]{1,0:T(8,128)(2,1)} %fusion), channel_id=1, source_target_pairs={{4,0},{5,1},{6,2},{7,3},{8,4},{9,5},{10,6},{11,7},{12,8},{13,9},{1... | collective-permute-start | bytes 1327112 | tf_op jit(solution)/shard_map/ppermute | solution.py:107
  41.8 1.9 %convolution_multiply_fusion = f32[192,1152]{1,0:T(8,128)S(1)} fusion(bf16[768,192]{0,1:T(8,128)(2,1)} %copy-done.4, f32[]{:T(128)} %bitcast, bf16[192,1152]{1,0:T(8,128)(2,1)} %copy-done.2, bf16[192,1152]{1,0:T(8,128)(2,1)} %copy-done.3, bf16[192,1152]{1,0:T(8,128)(2,1)} %copy-done.1, bf16[192,1152]{1,0:T(8,128)(2,1)S(1)} %get-tuple-element.26), kind=kOutput, calls=%fused_computation.1 | convolution fusion | flops 347037696 | bytes 2949124 | tf_op jit(solution)/shard_map/dot_general | solution.py:78
  43.7 4.5 %collective-permute-done.4 = bf16[192,1152]{1,0:T(8,128)(2,1)} collective-permute-done((bf16[192,1152]{1,0:T(8,128)(2,1)}, bf16[192,1152]{1,0:T(8,128)(2,1)}, u32[]{:S(2)}, u32[]{:S(2)}) %collective-permute-start.4) | collective-permute-done | bytes 442400 | tf_op jit(solution)/shard_map/ppermute | solution.py:29
  48.1 3.2 %collective-permute-start.5 = (bf16[192,1152]{1,0:T(8,128)(2,1)}, bf16[192,1152]{1,0:T(8,128)(2,1)S(1)}, u32[]{:S(2)}, u32[]{:S(2)}) collective-permute-start(bf16[192,1152]{1,0:T(8,128)(2,1)} %collective-permute-done.4), channel_id=1, source_target_pairs={{24,8},{25,9},{26,10},{27,11},{28,12},{29,13},{30,14},{31,15},{40,... | collective-permute-start | bytes 1327112 | tf_op jit(solution)/shard_map/ppermute | solution.py:39
  51.4 10.9 %collective-permute-done.3 = bf16[192,1152]{1,0:T(8,128)(2,1)} collective-permute-done((bf16[192,1152]{1,0:T(8,128)(2,1)S(1)}, bf16[192,1152]{1,0:T(8,128)(2,1)}, u32[]{:S(2)}, u32[]{:S(2)}) %collective-permute-start.3) | collective-permute-done | bytes 442400 | tf_op jit(solution)/shard_map/ppermute | solution.py:44
  62.3 2.0 %fusion.23 = f32[192,1152]{1,0:T(8,128)} fusion(f32[384,1152]{1,0:T(8,128)S(1)} %add_multiply_fusion, bf16[192,1152]{1,0:T(8,128)(2,1)} %collective-permute-done.3, bf16[384,1152]{1,0:T(8,128)(2,1)S(1)} %collective-permute-done.2), kind=kLoop, calls=%fused_computation.35 | loop fusion | flops 884736 | bytes 2654208 | tf_op jit(solution)/shard_map/add | solution.py:114
  64.4 9.7 %collective-permute-done.5 = bf16[192,1152]{1,0:T(8,128)(2,1)S(1)} collective-permute-done((bf16[192,1152]{1,0:T(8,128)(2,1)}, bf16[192,1152]{1,0:T(8,128)(2,1)S(1)}, u32[]{:S(2)}, u32[]{:S(2)}) %collective-permute-start.5) | collective-permute-done | bytes 442400 | tf_op jit(solution)/shard_map/ppermute | solution.py:39
  74.1 2.2 %convert_add_fusion = f32[192,1152]{1,0:T(8,128)} fusion(bf16[192,1152]{1,0:T(8,128)(2,1)S(1)} %collective-permute-done.5, bf16[192,1152]{1,0:T(8,128)(2,1)} %collective-permute-done.4, f32[192,1152]{1,0:T(8,128)S(1)} %convolution_multiply_fusion, bf16[192,1152]{1,0:T(8,128)(2,1)S(1)} %collective-permute-done.6, pred[]{:T(512)S(6)} %ge.3), kind=kLoop, calls=%fused_computation.36 | loop fusion | flops 1548288 | bytes 3096577 | tf_op jit(solution)/shard_map/add | solution.py:116
  (17 shorter events, 0.7 us)
Async XLA Ops:
  0.6 23.5 %collective-permute-start.1 = (bf16[192,1152]{1,0:T(8,128)(2,1)}, bf16[192,1152]{1,0:T(8,128)(2,1)S(1)}, u32[]{:S(2)}, u32[]{:S(2)}) collective-permute-start(bf16[192,1152]{1,0:T(8,128)(2,1)} %param.6), channel_id=1, source_target_pairs={{0,4},{1,5},{2,6},{3,7},{4,8},{5,9},{6,10},{7,11},{8,12},{9,13},{1... | collective-permute-start | bytes 1327112 | tf_op jit(solution)/shard_map/ppermute | solution.py:24
  6.1 3.1 %copy-start = (bf16[192,1152]{1,0:T(8,128)(2,1)S(1)}, bf16[192,1152]{1,0:T(8,128)(2,1)}, u32[]{:S(2)}) copy-start(bf16[192,1152]{1,0:T(8,128)(2,1)} %param.6) | copy-start | bytes 1327108
  7.8 22.3 %copy-start.1 = (bf16[192,1152]{1,0:T(8,128)(2,1)}, bf16[192,1152]{1,0:T(8,128)(2,1)S(1)}, u32[]{:S(2)}) copy-start(bf16[192,1152]{1,0:T(8,128)(2,1)S(1)} %get-tuple-element.27) | copy-start | bytes 1327108
  7.8 22.3 %copy-start.2 = (bf16[192,1152]{1,0:T(8,128)(2,1)}, bf16[192,1152]{1,0:T(8,128)(2,1)S(1)}, u32[]{:S(2)}) copy-start(bf16[192,1152]{1,0:T(8,128)(2,1)S(1)} %get-tuple-element.28) | copy-start | bytes 1327108
  7.8 22.3 %copy-start.3 = (bf16[192,1152]{1,0:T(8,128)(2,1)}, bf16[192,1152]{1,0:T(8,128)(2,1)S(1)}, u32[]{:S(2)}) copy-start(bf16[192,1152]{1,0:T(8,128)(2,1)S(1)} %get-tuple-element.29) | copy-start | bytes 1327108
  10.0 5.1 %copy-start.4 = (bf16[768,192]{0,1:T(8,128)(2,1)}, bf16[768,192]{0,1:T(8,128)(2,1)S(1)}, u32[]{:S(2)}) copy-start(bf16[768,192]{0,1:T(8,128)(2,1)S(1)} %fusion.21) | copy-start | bytes 884740
  10.0 16.9 %collective-permute-start = (bf16[192,1152]{1,0:T(8,128)(2,1)S(1)}, bf16[192,1152]{1,0:T(8,128)(2,1)S(1)}, u32[]{:S(2)}, u32[]{:S(2)}) collective-permute-start(bf16[192,1152]{1,0:T(8,128)(2,1)S(1)} %copy-done), channel_id=1, source_target_pairs={{0,8},{1,9},{2,10},{3,11},{4,12},{5,13},{6,14},{7,15},{8,16},{9,17... | collective-permute-start | bytes 1327112 | tf_op jit(solution)/shard_map/ppermute | solution.py:24
  28.2 5.7 %collective-permute-start.2 = (bf16[384,1152]{1,0:T(8,128)(2,1)S(1)}, bf16[384,1152]{1,0:T(8,128)(2,1)S(1)}, u32[]{:S(2)}, u32[]{:S(2)}) collective-permute-start(bf16[384,1152]{1,0:T(8,128)(2,1)S(1)} %multiply_convert_fusion), channel_id=1, source_target_pairs={{0,1},{1,0},{2,3},{3,2},{4,5},{5,4},{6,7},{7,6},{8,9},{9,8},{10,11... | collective-permute-start | bytes 2654216 | tf_op jit(solution)/shard_map/ppermute | solution.py:44
  31.5 16.7 %collective-permute-start.4 = (bf16[192,1152]{1,0:T(8,128)(2,1)}, bf16[192,1152]{1,0:T(8,128)(2,1)}, u32[]{:S(2)}, u32[]{:S(2)}) collective-permute-start(bf16[192,1152]{1,0:T(8,128)(2,1)} %fusion.1), channel_id=1, source_target_pairs={{0,8},{4,12},{8,0},{12,4},{16,24},{20,28},{24,16},{28,20},{32,40},... | collective-permute-start | bytes 1327112 | tf_op jit(solution)/shard_map/ppermute | solution.py:29
  34.0 28.3 %collective-permute-start.3 = (bf16[192,1152]{1,0:T(8,128)(2,1)S(1)}, bf16[192,1152]{1,0:T(8,128)(2,1)}, u32[]{:S(2)}, u32[]{:S(2)}) collective-permute-start(bf16[192,1152]{1,0:T(8,128)(2,1)S(1)} %fusion.22), channel_id=1, source_target_pairs={{0,2},{1,3},{2,0},{3,1},{4,6},{5,7},{6,4},{7,5},{8,10},{9,11},{10,... | collective-permute-start | bytes 1327112 | tf_op jit(solution)/shard_map/ppermute | solution.py:44
  39.8 34.3 %collective-permute-start.6 = (bf16[192,1152]{1,0:T(8,128)(2,1)}, bf16[192,1152]{1,0:T(8,128)(2,1)S(1)}, u32[]{:S(2)}, u32[]{:S(2)}) collective-permute-start(bf16[192,1152]{1,0:T(8,128)(2,1)} %fusion), channel_id=1, source_target_pairs={{4,0},{5,1},{6,2},{7,3},{8,4},{9,5},{10,6},{11,7},{12,8},{13,9},{1... | collective-permute-start | bytes 1327112 | tf_op jit(solution)/shard_map/ppermute | solution.py:107
  48.1 25.9 %collective-permute-start.5 = (bf16[192,1152]{1,0:T(8,128)(2,1)}, bf16[192,1152]{1,0:T(8,128)(2,1)S(1)}, u32[]{:S(2)}, u32[]{:S(2)}) collective-permute-start(bf16[192,1152]{1,0:T(8,128)(2,1)} %collective-permute-done.4), channel_id=1, source_target_pairs={{24,8},{25,9},{26,10},{27,11},{28,12},{29,13},{30,14},{31,15},{40,... | collective-permute-start | bytes 1327112 | tf_op jit(solution)/shard_map/ppermute | solution.py:39

commit v6 on v5

--- a/solution.py
+++ b/solution.py
@@ -84,29 +84,28 @@
     text2 = sent(going, 2)
     w1 = weight(text1, F32(-1.0))
     term1 = text_term(w1).astype(BF)
-    early = jnp.dot(w0, caption, preferred_element_type=F32) + jnp.dot(
-        w1, text1, preferred_element_type=F32
-    )
+
+    def product(w, rows, text):
+        return jnp.dot(w[rows], text, preferred_element_type=F32)
+
+    theirs, ours = slice(0, 2 * width), slice(2 * width, 4 * width)
+    early = product(w0, theirs, caption) + product(w1, theirs, text1)
     text2, term1, early = lax.optimization_barrier((text2, term1, early))
     w2 = weight(text2, F32(-1.0))
-
-    def image_part(rows):
-        return scale * (
-            early[rows] + jnp.dot(w2[rows], text2, preferred_element_type=F32)
-        )
-
-    give = image_part(slice(0, 2 * width)).astype(BF)
-    give, w2, term1 = lax.optimization_barrier((give, w2, term1))
+    give = (scale * (early + product(w2, theirs, text2))).astype(BF)
+    give, w0, w1, w2, term1 = lax.optimization_barrier((give, w0, w1, w2, term1))
     got = swapped(give, 1)
-    keep = image_part(slice(2 * width, 4 * width))
+    keep = product(w0, ours, caption) + product(w1, ours, text1)
+    keep, w2 = lax.optimization_barrier((keep, w2))
+    keep = scale * (keep + product(w2, ours, text2))
     far = (keep[:width] + got[:width].astype(F32)).astype(BF)
     near = keep[width:] + got[width:].astype(F32)
     term2 = text_term(w2).astype(BF)
     back2 = turned(term2, 2)
-    w0, term1, term2 = lax.optimization_barrier((w0, term1, term2))
+    w0, term1, _ = lax.optimization_barrier((w0, term1, term2))
     back1 = lax.ppermute(term1, AXES, [(j, i) for i, j in route(1)])
+    other = swapped(far, 2)
     text_grad = text_term(w0)
-    other = swapped(far, 2)
     x = lax.axis_index("blk") % X
     down = handed_down(back2)
     own2 = jnp.where(x >= X - 2, F32(0.0), back2.astype(F32))

time: 76.9 us -> 77.9 us (1.013)
    dot_general x4 -> x6, matrix products: 2.4 us -> 2.8 us  [product(): return jnp.dot(w[rows], text, preferred_element_type=F32)]
  transfers between devices with their start and end apart: 7 -> 7, of which waited for: 4 -> 5; matrix products, arithmetic and copies ran while one was open for 17% -> 17% of each run, Pallas kernels for 0% -> 0%
where the time goes in v6:
time: 77.9 us; the launch traced here: 77.2 us
  waiting for transfers between devices  34.3 us (44%)
  starting transfers between devices  24 us (31%)
  matrix products  9.68 us (12%)
  other arithmetic  4.52 us (6%)
  local copies, waits for them, and re-layouts  2.48 us (3%)
  between operations  2.24 us (3%)
    ppermute x2, waiting for transfers between devices, swapped(): return lax.ppermute(block, 'grp', [(i, i ^ bit) for i in range(n)])  11 us
    ppermute x1, waiting for transfers between devices, handed_down(): return lax.ppermute(block, AXES, [(j, i) for i, j in crossing])  9.69 us
    ppermute x2, waiting for transfers between devices, sent(): return lax.ppermute(block, AXES, route(distance))  9.32 us
    ppermute x2, starting transfers between devices, sent(): return lax.ppermute(block, AXES, route(distance))  8.94 us
    ppermute x2, starting transfers between devices, swapped(): return lax.ppermute(block, 'grp', [(i, i ^ bit) for i in range(n)])  7.7 us
    dot_general x3, matrix products, text_term(): lax.dot_general(w, photo, (((0,), (0,)), ((), ())), preferred_element_typ...  4.62 us
    ppermute x1, waiting for transfers between devices, turned(): lax.ppermute(block, 'blk', [(b, b // X * X + (b - distance) % X) for b in...  4.21 us
    ppermute x1, starting transfers between devices, handed_down(): return lax.ppermute(block, AXES, [(j, i) for i, j in crossing])  3.25 us
  transfers between devices with their start and end apart: 7, of which 5 were waited for; matrix products, arithmetic and copies ran while one was open for 17% of the time, Pallas kernels for 0%

profile of v6, /device:TPU:254, one launch (start us, length us, event | category | flops | bytes accessed | tf_op | source)
XLA Modules:
  0.0 77.2 jit_solution(3018604977818426332)
XLA Ops:
  0.6 4.6 %collective-permute-start.1 = (bf16[192,1152]{1,0:T(8,128)(2,1)}, bf16[192,1152]{1,0:T(8,128)(2,1)S(1)}, u32[]{:S(2)}, u32[]{:S(2)}) collective-permute-start(bf16[192,1152]{1,0:T(8,128)(2,1)} %param.6), channel_id=1, source_target_pairs={{0,4},{1,5},{2,6},{3,7},{4,8},{5,9},{6,10},{7,11},{8,12},{9,13},{1... | collective-permute-start | bytes 1327112 | tf_op jit(solution)/shard_map/ppermute | solution.py:24
  6.6 0.8 %constant_dynamic-slice_fusion.7 = (s32[1,192]{1,0:T(1,128)S(1)}, s32[1,192]{1,0:T(1,128)S(1)}, s32[1,192]{1,0:T(1,128)S(1)}, s32[1,192]{1,0:T(1,128)S(1)}) fusion(s32[1,768]{1,0:T(1,128)} %param.7, s32[]{:T(128)S(6)} %select_n.35, s32[]{:T(128)S(6)} %select_n.36, s32[]{:T(128)S(6)} %select_n.38, s32[]{:T(128)S(6)} %select_n.37), kind=kLoop, calls=%fused_computation.56 | loop fusion | bytes 6160 | tf_op jit(solution)/shard_map/dynamic_slice | solution.py:57
  7.5 1.6 %constant_dynamic-slice_fusion.3 = (bf16[192,1152]{1,0:T(8,128)(2,1)S(1)}, bf16[192,1152]{1,0:T(8,128)(2,1)S(1)}, bf16[192,1152]{1,0:T(8,128)(2,1)S(1)}, bf16[192,1152]{1,0:T(8,128)(2,1)S(1)}) fusion(bf16[768,1152]{1,0:T(8,128)(2,1)} %param.5, s32[]{:T(128)S(6)} %select_n.35, s32[]{:T(128)S(6)} %select_n.36, s32[]{:T(128)S(6)} %select_n.38, s32[]{:T(128)S(6)} %select_n.37), kind=kLoop, calls=%fused_computation.52 | loop fusion | bytes 3538960 | tf_op jit(solution)/shard_map/dynamic_slice | solution.py:57
  9.2 0.8 %fusion.22 = bf16[768,192]{0,1:T(8,128)(2,1)S(1)} fusion(bf16[192,1152]{1,0:T(8,128)(2,1)S(1)} %copy-done, f32[]{:T(128)} %bitcast.18, f32[]{:T(128)} %bitcast, s32[768]{0:T(1024)S(1)} %pad_add_fusion, s32[192]{0:T(256)S(1)} %iota_add_fusion, bf16[192,1152]{1,0:T(8,128)(2,1)S(1)} %get-tuple-element.36, bf16[192,1152]{1,0:T(8,128)(2,1)S(1)} %get-tuple-element.37, ...), kind=kOutput, calls=%fused_computation.33 | convolution fusion | flops 348438528 | bytes 2510600 | tf_op jit(solution)/shard_map/dot_general | solution.py:70
  10.0 4.3 %collective-permute-start = (bf16[192,1152]{1,0:T(8,128)(2,1)S(1)}, bf16[192,1152]{1,0:T(8,128)(2,1)S(1)}, u32[]{:S(2)}, u32[]{:S(2)}) collective-permute-start(bf16[192,1152]{1,0:T(8,128)(2,1)S(1)} %copy-done), channel_id=1, source_target_pairs={{0,8},{1,9},{2,10},{3,11},{4,12},{5,13},{6,14},{7,15},{8,16},{9,17... | collective-permute-start | bytes 1327112 | tf_op jit(solution)/shard_map/ppermute | solution.py:24
  14.8 9.3 %collective-permute-done.1 = bf16[192,1152]{1,0:T(8,128)(2,1)S(1)} collective-permute-done((bf16[192,1152]{1,0:T(8,128)(2,1)}, bf16[192,1152]{1,0:T(8,128)(2,1)S(1)}, u32[]{:S(2)}, u32[]{:S(2)}) %collective-permute-start.1) | collective-permute-done | bytes 442400 | tf_op jit(solution)/shard_map/ppermute | solution.py:24
  24.1 0.7 fusion.21
  24.9 1.3 %fusion.1 = bf16[192,1152]{1,0:T(8,128)(2,1)} fusion(bf16[768,192]{0,1:T(8,128)(2,1)S(1)} %fusion.21, f32[]{:T(128)} %bitcast, bf16[192,1152]{1,0:T(8,128)(2,1)S(1)} %get-tuple-element.36, bf16[192,1152]{1,0:T(8,128)(2,1)S(1)} %get-tuple-element.37, bf16[192,1152]{1,0:T(8,128)(2,1)S(1)} %get-tuple-element.35, bf16[192,1152]{1,0:T(8,128)(2,1)S(1)} %get-tuple-element.34), kind=kOutput, calls=%fused_computation.7 | convolution fusion | flops 347258880 | bytes 2506756 | tf_op jit(solution)/shard_map/dot_general | solution.py:78
  26.2 0.5 convolution_add_fusion.2
  26.7 0.7 fusion.20
  28.1 1.9 %collective-permute-start.2 = (bf16[384,1152]{1,0:T(8,128)(2,1)S(1)}, bf16[384,1152]{1,0:T(8,128)(2,1)S(1)}, u32[]{:S(2)}, u32[]{:S(2)}) collective-permute-start(bf16[384,1152]{1,0:T(8,128)(2,1)S(1)} %multiply_convert_fusion), channel_id=1, source_target_pairs={{0,1},{1,0},{2,3},{3,2},{4,5},{5,4},{6,7},{7,6},{8,9},{9,8},{10,11... | collective-permute-start | bytes 2654216 | tf_op jit(solution)/shard_map/ppermute | solution.py:44
  30.5 0.5 convolution_add_fusion.1
  31.0 1.3 %fusion.2 = bf16[192,1152]{1,0:T(8,128)(2,1)} fusion(bf16[768,192]{0,1:T(8,128)(2,1)S(1)} %fusion.20, f32[]{:T(128)} %bitcast, bf16[192,1152]{1,0:T(8,128)(2,1)S(1)} %get-tuple-element.36, bf16[192,1152]{1,0:T(8,128)(2,1)S(1)} %get-tuple-element.37, bf16[192,1152]{1,0:T(8,128)(2,1)S(1)} %get-tuple-element.35, bf16[192,1152]{1,0:T(8,128)(2,1)S(1)} %get-tuple-element.34), kind=kOutput, calls=%fused_computation.8 | convolution fusion | flops 347258880 | bytes 2506756 | tf_op jit(solution)/shard_map/dot_general | solution.py:78
  32.3 2.2 %collective-permute-start.4 = (bf16[192,1152]{1,0:T(8,128)(2,1)}, bf16[192,1152]{1,0:T(8,128)(2,1)}, u32[]{:S(2)}, u32[]{:S(2)}) collective-permute-start(bf16[192,1152]{1,0:T(8,128)(2,1)} %fusion.2), channel_id=1, source_target_pairs={{0,8},{4,12},{8,0},{12,4},{16,24},{20,28},{24,16},{28,20},{32,40},... | collective-permute-start | bytes 1327112 | tf_op jit(solution)/shard_map/ppermute | solution.py:29
  34.6 0.5 fusion
  35.1 5.8 %collective-permute-start.3 = (bf16[192,1152]{1,0:T(8,128)(2,1)S(1)}, bf16[192,1152]{1,0:T(8,128)(2,1)}, u32[]{:S(2)}, u32[]{:S(2)}) collective-permute-start(bf16[192,1152]{1,0:T(8,128)(2,1)S(1)} %fusion.23), channel_id=1, source_target_pairs={{0,2},{1,3},{2,0},{3,1},{4,6},{5,7},{6,4},{7,5},{8,10},{9,11},{10,... | collective-permute-start | bytes 1327112 | tf_op jit(solution)/shard_map/ppermute | solution.py:44
  40.9 1.9 %collective-permute-start.6 = (bf16[192,1152]{1,0:T(8,128)(2,1)}, bf16[192,1152]{1,0:T(8,128)(2,1)S(1)}, u32[]{:S(2)}, u32[]{:S(2)}) collective-permute-start(bf16[192,1152]{1,0:T(8,128)(2,1)} %fusion.1), channel_id=1, source_target_pairs={{4,0},{5,1},{6,2},{7,3},{8,4},{9,5},{10,6},{11,7},{12,8},{13,9},{1... | collective-permute-start | bytes 1327112 | tf_op jit(solution)/shard_map/ppermute | solution.py:106
  42.9 1.9 %convolution_multiply_fusion = f32[192,1152]{1,0:T(8,128)S(1)} fusion(bf16[768,192]{0,1:T(8,128)(2,1)} %copy-done.4, f32[]{:T(128)} %bitcast, bf16[192,1152]{1,0:T(8,128)(2,1)} %copy-done.2, bf16[192,1152]{1,0:T(8,128)(2,1)} %copy-done.3, bf16[192,1152]{1,0:T(8,128)(2,1)} %copy-done.1, bf16[192,1152]{1,0:T(8,128)(2,1)S(1)} %get-tuple-element.34), kind=kOutput, calls=%fused_computation.4 | convolution fusion | flops 347037696 | bytes 2949124 | tf_op jit(solution)/shard_map/dot_general | solution.py:78
  44.8 4.2 %collective-permute-done.4 = bf16[192,1152]{1,0:T(8,128)(2,1)} collective-permute-done((bf16[192,1152]{1,0:T(8,128)(2,1)}, bf16[192,1152]{1,0:T(8,128)(2,1)}, u32[]{:S(2)}, u32[]{:S(2)}) %collective-permute-start.4) | collective-permute-done | bytes 442400 | tf_op jit(solution)/shard_map/ppermute | solution.py:29
  49.0 3.2 %collective-permute-start.5 = (bf16[192,1152]{1,0:T(8,128)(2,1)}, bf16[192,1152]{1,0:T(8,128)(2,1)S(1)}, u32[]{:S(2)}, u32[]{:S(2)}) collective-permute-start(bf16[192,1152]{1,0:T(8,128)(2,1)} %collective-permute-done.4), channel_id=1, source_target_pairs={{24,8},{25,9},{26,10},{27,11},{28,12},{29,13},{30,14},{31,15},{40,... | collective-permute-start | bytes 1327112 | tf_op jit(solution)/shard_map/ppermute | solution.py:39
  52.3 11.0 %collective-permute-done.3 = bf16[192,1152]{1,0:T(8,128)(2,1)} collective-permute-done((bf16[192,1152]{1,0:T(8,128)(2,1)S(1)}, bf16[192,1152]{1,0:T(8,128)(2,1)}, u32[]{:S(2)}, u32[]{:S(2)}) %collective-permute-start.3) | collective-permute-done | bytes 442400 | tf_op jit(solution)/shard_map/ppermute | solution.py:44
  63.3 2.0 %fusion.24 = f32[192,1152]{1,0:T(8,128)} fusion(f32[384,1152]{1,0:T(8,128)S(1)} %fusion, bf16[192,1152]{1,0:T(8,128)(2,1)} %collective-permute-done.3, bf16[384,1152]{1,0:T(8,128)(2,1)S(1)} %collective-permute-done.2), kind=kLoop, calls=%fused_computation.37 | loop fusion | flops 884736 | bytes 2654208 | tf_op jit(solution)/shard_map/add | solution.py:113
  65.3 9.7 %collective-permute-done.5 = bf16[192,1152]{1,0:T(8,128)(2,1)S(1)} collective-permute-done((bf16[192,1152]{1,0:T(8,128)(2,1)}, bf16[192,1152]{1,0:T(8,128)(2,1)S(1)}, u32[]{:S(2)}, u32[]{:S(2)}) %collective-permute-start.5) | collective-permute-done | bytes 442400 | tf_op jit(solution)/shard_map/ppermute | solution.py:39
  75.1 2.1 %convert_add_fusion = f32[192,1152]{1,0:T(8,128)} fusion(bf16[192,1152]{1,0:T(8,128)(2,1)S(1)} %collective-permute-done.5, bf16[192,1152]{1,0:T(8,128)(2,1)} %collective-permute-done.4, f32[192,1152]{1,0:T(8,128)S(1)} %convolution_multiply_fusion, bf16[192,1152]{1,0:T(8,128)(2,1)S(1)} %collective-permute-done.6, pred[]{:T(512)S(6)} %ge.3), kind=kLoop, calls=%fused_computation.38 | loop fusion | flops 1548288 | bytes 3096577 | tf_op jit(solution)/shard_map/add | solution.py:115
  (20 shorter events, 1.8 us)
Async XLA Ops:
  0.6 23.5 %collective-permute-start.1 = (bf16[192,1152]{1,0:T(8,128)(2,1)}, bf16[192,1152]{1,0:T(8,128)(2,1)S(1)}, u32[]{:S(2)}, u32[]{:S(2)}) collective-permute-start(bf16[192,1152]{1,0:T(8,128)(2,1)} %param.6), channel_id=1, source_target_pairs={{0,4},{1,5},{2,6},{3,7},{4,8},{5,9},{6,10},{7,11},{8,12},{9,13},{1... | collective-permute-start | bytes 1327112 | tf_op jit(solution)/shard_map/ppermute | solution.py:24
  7.5 1.7 %copy-start = (bf16[192,1152]{1,0:T(8,128)(2,1)S(1)}, bf16[192,1152]{1,0:T(8,128)(2,1)}, u32[]{:S(2)}) copy-start(bf16[192,1152]{1,0:T(8,128)(2,1)} %param.6) | copy-start | bytes 1327108
  9.1 21.9 %copy-start.1 = (bf16[192,1152]{1,0:T(8,128)(2,1)}, bf16[192,1152]{1,0:T(8,128)(2,1)S(1)}, u32[]{:S(2)}) copy-start(bf16[192,1152]{1,0:T(8,128)(2,1)S(1)} %get-tuple-element.35) | copy-start | bytes 1327108
  9.1 21.9 %copy-start.2 = (bf16[192,1152]{1,0:T(8,128)(2,1)}, bf16[192,1152]{1,0:T(8,128)(2,1)S(1)}, u32[]{:S(2)}) copy-start(bf16[192,1152]{1,0:T(8,128)(2,1)S(1)} %get-tuple-element.36) | copy-start | bytes 1327108
  9.1 21.9 %copy-start.3 = (bf16[192,1152]{1,0:T(8,128)(2,1)}, bf16[192,1152]{1,0:T(8,128)(2,1)S(1)}, u32[]{:S(2)}) copy-start(bf16[192,1152]{1,0:T(8,128)(2,1)S(1)} %get-tuple-element.37) | copy-start | bytes 1327108
  10.0 20.0 %copy-start.4 = (bf16[768,192]{0,1:T(8,128)(2,1)}, bf16[768,192]{0,1:T(8,128)(2,1)S(1)}, u32[]{:S(2)}) copy-start(bf16[768,192]{0,1:T(8,128)(2,1)S(1)} %fusion.22) | copy-start | bytes 884740
  10.0 16.7 %collective-permute-start = (bf16[192,1152]{1,0:T(8,128)(2,1)S(1)}, bf16[192,1152]{1,0:T(8,128)(2,1)S(1)}, u32[]{:S(2)}, u32[]{:S(2)}) collective-permute-start(bf16[192,1152]{1,0:T(8,128)(2,1)S(1)} %copy-done), channel_id=1, source_target_pairs={{0,8},{1,9},{2,10},{3,11},{4,12},{5,13},{6,14},{7,15},{8,16},{9,17... | collective-permute-start | bytes 1327112 | tf_op jit(solution)/shard_map/ppermute | solution.py:24
  28.1 7.0 %collective-permute-start.2 = (bf16[384,1152]{1,0:T(8,128)(2,1)S(1)}, bf16[384,1152]{1,0:T(8,128)(2,1)S(1)}, u32[]{:S(2)}, u32[]{:S(2)}) collective-permute-start(bf16[384,1152]{1,0:T(8,128)(2,1)S(1)} %multiply_convert_fusion), channel_id=1, source_target_pairs={{0,1},{1,0},{2,3},{3,2},{4,5},{5,4},{6,7},{7,6},{8,9},{9,8},{10,11... | collective-permute-start | bytes 2654216 | tf_op jit(solution)/shard_map/ppermute | solution.py:44
  32.3 16.7 %collective-permute-start.4 = (bf16[192,1152]{1,0:T(8,128)(2,1)}, bf16[192,1152]{1,0:T(8,128)(2,1)}, u32[]{:S(2)}, u32[]{:S(2)}) collective-permute-start(bf16[192,1152]{1,0:T(8,128)(2,1)} %fusion.2), channel_id=1, source_target_pairs={{0,8},{4,12},{8,0},{12,4},{16,24},{20,28},{24,16},{28,20},{32,40},... | collective-permute-start | bytes 1327112 | tf_op jit(solution)/shard_map/ppermute | solution.py:29
  35.1 28.1 %collective-permute-start.3 = (bf16[192,1152]{1,0:T(8,128)(2,1)S(1)}, bf16[192,1152]{1,0:T(8,128)(2,1)}, u32[]{:S(2)}, u32[]{:S(2)}) collective-permute-start(bf16[192,1152]{1,0:T(8,128)(2,1)S(1)} %fusion.23), channel_id=1, source_target_pairs={{0,2},{1,3},{2,0},{3,1},{4,6},{5,7},{6,4},{7,5},{8,10},{9,11},{10,... | collective-permute-start | bytes 1327112 | tf_op jit(solution)/shard_map/ppermute | solution.py:44
  40.9 34.1 %collective-permute-start.6 = (bf16[192,1152]{1,0:T(8,128)(2,1)}, bf16[192,1152]{1,0:T(8,128)(2,1)S(1)}, u32[]{:S(2)}, u32[]{:S(2)}) collective-permute-start(bf16[192,1152]{1,0:T(8,128)(2,1)} %fusion.1), channel_id=1, source_target_pairs={{4,0},{5,1},{6,2},{7,3},{8,4},{9,5},{10,6},{11,7},{12,8},{13,9},{1... | collective-permute-start | bytes 1327112 | tf_op jit(solution)/shard_map/ppermute | solution.py:106
  49.0 26.0 %collective-permute-start.5 = (bf16[192,1152]{1,0:T(8,128)(2,1)}, bf16[192,1152]{1,0:T(8,128)(2,1)S(1)}, u32[]{:S(2)}, u32[]{:S(2)}) collective-permute-start(bf16[192,1152]{1,0:T(8,128)(2,1)} %collective-permute-done.4), channel_id=1, source_target_pairs={{24,8},{25,9},{26,10},{27,11},{28,12},{29,13},{30,14},{31,15},{40,... | collective-permute-start | bytes 1327112 | tf_op jit(solution)/shard_map/ppermute | solution.py:39

commit v7 on v6

--- a/solution.py
+++ b/solution.py
@@ -100,19 +100,20 @@
     keep = scale * (keep + product(w2, ours, text2))
     far = (keep[:width] + got[:width].astype(F32)).astype(BF)
     near = keep[width:] + got[width:].astype(F32)
+    other = swapped(far, 2)
+    w2, _ = lax.optimization_barrier((w2, far))
     term2 = text_term(w2).astype(BF)
     back2 = turned(term2, 2)
     w0, term1, _ = lax.optimization_barrier((w0, term1, term2))
     back1 = lax.ppermute(term1, AXES, [(j, i) for i, j in route(1)])
-    other = swapped(far, 2)
     text_grad = text_term(w0)
-    x = lax.axis_index("blk") % X
-    down = handed_down(back2)
-    own2 = jnp.where(x >= X - 2, F32(0.0), back2.astype(F32))
 
     image_grad = near + other.astype(F32)
-    image_grad, down = lax.optimization_barrier((image_grad, down))
-    text_grad = text_grad + back1.astype(F32) + own2 + down.astype(F32)
+    back2, _ = lax.optimization_barrier((back2, image_grad))
+    x = lax.axis_index("blk") % X
+    down = handed_down(jnp.where(x >= X - 2, back2, BF(0.0)))
+    text_grad = text_grad + jnp.where(x >= X - 2, F32(0.0), back2.astype(F32))
+    text_grad = text_grad + back1.astype(F32) + down.astype(F32)
     return image_grad, text_grad
 
 

time: 77.9 us -> 86.8 us (1.11)
  the two profiles are of different devices: /device:TPU:254 before, /device:TPU:6 now
where the time goes in v7:
time: 86.8 us; the launch traced here: 86.3 us
  starting transfers between devices  43.5 us (50%)
  waiting for transfers between devices  25.5 us (29%)
  matrix products  8.98 us (10%)
  other arithmetic  3.53 us (4%)
  local copies, waits for them, and re-layouts  2.51 us (3%)
  between operations  2.32 us (3%)
    ppermute x1, starting transfers between devices, turned(): lax.ppermute(block, 'blk', [(b, b // X * X + (b - distance) % X) for b in...  13.4 us
    ppermute x1, starting transfers between devices, handed_down(): return lax.ppermute(block, AXES, [(j, i) for i, j in crossing])  11.1 us
    ppermute x2, starting transfers between devices, swapped(): return lax.ppermute(block, 'grp', [(i, i ^ bit) for i in range(n)])  8.77 us
    ppermute x1, waiting for transfers between devices, handed_down(): return lax.ppermute(block, AXES, [(j, i) for i, j in crossing])  8.7 us
    ppermute x1, waiting for transfers between devices, turned(): lax.ppermute(block, 'blk', [(b, b // X * X + (b - distance) % X) for b in...  8.21 us
    ppermute x2, starting transfers between devices, sent(): return lax.ppermute(block, AXES, route(distance))  7.73 us
    ppermute x2, waiting for transfers between devices, sent(): return lax.ppermute(block, AXES, route(distance))  7.66 us
    dot_general x3, matrix products, text_term(): lax.dot_general(w, photo, (((0,), (0,)), ((), ())), preferred_element_typ...  3.89 us
  transfers between devices with their start and end apart: 7, of which 5 were waited for; matrix products, arithmetic and copies ran while one was open for 14% of the time, Pallas kernels for 0%

profile of v7, /device:TPU:6, one launch (start us, length us, event | category | flops | bytes accessed | tf_op | source)
XLA Modules:
  0.0 86.3 jit_solution(12727950396612739473)
XLA Ops:
  0.6 3.4 %collective-permute-start.1 = (bf16[192,1152]{1,0:T(8,128)(2,1)}, bf16[192,1152]{1,0:T(8,128)(2,1)S(1)}, u32[]{:S(2)}, u32[]{:S(2)}) collective-permute-start(bf16[192,1152]{1,0:T(8,128)(2,1)} %param.6), channel_id=1, source_target_pairs={{0,4},{1,5},{2,6},{3,7},{4,8},{5,9},{6,10},{7,11},{8,12},{9,13},{1... | collective-permute-start | bytes 1327112 | tf_op jit(solution)/shard_map/ppermute | solution.py:24
  5.4 0.8 constant_dynamic-slice_fusion.7
  6.3 1.6 %constant_dynamic-slice_fusion.3 = (bf16[192,1152]{1,0:T(8,128)(2,1)S(1)}, bf16[192,1152]{1,0:T(8,128)(2,1)S(1)}, bf16[192,1152]{1,0:T(8,128)(2,1)S(1)}, bf16[192,1152]{1,0:T(8,128)(2,1)S(1)}) fusion(bf16[768,1152]{1,0:T(8,128)(2,1)} %param.5, s32[]{:T(128)S(6)} %select_n.41, s32[]{:T(128)S(6)} %select_n.42, s32[]{:T(128)S(6)} %select_n.44, s32[]{:T(128)S(6)} %select_n.43), kind=kLoop, calls=%fused_computation.53 | loop fusion | bytes 3538960 | tf_op jit(solution)/shard_map/dynamic_slice | solution.py:57
  8.0 0.8 fusion.22
  8.8 4.3 %collective-permute-start = (bf16[192,1152]{1,0:T(8,128)(2,1)S(1)}, bf16[192,1152]{1,0:T(8,128)(2,1)S(1)}, u32[]{:S(2)}, u32[]{:S(2)}) collective-permute-start(bf16[192,1152]{1,0:T(8,128)(2,1)S(1)} %copy-done), channel_id=1, source_target_pairs={{0,8},{1,9},{2,10},{3,11},{4,12},{5,13},{6,14},{7,15},{8,16},{9,17... | collective-permute-start | bytes 1327112 | tf_op jit(solution)/shard_map/ppermute | solution.py:24
  13.6 1.0 %collective-permute-done.1 = bf16[192,1152]{1,0:T(8,128)(2,1)S(1)} collective-permute-done((bf16[192,1152]{1,0:T(8,128)(2,1)}, bf16[192,1152]{1,0:T(8,128)(2,1)S(1)}, u32[]{:S(2)}, u32[]{:S(2)}) %collective-permute-start.1) | collective-permute-done | bytes 442400 | tf_op jit(solution)/shard_map/ppermute | solution.py:24
  14.6 0.7 fusion.21
  15.4 1.3 %fusion.1 = bf16[192,1152]{1,0:T(8,128)(2,1)} fusion(bf16[768,192]{0,1:T(8,128)(2,1)S(1)} %fusion.21, f32[]{:T(128)} %bitcast, bf16[192,1152]{1,0:T(8,128)(2,1)S(1)} %get-tuple-element.36, bf16[192,1152]{1,0:T(8,128)(2,1)S(1)} %get-tuple-element.37, bf16[192,1152]{1,0:T(8,128)(2,1)S(1)} %get-tuple-element.35, bf16[192,1152]{1,0:T(8,128)(2,1)S(1)} %get-tuple-element.34), kind=kOutput, calls=%fused_computation.7 | convolution fusion | flops 347258880 | bytes 2506756 | tf_op jit(solution)/shard_map/dot_general | solution.py:78
  16.7 0.5 convolution_add_fusion.2
  17.2 6.6 %collective-permute-done = bf16[192,1152]{1,0:T(8,128)(2,1)S(1)} collective-permute-done((bf16[192,1152]{1,0:T(8,128)(2,1)S(1)}, bf16[192,1152]{1,0:T(8,128)(2,1)S(1)}, u32[]{:S(2)}, u32[]{:S(2)}) %collective-permute-start) | collective-permute-done | bytes 442400 | tf_op jit(solution)/shard_map/ppermute | solution.py:24
  23.8 0.7 fusion.20
  25.2 1.9 %collective-permute-start.2 = (bf16[384,1152]{1,0:T(8,128)(2,1)S(1)}, bf16[384,1152]{1,0:T(8,128)(2,1)S(1)}, u32[]{:S(2)}, u32[]{:S(2)}) collective-permute-start(bf16[384,1152]{1,0:T(8,128)(2,1)S(1)} %multiply_convert_fusion), channel_id=1, source_target_pairs={{0,1},{1,0},{2,3},{3,2},{4,5},{5,4},{6,7},{7,6},{8,9},{9,8},{10,11... | collective-permute-start | bytes 2654216 | tf_op jit(solution)/shard_map/ppermute | solution.py:44
  28.1 0.5 fusion
  28.6 0.9 %collective-permute-done.2 = bf16[384,1152]{1,0:T(8,128)(2,1)S(1)} collective-permute-done((bf16[384,1152]{1,0:T(8,128)(2,1)S(1)}, bf16[384,1152]{1,0:T(8,128)(2,1)S(1)}, u32[]{:S(2)}, u32[]{:S(2)}) %collective-permute-start.2) | collective-permute-done | bytes 884768 | tf_op jit(solution)/shard_map/ppermute | solution.py:44
  29.6 6.9 %collective-permute-start.3 = (bf16[192,1152]{1,0:T(8,128)(2,1)S(1)}, bf16[192,1152]{1,0:T(8,128)(2,1)}, u32[]{:S(2)}, u32[]{:S(2)}) collective-permute-start(bf16[192,1152]{1,0:T(8,128)(2,1)S(1)} %fusion.23), channel_id=1, source_target_pairs={{0,2},{1,3},{2,0},{3,1},{4,6},{5,7},{6,4},{7,5},{8,10},{9,11},{10,... | collective-permute-start | bytes 1327112 | tf_op jit(solution)/shard_map/ppermute | solution.py:44
  36.5 2.0 %fusion.2 = bf16[192,1152]{1,0:T(8,128)(2,1)S(1)} fusion(bf16[768,192]{0,1:T(8,128)(2,1)} %copy-done.9, f32[]{:T(128)} %bitcast, bf16[192,1152]{1,0:T(8,128)(2,1)} %copy-done.3, bf16[192,1152]{1,0:T(8,128)(2,1)} %copy-done.5, bf16[192,1152]{1,0:T(8,128)(2,1)} %copy-done.1, bf16[192,1152]{1,0:T(8,128)(2,1)S(1)} %get-tuple-element.34), kind=kOutput, calls=%fused_computation.8 | convolution fusion | flops 347258880 | bytes 2506756 | tf_op jit(solution)/shard_map/dot_general | solution.py:78
  38.6 13.4 %collective-permute-start.4 = (bf16[192,1152]{1,0:T(8,128)(2,1)S(1)}, bf16[192,1152]{1,0:T(8,128)(2,1)S(1)}, u32[]{:S(2)}, u32[]{:S(2)}) collective-permute-start(bf16[192,1152]{1,0:T(8,128)(2,1)S(1)} %fusion.2), channel_id=1, source_target_pairs={{0,8},{4,12},{8,0},{12,4},{16,24},{20,28},{24,16},{28,20},{32,40},... | collective-permute-start | bytes 1327112 | tf_op jit(solution)/shard_map/ppermute | solution.py:29
  52.0 2.5 %collective-permute-start.5 = (bf16[192,1152]{1,0:T(8,128)(2,1)S(1)}, bf16[192,1152]{1,0:T(8,128)(2,1)S(1)}, u32[]{:S(2)}, u32[]{:S(2)}) collective-permute-start(bf16[192,1152]{1,0:T(8,128)(2,1)S(1)} %copy-done.10), channel_id=1, source_target_pairs={{4,0},{5,1},{6,2},{7,3},{8,4},{9,5},{10,6},{11,7},{12,8},{13,9},{1... | collective-permute-start | bytes 1327112 | tf_op jit(solution)/shard_map/ppermute | solution.py:108
  54.5 2.0 %fusion.24 = f32[192,1152]{1,0:T(8,128)} fusion(f32[384,1152]{1,0:T(8,128)S(1)} %fusion, bf16[192,1152]{1,0:T(8,128)(2,1)} %collective-permute-done.3, bf16[384,1152]{1,0:T(8,128)(2,1)S(1)} %collective-permute-done.2), kind=kLoop, calls=%fused_computation.37 | loop fusion | flops 884736 | bytes 2654208 | tf_op jit(solution)/shard_map/add | solution.py:111
  56.5 8.2 %collective-permute-done.4 = bf16[192,1152]{1,0:T(8,128)(2,1)S(1)} collective-permute-done((bf16[192,1152]{1,0:T(8,128)(2,1)S(1)}, bf16[192,1152]{1,0:T(8,128)(2,1)S(1)}, u32[]{:S(2)}, u32[]{:S(2)}) %collective-permute-start.4) | collective-permute-done | bytes 442400 | tf_op jit(solution)/shard_map/ppermute | solution.py:29
  64.8 11.1 %collective-permute-start.6 = (bf16[192,1152]{1,0:T(8,128)(2,1)S(1)}, bf16[192,1152]{1,0:T(8,128)(2,1)S(1)}, u32[]{:S(2)}, u32[]{:S(2)}) collective-permute-start(bf16[192,1152]{1,0:T(8,128)(2,1)S(1)} %broadcast_select_fusion), channel_id=1, source_target_pairs={{24,8},{25,9},{26,10},{27,11},{28,12},{29,13},{30,14},{31,15},{40,... | collective-permute-start | bytes 1327112 | tf_op jit(solution)/shard_map/ppermute | solution.py:39
  75.9 0.6 convolution_multiply_fusion
  76.5 8.7 %collective-permute-done.6 = bf16[192,1152]{1,0:T(8,128)(2,1)S(1)} collective-permute-done((bf16[192,1152]{1,0:T(8,128)(2,1)S(1)}, bf16[192,1152]{1,0:T(8,128)(2,1)S(1)}, u32[]{:S(2)}, u32[]{:S(2)}) %collective-permute-start.6) | collective-permute-done | bytes 442400 | tf_op jit(solution)/shard_map/ppermute | solution.py:39
  85.2 1.1 %convert_add_fusion = f32[192,1152]{1,0:T(8,128)} fusion(bf16[192,1152]{1,0:T(8,128)(2,1)S(1)} %collective-permute-done.6, bf16[192,1152]{1,0:T(8,128)(2,1)S(1)} %collective-permute-done.5, f32[192,1152]{1,0:T(8,128)S(1)} %convolution_multiply_fusion, bf16[192,1152]{1,0:T(8,128)(2,1)S(1)} %collective-permute-done.4, pred[]{:T(512)S(6)} %ge.4), kind=kLoop, calls=%fused_computation.38 | loop fusion | flops 1548288 | bytes 3096577 | tf_op jit(solution)/shard_map/add | solution.py:116
  (33 shorter events, 2.3 us)
Async XLA Ops:
  0.6 14.0 %collective-permute-start.1 = (bf16[192,1152]{1,0:T(8,128)(2,1)}, bf16[192,1152]{1,0:T(8,128)(2,1)S(1)}, u32[]{:S(2)}, u32[]{:S(2)}) collective-permute-start(bf16[192,1152]{1,0:T(8,128)(2,1)} %param.6), channel_id=1, source_target_pairs={{0,4},{1,5},{2,6},{3,7},{4,8},{5,9},{6,10},{7,11},{8,12},{9,13},{1... | collective-permute-start | bytes 1327112 | tf_op jit(solution)/shard_map/ppermute | solution.py:24
  6.3 1.7 %copy-start = (bf16[192,1152]{1,0:T(8,128)(2,1)S(1)}, bf16[192,1152]{1,0:T(8,128)(2,1)}, u32[]{:S(2)}) copy-start(bf16[192,1152]{1,0:T(8,128)(2,1)} %param.6) | copy-start | bytes 1327108
  7.9 15.9 %copy-start.1 = (bf16[192,1152]{1,0:T(8,128)(2,1)}, bf16[192,1152]{1,0:T(8,128)(2,1)S(1)}, u32[]{:S(2)}) copy-start(bf16[192,1152]{1,0:T(8,128)(2,1)S(1)} %get-tuple-element.35) | copy-start | bytes 1327108
  7.9 15.9 %copy-start.3 = (bf16[192,1152]{1,0:T(8,128)(2,1)}, bf16[192,1152]{1,0:T(8,128)(2,1)S(1)}, u32[]{:S(2)}) copy-start(bf16[192,1152]{1,0:T(8,128)(2,1)S(1)} %get-tuple-element.36) | copy-start | bytes 1327108
  7.9 15.9 %copy-start.5 = (bf16[192,1152]{1,0:T(8,128)(2,1)}, bf16[192,1152]{1,0:T(8,128)(2,1)S(1)}, u32[]{:S(2)}) copy-start(bf16[192,1152]{1,0:T(8,128)(2,1)S(1)} %get-tuple-element.37) | copy-start | bytes 1327108
  8.8 18.4 %copy-start.7 = (bf16[768,192]{0,1:T(8,128)(2,1)}, bf16[768,192]{0,1:T(8,128)(2,1)S(1)}, u32[]{:S(2)}) copy-start(bf16[768,192]{0,1:T(8,128)(2,1)S(1)} %fusion.22) | copy-start | bytes 884740
  8.8 15.0 %collective-permute-start = (bf16[192,1152]{1,0:T(8,128)(2,1)S(1)}, bf16[192,1152]{1,0:T(8,128)(2,1)S(1)}, u32[]{:S(2)}, u32[]{:S(2)}) collective-permute-start(bf16[192,1152]{1,0:T(8,128)(2,1)S(1)} %copy-done), channel_id=1, source_target_pairs={{0,8},{1,9},{2,10},{3,11},{4,12},{5,13},{6,14},{7,15},{8,16},{9,17... | collective-permute-start | bytes 1327112 | tf_op jit(solution)/shard_map/ppermute | solution.py:24
  24.6 3.5 %copy-start.9 = (bf16[768,192]{0,1:T(8,128)(2,1)}, bf16[768,192]{0,1:T(8,128)(2,1)S(1)}, u32[]{:S(2)}) copy-start(bf16[768,192]{0,1:T(8,128)(2,1)S(1)} %fusion.20) | copy-start | bytes 884740
  25.2 4.3 %collective-permute-start.2 = (bf16[384,1152]{1,0:T(8,128)(2,1)S(1)}, bf16[384,1152]{1,0:T(8,128)(2,1)S(1)}, u32[]{:S(2)}, u32[]{:S(2)}) collective-permute-start(bf16[384,1152]{1,0:T(8,128)(2,1)S(1)} %multiply_convert_fusion), channel_id=1, source_target_pairs={{0,1},{1,0},{2,3},{3,2},{4,5},{5,4},{6,7},{7,6},{8,9},{9,8},{10,11... | collective-permute-start | bytes 2654216 | tf_op jit(solution)/shard_map/ppermute | solution.py:44
  29.6 24.8 %collective-permute-start.3 = (bf16[192,1152]{1,0:T(8,128)(2,1)S(1)}, bf16[192,1152]{1,0:T(8,128)(2,1)}, u32[]{:S(2)}, u32[]{:S(2)}) collective-permute-start(bf16[192,1152]{1,0:T(8,128)(2,1)S(1)} %fusion.23), channel_id=1, source_target_pairs={{0,2},{1,3},{2,0},{3,1},{4,6},{5,7},{6,4},{7,5},{8,10},{9,11},{10,... | collective-permute-start | bytes 1327112 | tf_op jit(solution)/shard_map/ppermute | solution.py:44
  36.5 15.4 %copy-start.10 = (bf16[192,1152]{1,0:T(8,128)(2,1)S(1)}, bf16[192,1152]{1,0:T(8,128)(2,1)}, u32[]{:S(2)}) copy-start(bf16[192,1152]{1,0:T(8,128)(2,1)} %fusion.1) | copy-start | bytes 1327108
  38.5 37.4 %copy-start.2 = (bf16[192,1152]{1,0:T(8,128)(2,1)S(1)}, bf16[192,1152]{1,0:T(8,128)(2,1)}, u32[]{:S(2)}) copy-start(bf16[192,1152]{1,0:T(8,128)(2,1)} %copy-done.1) | copy-start | bytes 1327108
  38.5 37.4 %copy-start.4 = (bf16[192,1152]{1,0:T(8,128)(2,1)S(1)}, bf16[192,1152]{1,0:T(8,128)(2,1)}, u32[]{:S(2)}) copy-start(bf16[192,1152]{1,0:T(8,128)(2,1)} %copy-done.3) | copy-start | bytes 1327108
  38.5 37.4 %copy-start.6 = (bf16[192,1152]{1,0:T(8,128)(2,1)S(1)}, bf16[192,1152]{1,0:T(8,128)(2,1)}, u32[]{:S(2)}) copy-start(bf16[192,1152]{1,0:T(8,128)(2,1)} %copy-done.5) | copy-start | bytes 1327108
  38.6 37.4 %copy-start.8 = (bf16[768,192]{0,1:T(8,128)(2,1)S(1)}, bf16[768,192]{0,1:T(8,128)(2,1)}, u32[]{:S(2)}) copy-start(bf16[768,192]{0,1:T(8,128)(2,1)} %copy-done.7) | copy-start | bytes 884740
  38.6 26.1 %collective-permute-start.4 = (bf16[192,1152]{1,0:T(8,128)(2,1)S(1)}, bf16[192,1152]{1,0:T(8,128)(2,1)S(1)}, u32[]{:S(2)}, u32[]{:S(2)}) collective-permute-start(bf16[192,1152]{1,0:T(8,128)(2,1)S(1)} %fusion.2), channel_id=1, source_target_pairs={{0,8},{4,12},{8,0},{12,4},{16,24},{20,28},{24,16},{28,20},{32,40},... | collective-permute-start | bytes 1327112 | tf_op jit(solution)/shard_map/ppermute | solution.py:29
  52.0 24.5 %collective-permute-start.5 = (bf16[192,1152]{1,0:T(8,128)(2,1)S(1)}, bf16[192,1152]{1,0:T(8,128)(2,1)S(1)}, u32[]{:S(2)}, u32[]{:S(2)}) collective-permute-start(bf16[192,1152]{1,0:T(8,128)(2,1)S(1)} %copy-done.10), channel_id=1, source_target_pairs={{4,0},{5,1},{6,2},{7,3},{8,4},{9,5},{10,6},{11,7},{12,8},{13,9},{1... | collective-permute-start | bytes 1327112 | tf_op jit(solution)/shard_map/ppermute | solution.py:108
  64.8 20.5 %collective-permute-start.6 = (bf16[192,1152]{1,0:T(8,128)(2,1)S(1)}, bf16[192,1152]{1,0:T(8,128)(2,1)S(1)}, u32[]{:S(2)}, u32[]{:S(2)}) collective-permute-start(bf16[192,1152]{1,0:T(8,128)(2,1)S(1)} %broadcast_select_fusion), channel_id=1, source_target_pairs={{24,8},{25,9},{26,10},{27,11},{28,12},{29,13},{30,14},{31,15},{40,... | collective-permute-start | bytes 1327112 | tf_op jit(solution)/shard_map/ppermute | solution.py:39

commit v8 on v6

--- a/solution.py
+++ b/solution.py
@@ -95,9 +95,10 @@
     give = (scale * (early + product(w2, theirs, text2))).astype(BF)
     give, w0, w1, w2, term1 = lax.optimization_barrier((give, w0, w1, w2, term1))
     got = swapped(give, 1)
-    keep = product(w0, ours, caption) + product(w1, ours, text1)
-    keep, w2 = lax.optimization_barrier((keep, w2))
-    keep = scale * (keep + product(w2, ours, text2))
+    keep = scale * (
+        product(w0, ours, caption) + product(w1, ours, text1) + product(w2, ours, text2)
+    )
+    w2, _ = lax.optimization_barrier((w2, keep))
     far = (keep[:width] + got[:width].astype(F32)).astype(BF)
     near = keep[width:] + got[width:].astype(F32)
     term2 = text_term(w2).astype(BF)
@@ -105,9 +106,10 @@
     w0, term1, _ = lax.optimization_barrier((w0, term1, term2))
     back1 = lax.ppermute(term1, AXES, [(j, i) for i, j in route(1)])
     other = swapped(far, 2)
+    w0, _ = lax.optimization_barrier((w0, far))
     text_grad = text_term(w0)
     x = lax.axis_index("blk") % X
-    down = handed_down(back2)
+    down = handed_down(jnp.where(x >= X - 2, back2, BF(0.0)))
     own2 = jnp.where(x >= X - 2, F32(0.0), back2.astype(F32))
 
     image_grad = near + other.astype(F32)

time: 77.9 us -> 87 us (1.12)
  the two profiles are of different devices: /device:TPU:254 before, /device:TPU:8 now
where the time goes in v8:
time: 87 us; the launch traced here: 86.7 us
  waiting for transfers between devices  39.8 us (46%)
  starting transfers between devices  32.9 us (38%)
  matrix products  6.79 us (8%)
  other arithmetic  2.52 us (3%)
  local copies, waits for them, and re-layouts  2.46 us (3%)
  between operations  2.19 us (3%)
    ppermute x2, waiting for transfers between devices, swapped(): return lax.ppermute(block, 'grp', [(i, i ^ bit) for i in range(n)])  29.3 us
    ppermute x1, starting transfers between devices, on_device(): back1 = lax.ppermute(term1, AXES, [(j, i) for i, j in route(1)])  14.7 us
    ppermute x2, waiting for transfers between devices, sent(): return lax.ppermute(block, AXES, route(distance))  10.6 us
    ppermute x2, starting transfers between devices, sent(): return lax.ppermute(block, AXES, route(distance))  8.03 us
    ppermute x2, starting transfers between devices, swapped(): return lax.ppermute(block, 'grp', [(i, i ^ bit) for i in range(n)])  6.65 us
    ppermute x1, starting transfers between devices, turned(): lax.ppermute(block, 'blk', [(b, b // X * X + (b - distance) % X) for b in...  2.82 us
    dot_general x6, matrix products, product(): return jnp.dot(w[rows], text, preferred_element_type=F32)  2.81 us
    dynamic_slice x2, local copies, waits for them, and re-layouts, ordered(): lax.dynamic_slice_in_dim(rows, (place ^ bits) * width, width, 0)  2.46 us
  transfers between devices with their start and end apart: 7, of which 3 were waited for; matrix products, arithmetic and copies ran while one was open for 11% of the time, Pallas kernels for 0%

profile of v8, /device:TPU:8, one launch (start us, length us, event | category | flops | bytes accessed | tf_op | source)
XLA Modules:
  0.0 86.7 jit_solution(13267626572918129565)
XLA Ops:
  0.6 3.4 %collective-permute-start.1 = (bf16[192,1152]{1,0:T(8,128)(2,1)}, bf16[192,1152]{1,0:T(8,128)(2,1)S(1)}, u32[]{:S(2)}, u32[]{:S(2)}) collective-permute-start(bf16[192,1152]{1,0:T(8,128)(2,1)} %param.6), channel_id=1, source_target_pairs={{0,4},{1,5},{2,6},{3,7},{4,8},{5,9},{6,10},{7,11},{8,12},{9,13},{1... | collective-permute-start | bytes 1327112 | tf_op jit(solution)/shard_map/ppermute | solution.py:24
  5.4 0.8 constant_dynamic-slice_fusion.7
  6.3 1.6 %constant_dynamic-slice_fusion.3 = (bf16[192,1152]{1,0:T(8,128)(2,1)S(1)}, bf16[192,1152]{1,0:T(8,128)(2,1)S(1)}, bf16[192,1152]{1,0:T(8,128)(2,1)S(1)}, bf16[192,1152]{1,0:T(8,128)(2,1)S(1)}) fusion(bf16[768,1152]{1,0:T(8,128)(2,1)} %param.5, s32[]{:T(128)S(6)} %select_n.41, s32[]{:T(128)S(6)} %select_n.42, s32[]{:T(128)S(6)} %select_n.44, s32[]{:T(128)S(6)} %select_n.43), kind=kLoop, calls=%fused_computation.53 | loop fusion | bytes 3538960 | tf_op jit(solution)/shard_map/dynamic_slice | solution.py:57
  8.0 0.8 fusion.22
  8.8 4.6 %collective-permute-start = (bf16[192,1152]{1,0:T(8,128)(2,1)S(1)}, bf16[192,1152]{1,0:T(8,128)(2,1)S(1)}, u32[]{:S(2)}, u32[]{:S(2)}) collective-permute-start(bf16[192,1152]{1,0:T(8,128)(2,1)S(1)} %copy-done), channel_id=1, source_target_pairs={{0,8},{1,9},{2,10},{3,11},{4,12},{5,13},{6,14},{7,15},{8,16},{9,17... | collective-permute-start | bytes 1327112 | tf_op jit(solution)/shard_map/ppermute | solution.py:24
  13.9 4.8 %collective-permute-done.1 = bf16[192,1152]{1,0:T(8,128)(2,1)S(1)} collective-permute-done((bf16[192,1152]{1,0:T(8,128)(2,1)}, bf16[192,1152]{1,0:T(8,128)(2,1)S(1)}, u32[]{:S(2)}, u32[]{:S(2)}) %collective-permute-start.1) | collective-permute-done | bytes 442400 | tf_op jit(solution)/shard_map/ppermute | solution.py:24
  18.7 0.7 fusion.21
  19.5 0.6 fusion.1
  20.0 0.5 convolution_add_fusion.2
  20.5 5.7 %collective-permute-done = bf16[192,1152]{1,0:T(8,128)(2,1)S(1)} collective-permute-done((bf16[192,1152]{1,0:T(8,128)(2,1)S(1)}, bf16[192,1152]{1,0:T(8,128)(2,1)S(1)}, u32[]{:S(2)}, u32[]{:S(2)}) %collective-permute-start) | collective-permute-done | bytes 442400 | tf_op jit(solution)/shard_map/ppermute | solution.py:24
  26.2 0.7 fusion.20
  27.0 0.5 fusion.25
  27.6 1.9 %collective-permute-start.2 = (bf16[384,1152]{1,0:T(8,128)(2,1)S(1)}, bf16[384,1152]{1,0:T(8,128)(2,1)S(1)}, u32[]{:S(2)}, u32[]{:S(2)}) collective-permute-start(bf16[384,1152]{1,0:T(8,128)(2,1)S(1)} %multiply_convert_fusion), channel_id=1, source_target_pairs={{0,1},{1,0},{2,3},{3,2},{4,5},{5,4},{6,7},{7,6},{8,9},{9,8},{10,11... | collective-permute-start | bytes 2654216 | tf_op jit(solution)/shard_map/ppermute | solution.py:44
  30.0 0.5 convolution_add_fusion.1
  30.5 0.5 fusion
  31.0 0.6 fusion.2
  31.6 2.8 %collective-permute-start.4 = (bf16[192,1152]{1,0:T(8,128)(2,1)S(1)}, bf16[192,1152]{1,0:T(8,128)(2,1)S(1)}, u32[]{:S(2)}, u32[]{:S(2)}) collective-permute-start(bf16[192,1152]{1,0:T(8,128)(2,1)S(1)} %fusion.2), channel_id=1, source_target_pairs={{0,8},{4,12},{8,0},{12,4},{16,24},{20,28},{24,16},{28,20},{32,40},... | collective-permute-start | bytes 1327112 | tf_op jit(solution)/shard_map/ppermute | solution.py:29
  34.4 14.7 %collective-permute-start.6 = (bf16[192,1152]{1,0:T(8,128)(2,1)S(1)}, bf16[192,1152]{1,0:T(8,128)(2,1)S(1)}, u32[]{:S(2)}, u32[]{:S(2)}) collective-permute-start(bf16[192,1152]{1,0:T(8,128)(2,1)S(1)} %fusion.1), channel_id=1, source_target_pairs={{4,0},{5,1},{6,2},{7,3},{8,4},{9,5},{10,6},{11,7},{12,8},{13,9},{1... | collective-permute-start | bytes 1327112 | tf_op jit(solution)/shard_map/ppermute | solution.py:107
  49.2 4.7 %collective-permute-start.3 = (bf16[192,1152]{1,0:T(8,128)(2,1)S(1)}, bf16[192,1152]{1,0:T(8,128)(2,1)S(1)}, u32[]{:S(2)}, u32[]{:S(2)}) collective-permute-start(bf16[192,1152]{1,0:T(8,128)(2,1)S(1)} %fusion.23), channel_id=1, source_target_pairs={{0,2},{1,3},{2,0},{3,1},{4,6},{5,7},{6,4},{7,5},{8,10},{9,11},{10,... | collective-permute-start | bytes 1327112 | tf_op jit(solution)/shard_map/ppermute | solution.py:44
  54.0 0.7 collective-permute-start.5
  54.7 0.6 convolution_multiply_fusion
  55.3 29.3 %collective-permute-done.3 = bf16[192,1152]{1,0:T(8,128)(2,1)S(1)} collective-permute-done((bf16[192,1152]{1,0:T(8,128)(2,1)S(1)}, bf16[192,1152]{1,0:T(8,128)(2,1)S(1)}, u32[]{:S(2)}, u32[]{:S(2)}) %collective-permute-start.3) | collective-permute-done | bytes 442400 | tf_op jit(solution)/shard_map/ppermute | solution.py:44
  84.6 1.0 %fusion.24 = f32[192,1152]{1,0:T(8,128)} fusion(f32[384,1152]{1,0:T(8,128)S(1)} %fusion, bf16[192,1152]{1,0:T(8,128)(2,1)S(1)} %collective-permute-done.3, bf16[384,1152]{1,0:T(8,128)(2,1)S(1)} %collective-permute-done.2), kind=kLoop, calls=%fused_computation.37 | loop fusion | flops 884736 | bytes 2654208 | tf_op jit(solution)/shard_map/add | solution.py:115
  85.6 1.1 %convert_add_fusion = f32[192,1152]{1,0:T(8,128)} fusion(bf16[192,1152]{1,0:T(8,128)(2,1)S(1)} %collective-permute-done.5, bf16[192,1152]{1,0:T(8,128)(2,1)S(1)} %collective-permute-done.4, f32[192,1152]{1,0:T(8,128)S(1)} %convolution_multiply_fusion, bf16[192,1152]{1,0:T(8,128)(2,1)S(1)} %collective-permute-done.6, pred[]{:T(512)S(6)} %ge.4), kind=kLoop, calls=%fused_computation.38 | loop fusion | flops 1548288 | bytes 3096577 | tf_op jit(solution)/shard_map/add | solution.py:117
  (13 shorter events, 1.3 us)
Async XLA Ops:
  0.6 18.1 %collective-permute-start.1 = (bf16[192,1152]{1,0:T(8,128)(2,1)}, bf16[192,1152]{1,0:T(8,128)(2,1)S(1)}, u32[]{:S(2)}, u32[]{:S(2)}) collective-permute-start(bf16[192,1152]{1,0:T(8,128)(2,1)} %param.6), channel_id=1, source_target_pairs={{0,4},{1,5},{2,6},{3,7},{4,8},{5,9},{6,10},{7,11},{8,12},{9,13},{1... | collective-permute-start | bytes 1327112 | tf_op jit(solution)/shard_map/ppermute | solution.py:24
  6.3 1.7 %copy-start = (bf16[192,1152]{1,0:T(8,128)(2,1)S(1)}, bf16[192,1152]{1,0:T(8,128)(2,1)}, u32[]{:S(2)}) copy-start(bf16[192,1152]{1,0:T(8,128)(2,1)} %param.6) | copy-start | bytes 1327108
  8.8 17.5 %collective-permute-start = (bf16[192,1152]{1,0:T(8,128)(2,1)S(1)}, bf16[192,1152]{1,0:T(8,128)(2,1)S(1)}, u32[]{:S(2)}, u32[]{:S(2)}) collective-permute-start(bf16[192,1152]{1,0:T(8,128)(2,1)S(1)} %copy-done), channel_id=1, source_target_pairs={{0,8},{1,9},{2,10},{3,11},{4,12},{5,13},{6,14},{7,15},{8,16},{9,17... | collective-permute-start | bytes 1327112 | tf_op jit(solution)/shard_map/ppermute | solution.py:24
  27.6 21.5 %collective-permute-start.2 = (bf16[384,1152]{1,0:T(8,128)(2,1)S(1)}, bf16[384,1152]{1,0:T(8,128)(2,1)S(1)}, u32[]{:S(2)}, u32[]{:S(2)}) collective-permute-start(bf16[384,1152]{1,0:T(8,128)(2,1)S(1)} %multiply_convert_fusion), channel_id=1, source_target_pairs={{0,1},{1,0},{2,3},{3,2},{4,5},{5,4},{6,7},{7,6},{8,9},{9,8},{10,11... | collective-permute-start | bytes 2654216 | tf_op jit(solution)/shard_map/ppermute | solution.py:44
  31.6 22.4 %collective-permute-start.4 = (bf16[192,1152]{1,0:T(8,128)(2,1)S(1)}, bf16[192,1152]{1,0:T(8,128)(2,1)S(1)}, u32[]{:S(2)}, u32[]{:S(2)}) collective-permute-start(bf16[192,1152]{1,0:T(8,128)(2,1)S(1)} %fusion.2), channel_id=1, source_target_pairs={{0,8},{4,12},{8,0},{12,4},{16,24},{20,28},{24,16},{28,20},{32,40},... | collective-permute-start | bytes 1327112 | tf_op jit(solution)/shard_map/ppermute | solution.py:29
  34.4 51.2 %collective-permute-start.6 = (bf16[192,1152]{1,0:T(8,128)(2,1)S(1)}, bf16[192,1152]{1,0:T(8,128)(2,1)S(1)}, u32[]{:S(2)}, u32[]{:S(2)}) collective-permute-start(bf16[192,1152]{1,0:T(8,128)(2,1)S(1)} %fusion.1), channel_id=1, source_target_pairs={{4,0},{5,1},{6,2},{7,3},{8,4},{9,5},{10,6},{11,7},{12,8},{13,9},{1... | collective-permute-start | bytes 1327112 | tf_op jit(solution)/shard_map/ppermute | solution.py:107
  49.2 35.4 %collective-permute-start.3 = (bf16[192,1152]{1,0:T(8,128)(2,1)S(1)}, bf16[192,1152]{1,0:T(8,128)(2,1)S(1)}, u32[]{:S(2)}, u32[]{:S(2)}) collective-permute-start(bf16[192,1152]{1,0:T(8,128)(2,1)S(1)} %fusion.23), channel_id=1, source_target_pairs={{0,2},{1,3},{2,0},{3,1},{4,6},{5,7},{6,4},{7,5},{8,10},{9,11},{10,... | collective-permute-start | bytes 1327112 | tf_op jit(solution)/shard_map/ppermute | solution.py:44
  54.0 31.6 %collective-permute-start.5 = (bf16[192,1152]{1,0:T(8,128)(2,1)S(1)}, bf16[192,1152]{1,0:T(8,128)(2,1)S(1)}, u32[]{:S(2)}, u32[]{:S(2)}) collective-permute-start(bf16[192,1152]{1,0:T(8,128)(2,1)S(1)} %broadcast_select_fusion), channel_id=1, source_target_pairs={{24,8},{25,9},{26,10},{27,11},{28,12},{29,13},{30,14},{31,15},{40,... | collective-permute-start | bytes 1327112 | tf_op jit(solution)/shard_map/ppermute | solution.py:39

commit v9 on v8

--- a/solution.py
+++ b/solution.py
@@ -103,13 +103,14 @@
     near = keep[width:] + got[width:].astype(F32)
     term2 = text_term(w2).astype(BF)
     back2 = turned(term2, 2)
-    w0, term1, _ = lax.optimization_barrier((w0, term1, term2))
-    back1 = lax.ppermute(term1, AXES, [(j, i) for i, j in route(1)])
     other = swapped(far, 2)
     w0, _ = lax.optimization_barrier((w0, far))
     text_grad = text_term(w0)
     x = lax.axis_index("blk") % X
-    down = handed_down(jnp.where(x >= X - 2, back2, BF(0.0)))
+    going = jnp.where(x >= X - 2, back2, BF(0.0))
+    down = handed_down(going)
+    term1, _ = lax.optimization_barrier((term1, going))
+    back1 = lax.ppermute(term1, AXES, [(j, i) for i, j in route(1)])
     own2 = jnp.where(x >= X - 2, F32(0.0), back2.astype(F32))
 
     image_grad = near + other.astype(F32)

time: 87 us -> 78.1 us (0.90)
  the two profiles are of different devices: /device:TPU:8 before, /device:TPU:6 now
where the time goes in v9:
time: 78.1 us; the launch traced here: 77.8 us
  starting transfers between devices  37.4 us (48%)
  waiting for transfers between devices  26.4 us (34%)
  matrix products  6.8 us (9%)
  other arithmetic  2.52 us (3%)
  local copies, waits for them, and re-layouts  2.46 us (3%)
  between operations  2.18 us (3%)
    ppermute x1, starting transfers between devices, turned(): lax.ppermute(block, 'blk', [(b, b // X * X + (b - distance) % X) for b in...  15.4 us
    ppermute x2, waiting for transfers between devices, sent(): return lax.ppermute(block, AXES, route(distance))  8.39 us
    ppermute x2, starting transfers between devices, sent(): return lax.ppermute(block, AXES, route(distance))  7.73 us
    ppermute x2, starting transfers between devices, swapped(): return lax.ppermute(block, 'grp', [(i, i ^ bit) for i in range(n)])  6.65 us
    ppermute x1, waiting for transfers between devices, turned(): lax.ppermute(block, 'blk', [(b, b // X * X + (b - distance) % X) for b in...  6.01 us
    ppermute x1, starting transfers between devices, handed_down(): return lax.ppermute(block, AXES, [(j, i) for i, j in crossing])  5.7 us
    ppermute x1, waiting for transfers between devices, handed_down(): return lax.ppermute(block, AXES, [(j, i) for i, j in crossing])  5.34 us
    ppermute x1, waiting for transfers between devices, on_device(): back1 = lax.ppermute(term1, AXES, [(j, i) for i, j in route(1)])  4.69 us
  transfers between devices with their start and end apart: 7, of which 6 were waited for; matrix products, arithmetic and copies ran while one was open for 12% of the time, Pallas kernels for 0%

profile of v9, /device:TPU:6, one launch (start us, length us, event | category | flops | bytes accessed | tf_op | source)
XLA Modules:
  0.0 77.8 jit_solution(16387783466247585426)
XLA Ops:
  0.6 3.4 %collective-permute-start.1 = (bf16[192,1152]{1,0:T(8,128)(2,1)}, bf16[192,1152]{1,0:T(8,128)(2,1)S(1)}, u32[]{:S(2)}, u32[]{:S(2)}) collective-permute-start(bf16[192,1152]{1,0:T(8,128)(2,1)} %param.6), channel_id=1, source_target_pairs={{0,4},{1,5},{2,6},{3,7},{4,8},{5,9},{6,10},{7,11},{8,12},{9,13},{1... | collective-permute-start | bytes 1327112 | tf_op jit(solution)/shard_map/ppermute | solution.py:24
  5.4 0.8 %constant_dynamic-slice_fusion.7 = (s32[1,192]{1,0:T(1,128)S(1)}, s32[1,192]{1,0:T(1,128)S(1)}, s32[1,192]{1,0:T(1,128)S(1)}, s32[1,192]{1,0:T(1,128)S(1)}) fusion(s32[1,768]{1,0:T(1,128)} %param.7, s32[]{:T(128)S(6)} %select_n.41, s32[]{:T(128)S(6)} %select_n.42, s32[]{:T(128)S(6)} %select_n.44, s32[]{:T(128)S(6)} %select_n.43), kind=kLoop, calls=%fused_computation.57 | loop fusion | bytes 6160 | tf_op jit(solution)/shard_map/dynamic_slice | solution.py:57
  6.3 1.6 %constant_dynamic-slice_fusion.3 = (bf16[192,1152]{1,0:T(8,128)(2,1)S(1)}, bf16[192,1152]{1,0:T(8,128)(2,1)S(1)}, bf16[192,1152]{1,0:T(8,128)(2,1)S(1)}, bf16[192,1152]{1,0:T(8,128)(2,1)S(1)}) fusion(bf16[768,1152]{1,0:T(8,128)(2,1)} %param.5, s32[]{:T(128)S(6)} %select_n.41, s32[]{:T(128)S(6)} %select_n.42, s32[]{:T(128)S(6)} %select_n.44, s32[]{:T(128)S(6)} %select_n.43), kind=kLoop, calls=%fused_computation.53 | loop fusion | bytes 3538960 | tf_op jit(solution)/shard_map/dynamic_slice | solution.py:57
  8.0 0.8 %fusion.22 = bf16[768,192]{0,1:T(8,128)(2,1)S(1)} fusion(bf16[192,1152]{1,0:T(8,128)(2,1)S(1)} %copy-done, f32[]{:T(128)} %bitcast.18, f32[]{:T(128)} %bitcast, s32[768]{0:T(1024)S(1)} %pad_add_fusion, s32[192]{0:T(256)S(1)} %iota_add_fusion, bf16[192,1152]{1,0:T(8,128)(2,1)S(1)} %get-tuple-element.34, bf16[192,1152]{1,0:T(8,128)(2,1)S(1)} %get-tuple-element.35, ...), kind=kOutput, calls=%fused_computation.33 | convolution fusion | flops 348438528 | bytes 2510600 | tf_op jit(solution)/shard_map/dot_general | solution.py:70
  8.8 4.3 %collective-permute-start = (bf16[192,1152]{1,0:T(8,128)(2,1)S(1)}, bf16[192,1152]{1,0:T(8,128)(2,1)S(1)}, u32[]{:S(2)}, u32[]{:S(2)}) collective-permute-start(bf16[192,1152]{1,0:T(8,128)(2,1)S(1)} %copy-done), channel_id=1, source_target_pairs={{0,8},{1,9},{2,10},{3,11},{4,12},{5,13},{6,14},{7,15},{8,16},{9,17... | collective-permute-start | bytes 1327112 | tf_op jit(solution)/shard_map/ppermute | solution.py:24
  13.6 1.1 %collective-permute-done.1 = bf16[192,1152]{1,0:T(8,128)(2,1)S(1)} collective-permute-done((bf16[192,1152]{1,0:T(8,128)(2,1)}, bf16[192,1152]{1,0:T(8,128)(2,1)S(1)}, u32[]{:S(2)}, u32[]{:S(2)}) %collective-permute-start.1) | collective-permute-done | bytes 442400 | tf_op jit(solution)/shard_map/ppermute | solution.py:24
  14.6 0.7 fusion.21
  15.4 0.6 fusion.1
  16.0 0.5 convolution_add_fusion.2
  16.4 7.3 %collective-permute-done = bf16[192,1152]{1,0:T(8,128)(2,1)S(1)} collective-permute-done((bf16[192,1152]{1,0:T(8,128)(2,1)S(1)}, bf16[192,1152]{1,0:T(8,128)(2,1)S(1)}, u32[]{:S(2)}, u32[]{:S(2)}) %collective-permute-start) | collective-permute-done | bytes 442400 | tf_op jit(solution)/shard_map/ppermute | solution.py:24
  23.8 0.7 fusion.20
  25.2 1.9 %collective-permute-start.2 = (bf16[384,1152]{1,0:T(8,128)(2,1)S(1)}, bf16[384,1152]{1,0:T(8,128)(2,1)S(1)}, u32[]{:S(2)}, u32[]{:S(2)}) collective-permute-start(bf16[384,1152]{1,0:T(8,128)(2,1)S(1)} %multiply_convert_fusion), channel_id=1, source_target_pairs={{0,1},{1,0},{2,3},{3,2},{4,5},{5,4},{6,7},{7,6},{8,9},{9,8},{10,11... | collective-permute-start | bytes 2654216 | tf_op jit(solution)/shard_map/ppermute | solution.py:44
  28.5 0.6 fusion.2
  29.1 15.4 %collective-permute-start.4 = (bf16[192,1152]{1,0:T(8,128)(2,1)S(1)}, bf16[192,1152]{1,0:T(8,128)(2,1)S(1)}, u32[]{:S(2)}, u32[]{:S(2)}) collective-permute-start(bf16[192,1152]{1,0:T(8,128)(2,1)S(1)} %fusion.2), channel_id=1, source_target_pairs={{0,8},{4,12},{8,0},{12,4},{16,24},{20,28},{24,16},{28,20},{32,40},... | collective-permute-start | bytes 1327112 | tf_op jit(solution)/shard_map/ppermute | solution.py:29
  44.6 4.7 %collective-permute-start.3 = (bf16[192,1152]{1,0:T(8,128)(2,1)S(1)}, bf16[192,1152]{1,0:T(8,128)(2,1)S(1)}, u32[]{:S(2)}, u32[]{:S(2)}) collective-permute-start(bf16[192,1152]{1,0:T(8,128)(2,1)S(1)} %fusion.23), channel_id=1, source_target_pairs={{0,2},{1,3},{2,0},{3,1},{4,6},{5,7},{6,4},{7,5},{8,10},{9,11},{10,... | collective-permute-start | bytes 1327112 | tf_op jit(solution)/shard_map/ppermute | solution.py:44
  49.4 6.0 %collective-permute-done.4 = bf16[192,1152]{1,0:T(8,128)(2,1)S(1)} collective-permute-done((bf16[192,1152]{1,0:T(8,128)(2,1)S(1)}, bf16[192,1152]{1,0:T(8,128)(2,1)S(1)}, u32[]{:S(2)}, u32[]{:S(2)}) %collective-permute-start.4) | collective-permute-done | bytes 442400 | tf_op jit(solution)/shard_map/ppermute | solution.py:29
  55.4 5.7 %collective-permute-start.5 = (bf16[192,1152]{1,0:T(8,128)(2,1)S(1)}, bf16[192,1152]{1,0:T(8,128)(2,1)S(1)}, u32[]{:S(2)}, u32[]{:S(2)}) collective-permute-start(bf16[192,1152]{1,0:T(8,128)(2,1)S(1)} %broadcast_select_fusion), channel_id=1, source_target_pairs={{24,8},{25,9},{26,10},{27,11},{28,12},{29,13},{30,14},{31,15},{40,... | collective-permute-start | bytes 1327112 | tf_op jit(solution)/shard_map/ppermute | solution.py:39
  61.1 1.9 %collective-permute-start.6 = (bf16[192,1152]{1,0:T(8,128)(2,1)S(1)}, bf16[192,1152]{1,0:T(8,128)(2,1)S(1)}, u32[]{:S(2)}, u32[]{:S(2)}) collective-permute-start(bf16[192,1152]{1,0:T(8,128)(2,1)S(1)} %fusion.1), channel_id=1, source_target_pairs={{4,0},{5,1},{6,2},{7,3},{8,4},{9,5},{10,6},{11,7},{12,8},{13,9},{1... | collective-permute-start | bytes 1327112 | tf_op jit(solution)/shard_map/ppermute | solution.py:113
  63.1 0.6 convolution_multiply_fusion
  63.6 2.0 %collective-permute-done.3 = bf16[192,1152]{1,0:T(8,128)(2,1)S(1)} collective-permute-done((bf16[192,1152]{1,0:T(8,128)(2,1)S(1)}, bf16[192,1152]{1,0:T(8,128)(2,1)S(1)}, u32[]{:S(2)}, u32[]{:S(2)}) %collective-permute-start.3) | collective-permute-done | bytes 442400 | tf_op jit(solution)/shard_map/ppermute | solution.py:44
  65.6 1.0 %fusion.24 = f32[192,1152]{1,0:T(8,128)} fusion(f32[384,1152]{1,0:T(8,128)S(1)} %fusion, bf16[192,1152]{1,0:T(8,128)(2,1)S(1)} %collective-permute-done.3, bf16[384,1152]{1,0:T(8,128)(2,1)S(1)} %collective-permute-done.2), kind=kLoop, calls=%fused_computation.37 | loop fusion | flops 884736 | bytes 2654208 | tf_op jit(solution)/shard_map/add | solution.py:116
  66.6 5.3 %collective-permute-done.5 = bf16[192,1152]{1,0:T(8,128)(2,1)S(1)} collective-permute-done((bf16[192,1152]{1,0:T(8,128)(2,1)S(1)}, bf16[192,1152]{1,0:T(8,128)(2,1)S(1)}, u32[]{:S(2)}, u32[]{:S(2)}) %collective-permute-start.5) | collective-permute-done | bytes 442400 | tf_op jit(solution)/shard_map/ppermute | solution.py:39
  72.0 4.7 %collective-permute-done.6 = bf16[192,1152]{1,0:T(8,128)(2,1)S(1)} collective-permute-done((bf16[192,1152]{1,0:T(8,128)(2,1)S(1)}, bf16[192,1152]{1,0:T(8,128)(2,1)S(1)}, u32[]{:S(2)}, u32[]{:S(2)}) %collective-permute-start.6) | collective-permute-done | bytes 442400 | tf_op jit(solution)/shard_map/ppermute | solution.py:113
  76.7 1.1 %convert_add_fusion = f32[192,1152]{1,0:T(8,128)} fusion(bf16[192,1152]{1,0:T(8,128)(2,1)S(1)} %collective-permute-done.5, bf16[192,1152]{1,0:T(8,128)(2,1)S(1)} %collective-permute-done.4, f32[192,1152]{1,0:T(8,128)S(1)} %convolution_multiply_fusion, bf16[192,1152]{1,0:T(8,128)(2,1)S(1)} %collective-permute-done.6, pred[]{:T(512)S(6)} %ge.4), kind=kLoop, calls=%fused_computation.38 | loop fusion | flops 1548288 | bytes 3096577 | tf_op jit(solution)/shard_map/add | solution.py:118
  (13 shorter events, 2.7 us)
Async XLA Ops:
  0.6 14.0 %collective-permute-start.1 = (bf16[192,1152]{1,0:T(8,128)(2,1)}, bf16[192,1152]{1,0:T(8,128)(2,1)S(1)}, u32[]{:S(2)}, u32[]{:S(2)}) collective-permute-start(bf16[192,1152]{1,0:T(8,128)(2,1)} %param.6), channel_id=1, source_target_pairs={{0,4},{1,5},{2,6},{3,7},{4,8},{5,9},{6,10},{7,11},{8,12},{9,13},{1... | collective-permute-start | bytes 1327112 | tf_op jit(solution)/shard_map/ppermute | solution.py:24
  6.3 1.7 %copy-start = (bf16[192,1152]{1,0:T(8,128)(2,1)S(1)}, bf16[192,1152]{1,0:T(8,128)(2,1)}, u32[]{:S(2)}) copy-start(bf16[192,1152]{1,0:T(8,128)(2,1)} %param.6) | copy-start | bytes 1327108
  8.8 15.0 %collective-permute-start = (bf16[192,1152]{1,0:T(8,128)(2,1)S(1)}, bf16[192,1152]{1,0:T(8,128)(2,1)S(1)}, u32[]{:S(2)}, u32[]{:S(2)}) collective-permute-start(bf16[192,1152]{1,0:T(8,128)(2,1)S(1)} %copy-done), channel_id=1, source_target_pairs={{0,8},{1,9},{2,10},{3,11},{4,12},{5,13},{6,14},{7,15},{8,16},{9,17... | collective-permute-start | bytes 1327112 | tf_op jit(solution)/shard_map/ppermute | solution.py:24
  25.2 19.4 %collective-permute-start.2 = (bf16[384,1152]{1,0:T(8,128)(2,1)S(1)}, bf16[384,1152]{1,0:T(8,128)(2,1)S(1)}, u32[]{:S(2)}, u32[]{:S(2)}) collective-permute-start(bf16[384,1152]{1,0:T(8,128)(2,1)S(1)} %multiply_convert_fusion), channel_id=1, source_target_pairs={{0,1},{1,0},{2,3},{3,2},{4,5},{5,4},{6,7},{7,6},{8,9},{9,8},{10,11... | collective-permute-start | bytes 2654216 | tf_op jit(solution)/shard_map/ppermute | solution.py:44
  29.1 26.3 %collective-permute-start.4 = (bf16[192,1152]{1,0:T(8,128)(2,1)S(1)}, bf16[192,1152]{1,0:T(8,128)(2,1)S(1)}, u32[]{:S(2)}, u32[]{:S(2)}) collective-permute-start(bf16[192,1152]{1,0:T(8,128)(2,1)S(1)} %fusion.2), channel_id=1, source_target_pairs={{0,8},{4,12},{8,0},{12,4},{16,24},{20,28},{24,16},{28,20},{32,40},... | collective-permute-start | bytes 1327112 | tf_op jit(solution)/shard_map/ppermute | solution.py:29
  44.6 21.0 %collective-permute-start.3 = (bf16[192,1152]{1,0:T(8,128)(2,1)S(1)}, bf16[192,1152]{1,0:T(8,128)(2,1)S(1)}, u32[]{:S(2)}, u32[]{:S(2)}) collective-permute-start(bf16[192,1152]{1,0:T(8,128)(2,1)S(1)} %fusion.23), channel_id=1, source_target_pairs={{0,2},{1,3},{2,0},{3,1},{4,6},{5,7},{6,4},{7,5},{8,10},{9,11},{10,... | collective-permute-start | bytes 1327112 | tf_op jit(solution)/shard_map/ppermute | solution.py:44
  55.4 16.5 %collective-permute-start.5 = (bf16[192,1152]{1,0:T(8,128)(2,1)S(1)}, bf16[192,1152]{1,0:T(8,128)(2,1)S(1)}, u32[]{:S(2)}, u32[]{:S(2)}) collective-permute-start(bf16[192,1152]{1,0:T(8,128)(2,1)S(1)} %broadcast_select_fusion), channel_id=1, source_target_pairs={{24,8},{25,9},{26,10},{27,11},{28,12},{29,13},{30,14},{31,15},{40,... | collective-permute-start | bytes 1327112 | tf_op jit(solution)/shard_map/ppermute | solution.py:39
  61.1 15.5 %collective-permute-start.6 = (bf16[192,1152]{1,0:T(8,128)(2,1)S(1)}, bf16[192,1152]{1,0:T(8,128)(2,1)S(1)}, u32[]{:S(2)}, u32[]{:S(2)}) collective-permute-start(bf16[192,1152]{1,0:T(8,128)(2,1)S(1)} %fusion.1), channel_id=1, source_target_pairs={{4,0},{5,1},{6,2},{7,3},{8,4},{9,5},{10,6},{11,7},{12,8},{13,9},{1... | collective-permute-start | bytes 1327112 | tf_op jit(solution)/shard_map/ppermute | solution.py:113

commit v10 on v9

--- a/solution.py
+++ b/solution.py
@@ -92,17 +92,17 @@
     early = product(w0, theirs, caption) + product(w1, theirs, text1)
     text2, term1, early = lax.optimization_barrier((text2, term1, early))
     w2 = weight(text2, F32(-1.0))
+    term2 = text_term(w2).astype(BF)
+    back2 = turned(term2, 2)
+    w2, _ = lax.optimization_barrier((w2, term2))
     give = (scale * (early + product(w2, theirs, text2))).astype(BF)
     give, w0, w1, w2, term1 = lax.optimization_barrier((give, w0, w1, w2, term1))
     got = swapped(give, 1)
     keep = scale * (
         product(w0, ours, caption) + product(w1, ours, text1) + product(w2, ours, text2)
     )
-    w2, _ = lax.optimization_barrier((w2, keep))
     far = (keep[:width] + got[:width].astype(F32)).astype(BF)
     near = keep[width:] + got[width:].astype(F32)
-    term2 = text_term(w2).astype(BF)
-    back2 = turned(term2, 2)
     other = swapped(far, 2)
     w0, _ = lax.optimization_barrier((w0, far))
     text_grad = text_term(w0)

time: 78.1 us -> 76.8 us (0.983)
  the two profiles are of different devices: /device:TPU:6 before, /device:TPU:254 now
where the time goes in v10:
time: 76.8 us; the launch traced here: 76.3 us
  waiting for transfers between devices  37.6 us (49%)
  starting transfers between devices  24.6 us (32%)
  matrix products  6.8 us (9%)
  other arithmetic  2.54 us (3%)
  local copies, waits for them, and re-layouts  2.46 us (3%)
  between operations  2.19 us (3%)
    ppermute x2, waiting for transfers between devices, swapped(): return lax.ppermute(block, 'grp', [(i, i ^ bit) for i in range(n)])  17.4 us
    ppermute x1, waiting for transfers between devices, handed_down(): return lax.ppermute(block, AXES, [(j, i) for i, j in crossing])  10.8 us
    ppermute x2, waiting for transfers between devices, sent(): return lax.ppermute(block, AXES, route(distance))  9.34 us
    ppermute x2, starting transfers between devices, sent(): return lax.ppermute(block, AXES, route(distance))  8.94 us
    ppermute x2, starting transfers between devices, swapped(): return lax.ppermute(block, 'grp', [(i, i ^ bit) for i in range(n)])  7.65 us
    ppermute x1, starting transfers between devices, on_device(): back1 = lax.ppermute(term1, AXES, [(j, i) for i, j in route(1)])  3.08 us
    ppermute x1, starting transfers between devices, turned(): lax.ppermute(block, 'blk', [(b, b // X * X + (b - distance) % X) for b in...  2.96 us
    dot_general x6, matrix products, product(): return jnp.dot(w[rows], text, preferred_element_type=F32)  2.81 us
  transfers between devices with their start and end apart: 7, of which 5 were waited for; matrix products, arithmetic and copies ran while one was open for 12% of the time, Pallas kernels for 0%

profile of v10, /device:TPU:254, one launch (start us, length us, event | category | flops | bytes accessed | tf_op | source)
XLA Modules:
  0.0 76.3 jit_solution(11701489795938622525)
XLA Ops:
  0.6 4.6 %collective-permute-start.1 = (bf16[192,1152]{1,0:T(8,128)(2,1)}, bf16[192,1152]{1,0:T(8,128)(2,1)S(1)}, u32[]{:S(2)}, u32[]{:S(2)}) collective-permute-start(bf16[192,1152]{1,0:T(8,128)(2,1)} %param.6), channel_id=1, source_target_pairs={{0,4},{1,5},{2,6},{3,7},{4,8},{5,9},{6,10},{7,11},{8,12},{9,13},{1... | collective-permute-start | bytes 1327112 | tf_op jit(solution)/shard_map/ppermute | solution.py:24
  5.3 0.8 %constant_dynamic-slice_fusion.7 = (s32[1,192]{1,0:T(1,128)S(1)}, s32[1,192]{1,0:T(1,128)S(1)}, s32[1,192]{1,0:T(1,128)S(1)}, s32[1,192]{1,0:T(1,128)S(1)}) fusion(s32[1,768]{1,0:T(1,128)} %param.7, s32[]{:T(128)S(6)} %select_n.41, s32[]{:T(128)S(6)} %select_n.42, s32[]{:T(128)S(6)} %select_n.44, s32[]{:T(128)S(6)} %select_n.43), kind=kLoop, calls=%fused_computation.57 | loop fusion | bytes 6160 | tf_op jit(solution)/shard_map/dynamic_slice | solution.py:57
  6.2 1.6 %constant_dynamic-slice_fusion.3 = (bf16[192,1152]{1,0:T(8,128)(2,1)S(1)}, bf16[192,1152]{1,0:T(8,128)(2,1)S(1)}, bf16[192,1152]{1,0:T(8,128)(2,1)S(1)}, bf16[192,1152]{1,0:T(8,128)(2,1)S(1)}) fusion(bf16[768,1152]{1,0:T(8,128)(2,1)} %param.5, s32[]{:T(128)S(6)} %select_n.41, s32[]{:T(128)S(6)} %select_n.42, s32[]{:T(128)S(6)} %select_n.44, s32[]{:T(128)S(6)} %select_n.43), kind=kLoop, calls=%fused_computation.53 | loop fusion | bytes 3538960 | tf_op jit(solution)/shard_map/dynamic_slice | solution.py:57
  9.2 0.8 %fusion.22 = bf16[768,192]{0,1:T(8,128)(2,1)S(1)} fusion(bf16[192,1152]{1,0:T(8,128)(2,1)S(1)} %copy-done, f32[]{:T(128)} %bitcast.18, f32[]{:T(128)} %bitcast, s32[768]{0:T(1024)S(1)} %pad_add_fusion, s32[192]{0:T(256)S(1)} %iota_add_fusion, bf16[192,1152]{1,0:T(8,128)(2,1)S(1)} %get-tuple-element.34, bf16[192,1152]{1,0:T(8,128)(2,1)S(1)} %get-tuple-element.35, ...), kind=kOutput, calls=%fused_computation.33 | convolution fusion | flops 348438528 | bytes 2510600 | tf_op jit(solution)/shard_map/dot_general | solution.py:70
  10.0 4.3 %collective-permute-start = (bf16[192,1152]{1,0:T(8,128)(2,1)S(1)}, bf16[192,1152]{1,0:T(8,128)(2,1)S(1)}, u32[]{:S(2)}, u32[]{:S(2)}) collective-permute-start(bf16[192,1152]{1,0:T(8,128)(2,1)S(1)} %copy-done), channel_id=1, source_target_pairs={{0,8},{1,9},{2,10},{3,11},{4,12},{5,13},{6,14},{7,15},{8,16},{9,17... | collective-permute-start | bytes 1327112 | tf_op jit(solution)/shard_map/ppermute | solution.py:24
  14.3 0.5 fusion.32
  14.8 9.3 %collective-permute-done.1 = bf16[192,1152]{1,0:T(8,128)(2,1)S(1)} collective-permute-done((bf16[192,1152]{1,0:T(8,128)(2,1)}, bf16[192,1152]{1,0:T(8,128)(2,1)S(1)}, u32[]{:S(2)}, u32[]{:S(2)}) %collective-permute-start.1) | collective-permute-done | bytes 442400 | tf_op jit(solution)/shard_map/ppermute | solution.py:24
  24.1 0.7 fusion.21
  24.9 0.6 fusion.1
  25.5 0.5 convolution_add_fusion.2
  25.9 0.7 fusion.20
  26.7 0.6 fusion.2
  27.3 3.0 %collective-permute-start.4 = (bf16[192,1152]{1,0:T(8,128)(2,1)S(1)}, bf16[192,1152]{1,0:T(8,128)(2,1)S(1)}, u32[]{:S(2)}, u32[]{:S(2)}) collective-permute-start(bf16[192,1152]{1,0:T(8,128)(2,1)S(1)} %fusion.2), channel_id=1, source_target_pairs={{0,8},{4,12},{8,0},{12,4},{16,24},{20,28},{24,16},{28,20},{32,40},... | collective-permute-start | bytes 1327112 | tf_op jit(solution)/shard_map/ppermute | solution.py:29
  30.2 0.5 fusion.30
  30.9 1.9 %collective-permute-start.2 = (bf16[384,1152]{1,0:T(8,128)(2,1)S(1)}, bf16[384,1152]{1,0:T(8,128)(2,1)S(1)}, u32[]{:S(2)}, u32[]{:S(2)}) collective-permute-start(bf16[384,1152]{1,0:T(8,128)(2,1)S(1)} %multiply_convert_fusion), channel_id=1, source_target_pairs={{0,1},{1,0},{2,3},{3,2},{4,5},{5,4},{6,7},{7,6},{8,9},{9,8},{10,11... | collective-permute-start | bytes 2654216 | tf_op jit(solution)/shard_map/ppermute | solution.py:44
  34.2 1.0 %collective-permute-done.2 = bf16[384,1152]{1,0:T(8,128)(2,1)S(1)} collective-permute-done((bf16[384,1152]{1,0:T(8,128)(2,1)S(1)}, bf16[384,1152]{1,0:T(8,128)(2,1)S(1)}, u32[]{:S(2)}, u32[]{:S(2)}) %collective-permute-start.2) | collective-permute-done | bytes 884768 | tf_op jit(solution)/shard_map/ppermute | solution.py:44
  35.3 5.7 %collective-permute-start.3 = (bf16[192,1152]{1,0:T(8,128)(2,1)S(1)}, bf16[192,1152]{1,0:T(8,128)(2,1)S(1)}, u32[]{:S(2)}, u32[]{:S(2)}) collective-permute-start(bf16[192,1152]{1,0:T(8,128)(2,1)S(1)} %fusion.23), channel_id=1, source_target_pairs={{0,2},{1,3},{2,0},{3,1},{4,6},{5,7},{6,4},{7,5},{8,10},{9,11},{10,... | collective-permute-start | bytes 1327112 | tf_op jit(solution)/shard_map/ppermute | solution.py:44
  41.1 2.0 %collective-permute-start.5 = (bf16[192,1152]{1,0:T(8,128)(2,1)S(1)}, bf16[192,1152]{1,0:T(8,128)(2,1)S(1)}, u32[]{:S(2)}, u32[]{:S(2)}) collective-permute-start(bf16[192,1152]{1,0:T(8,128)(2,1)S(1)} %broadcast_select_fusion), channel_id=1, source_target_pairs={{24,8},{25,9},{26,10},{27,11},{28,12},{29,13},{30,14},{31,15},{40,... | collective-permute-start | bytes 1327112 | tf_op jit(solution)/shard_map/ppermute | solution.py:39
  43.1 3.1 %collective-permute-start.6 = (bf16[192,1152]{1,0:T(8,128)(2,1)S(1)}, bf16[192,1152]{1,0:T(8,128)(2,1)S(1)}, u32[]{:S(2)}, u32[]{:S(2)}) collective-permute-start(bf16[192,1152]{1,0:T(8,128)(2,1)S(1)} %fusion.1), channel_id=1, source_target_pairs={{4,0},{5,1},{6,2},{7,3},{8,4},{9,5},{10,6},{11,7},{12,8},{13,9},{1... | collective-permute-start | bytes 1327112 | tf_op jit(solution)/shard_map/ppermute | solution.py:113
  46.2 0.6 convolution_multiply_fusion
  46.8 16.4 %collective-permute-done.3 = bf16[192,1152]{1,0:T(8,128)(2,1)S(1)} collective-permute-done((bf16[192,1152]{1,0:T(8,128)(2,1)S(1)}, bf16[192,1152]{1,0:T(8,128)(2,1)S(1)}, u32[]{:S(2)}, u32[]{:S(2)}) %collective-permute-start.3) | collective-permute-done | bytes 442400 | tf_op jit(solution)/shard_map/ppermute | solution.py:44
  63.2 1.0 %fusion.24 = f32[192,1152]{1,0:T(8,128)} fusion(f32[384,1152]{1,0:T(8,128)S(1)} %fusion, bf16[192,1152]{1,0:T(8,128)(2,1)S(1)} %collective-permute-done.3, bf16[384,1152]{1,0:T(8,128)(2,1)S(1)} %collective-permute-done.2), kind=kLoop, calls=%fused_computation.37 | loop fusion | flops 884736 | bytes 2654208 | tf_op jit(solution)/shard_map/add | solution.py:116
  64.2 10.8 %collective-permute-done.5 = bf16[192,1152]{1,0:T(8,128)(2,1)S(1)} collective-permute-done((bf16[192,1152]{1,0:T(8,128)(2,1)S(1)}, bf16[192,1152]{1,0:T(8,128)(2,1)S(1)}, u32[]{:S(2)}, u32[]{:S(2)}) %collective-permute-start.5) | collective-permute-done | bytes 442400 | tf_op jit(solution)/shard_map/ppermute | solution.py:39
  75.1 1.1 %convert_add_fusion = f32[192,1152]{1,0:T(8,128)} fusion(bf16[192,1152]{1,0:T(8,128)(2,1)S(1)} %collective-permute-done.5, bf16[192,1152]{1,0:T(8,128)(2,1)S(1)} %collective-permute-done.4, f32[192,1152]{1,0:T(8,128)S(1)} %convolution_multiply_fusion, bf16[192,1152]{1,0:T(8,128)(2,1)S(1)} %collective-permute-done.6, pred[]{:T(512)S(6)} %ge.4), kind=kLoop, calls=%fused_computation.38 | loop fusion | flops 1548288 | bytes 3096577 | tf_op jit(solution)/shard_map/add | solution.py:118
  (13 shorter events, 1.8 us)
Async XLA Ops:
  0.6 23.5 %collective-permute-start.1 = (bf16[192,1152]{1,0:T(8,128)(2,1)}, bf16[192,1152]{1,0:T(8,128)(2,1)S(1)}, u32[]{:S(2)}, u32[]{:S(2)}) collective-permute-start(bf16[192,1152]{1,0:T(8,128)(2,1)} %param.6), channel_id=1, source_target_pairs={{0,4},{1,5},{2,6},{3,7},{4,8},{5,9},{6,10},{7,11},{8,12},{9,13},{1... | collective-permute-start | bytes 1327112 | tf_op jit(solution)/shard_map/ppermute | solution.py:24
  6.1 3.0 %copy-start = (bf16[192,1152]{1,0:T(8,128)(2,1)S(1)}, bf16[192,1152]{1,0:T(8,128)(2,1)}, u32[]{:S(2)}) copy-start(bf16[192,1152]{1,0:T(8,128)(2,1)} %param.6) | copy-start | bytes 1327108
  10.0 16.0 %collective-permute-start = (bf16[192,1152]{1,0:T(8,128)(2,1)S(1)}, bf16[192,1152]{1,0:T(8,128)(2,1)S(1)}, u32[]{:S(2)}, u32[]{:S(2)}) collective-permute-start(bf16[192,1152]{1,0:T(8,128)(2,1)S(1)} %copy-done), channel_id=1, source_target_pairs={{0,8},{1,9},{2,10},{3,11},{4,12},{5,13},{6,14},{7,15},{8,16},{9,17... | collective-permute-start | bytes 1327112 | tf_op jit(solution)/shard_map/ppermute | solution.py:24
  27.3 13.8 %collective-permute-start.4 = (bf16[192,1152]{1,0:T(8,128)(2,1)S(1)}, bf16[192,1152]{1,0:T(8,128)(2,1)S(1)}, u32[]{:S(2)}, u32[]{:S(2)}) collective-permute-start(bf16[192,1152]{1,0:T(8,128)(2,1)S(1)} %fusion.2), channel_id=1, source_target_pairs={{0,8},{4,12},{8,0},{12,4},{16,24},{20,28},{24,16},{28,20},{32,40},... | collective-permute-start | bytes 1327112 | tf_op jit(solution)/shard_map/ppermute | solution.py:29
  30.9 4.3 %collective-permute-start.2 = (bf16[384,1152]{1,0:T(8,128)(2,1)S(1)}, bf16[384,1152]{1,0:T(8,128)(2,1)S(1)}, u32[]{:S(2)}, u32[]{:S(2)}) collective-permute-start(bf16[384,1152]{1,0:T(8,128)(2,1)S(1)} %multiply_convert_fusion), channel_id=1, source_target_pairs={{0,1},{1,0},{2,3},{3,2},{4,5},{5,4},{6,7},{7,6},{8,9},{9,8},{10,11... | collective-permute-start | bytes 2654216 | tf_op jit(solution)/shard_map/ppermute | solution.py:44
  35.3 27.9 %collective-permute-start.3 = (bf16[192,1152]{1,0:T(8,128)(2,1)S(1)}, bf16[192,1152]{1,0:T(8,128)(2,1)S(1)}, u32[]{:S(2)}, u32[]{:S(2)}) collective-permute-start(bf16[192,1152]{1,0:T(8,128)(2,1)S(1)} %fusion.23), channel_id=1, source_target_pairs={{0,2},{1,3},{2,0},{3,1},{4,6},{5,7},{6,4},{7,5},{8,10},{9,11},{10,... | collective-permute-start | bytes 1327112 | tf_op jit(solution)/shard_map/ppermute | solution.py:44
  41.1 34.0 %collective-permute-start.5 = (bf16[192,1152]{1,0:T(8,128)(2,1)S(1)}, bf16[192,1152]{1,0:T(8,128)(2,1)S(1)}, u32[]{:S(2)}, u32[]{:S(2)}) collective-permute-start(bf16[192,1152]{1,0:T(8,128)(2,1)S(1)} %broadcast_select_fusion), channel_id=1, source_target_pairs={{24,8},{25,9},{26,10},{27,11},{28,12},{29,13},{30,14},{31,15},{40,... | collective-permute-start | bytes 1327112 | tf_op jit(solution)/shard_map/ppermute | solution.py:39
  43.1 32.0 %collective-permute-start.6 = (bf16[192,1152]{1,0:T(8,128)(2,1)S(1)}, bf16[192,1152]{1,0:T(8,128)(2,1)S(1)}, u32[]{:S(2)}, u32[]{:S(2)}) collective-permute-start(bf16[192,1152]{1,0:T(8,128)(2,1)S(1)} %fusion.1), channel_id=1, source_target_pairs={{4,0},{5,1},{6,2},{7,3},{8,4},{9,5},{10,6},{11,7},{12,8},{13,9},{1... | collective-permute-start | bytes 1327112 | tf_op jit(solution)/shard_map/ppermute | solution.py:113
